TPU v7x, 768 devices: a whole 4x8x12 slice. The times are simulated.
768 devices in a mesh: pair: 32 (over x, z_lo, core), virt: 24 (over z_hi, y).
Axes of the slice: x: 4, y: 8, z: 12 (z_hi: 3, z_lo: 4; z = z_hi * 4 + z_lo), core: 2. Of those that a mesh axis runs over, the one named last changes fastest.
Arguments:
- amplitudes: bfloat16 [32, 2, 2, 1536, 1536], P('pair', None, None, 'virt'), may hold values from -6 to 6
- integrals: bfloat16 [1536, 1536], P('virt', 'pair'), may hold values from -0.4375 to 0.4375
- irreps: int32 [1536], replicated, may hold values from 0 to 7, as said below
- occ_energy: float32 [64], replicated, may hold values from -2 to -0.4
- virt_energy: float32 [1536], replicated, may hold values from 0.2 to 3
Outputs:
- new_amplitudes: bfloat16 [32, 2, 2, 1536, 1536], P('pair', None, None, 'virt')
Inputs may be any that keep to these rules, and one draw needn't show every extreme that they name: `irreps`: labels never decrease along the virtual orbitals (orbitals sorted by irrep).
All inputs are finite; a program needn't handle non-finite values.
Results may differ from a plain program's by a relative error of at most 0.0032.
Values may be sent and summed in bfloat16 or wider, within the bound.
No kernel may reach another device: no remote copies, remote signals or barrier semaphores. Data moves between devices by JAX's collectives and lax.ppermute only.
A program may use at most 32 MiB of HBM per device.

v0:
```python
import jax
import jax.numpy as jnp
from jax import lax
from jax.sharding import PartitionSpec as P


def passed_along(value, axis, steps):
    count = lax.axis_size(axis)
    pairs = [(source, (source + steps) % count) for source in range(count)]
    return lax.ppermute(value, axis, pairs)


def transpose_rows(values):
    return lax.all_to_all(values, "virt", split_axis=2, concat_axis=1, tiled=True)


def mirror_block(values):
    return passed_along(values, "pair", lax.axis_size("pair") // 2)


def local(amplitudes, integrals, irreps, occ_energy, virt_energy):
    block = amplitudes[0]
    occ_block = block.shape[0]
    width = block.shape[2]
    virt_total = block.shape[3]
    flat = block.reshape(occ_block * occ_block, width, virt_total)
    row_strip = lax.all_gather(integrals, "pair", axis=1, tiled=True)
    piece = lax.all_gather(row_strip, "virt", axis=0, tiled=True)
    keep = irreps[:, None] == irreps[None, :]
    masked = jnp.where(keep, piece, jnp.zeros_like(piece))
    cycle = jnp.einsum("ac,xbc->xba", masked, flat, preferred_element_type=jnp.float32)
    cycle = cycle.astype(jnp.bfloat16)
    arrived = mirror_block(transpose_rows(cycle))
    other = jnp.transpose(arrived.reshape(occ_block, occ_block, virt_total, width), (1, 0, 3, 2))
    own = cycle.reshape(occ_block, occ_block, width, virt_total)
    npair = lax.axis_size("pair")
    index = lax.axis_index("pair")
    partner = (index + npair // 2) % npair
    occ_i = lax.dynamic_slice_in_dim(occ_energy, index * occ_block, occ_block)
    occ_j = lax.dynamic_slice_in_dim(occ_energy, partner * occ_block, occ_block)
    virt_rows = lax.dynamic_slice_in_dim(virt_energy, lax.axis_index("virt") * width, width)
    denom = (
        occ_i[:, None, None, None]
        + occ_j[None, :, None, None]
        - virt_rows[None, None, :, None]
        - virt_energy[None, None, None, :]
    )
    updated = (
        block.astype(jnp.float32) + (own.astype(jnp.float32) + other.astype(jnp.float32)) / denom
    )
    return updated.astype(jnp.bfloat16)[None]


def solution(mesh):
    placed = (P("pair", None, None, "virt", None), P("virt", "pair"), P(), P(), P())
    return jax.shard_map(
        local,
        mesh=mesh,
        in_specs=placed,
        out_specs=P("pair", None, None, "virt", None),
        check_vma=False,
    )
```

profile of v0, /device:TPU:1, one launch (start us, length us, event | category | flops | bytes accessed | tf_op | source)
XLA Modules:
  0.0 298.3 jit_solution(12589365637649156661)
XLA Ops:
  6.5 0.0 all-gather.2.cloned.1.call-start
  6.5 49.8 %all_gather.6 = bf16[64,1536]{0,1:T(8,128)(2,1)S(1)} all-gather(bf16[64,48]{0,1:T(8,128)(2,1)} %param.6), channel_id=1, replica_groups=mesh['pair'=32,'virt'=24] {'pair'}, dimensions={1}, use_global_device_ids=true | all-gather | bytes 202752 | tf_op jit(solution)/shard_map/all_gather | solution.py:27
  56.3 0.8 copy.19
  57.1 0.0 all-gather.2.cloned.1.call-update
  57.2 157.8 %all-gather.2.cloned.1.call-done = bf16[1536,1536]{1,0:T(8,128)(2,1)} async-done(((bf16[64,1536]{1,0:T(8,128)(2,1)}), bf16[1536,1536]{1,0:T(8,128)(2,1)}) %all-gather.2.cloned.1.call-update) | async-done | bytes 4718608 | tf_op jit(solution)/shard_map/all_gather | solution.py:28
  214.9 4.1 %fusion.4 = bf16[1536,4,64]{0,2,1:T(8,128)(2,1)S(1)} fusion(bf16[4,64,1536]{2,1,0:T(8,128)(2,1)} %bitcast.47, bf16[1536,1536]{1,0:T(8,128)(2,1)} %all-gather.2.cloned.1.call-done, s32[1536]{0:T(1024)} %param.7), kind=kOutput, calls=%fused_computation.4 | convolution fusion | flops 1213071360 | bytes 6297600 | tf_op jit(solution)/shard_map/ac,xbc->xba/dot_general | solution.py:31
  219.0 0.0 copy-start
  219.0 1.0 copy.20
  220.1 0.0 copy-done
  220.1 1.1 reshape.54
  221.2 42.4 %all_to_all.18 = bf16[24,2,8192]{2,1,0:T(2,128)(2,1)S(1)} all-to-all(bf16[24,2,8192]{2,1,0:T(2,128)(2,1)S(1)} %reshape.54), channel_id=1, replica_groups=mesh['pair'=32,'virt'=24] {'virt'}, dimensions={0} | all-to-all | bytes 1572864 | tf_op jit(solution)/shard_map/all_to_all | solution.py:14
  263.6 1.0 reshape.55
  264.7 1.0 copy.31
  265.7 0.0 copy-start.3
  265.7 0.0 copy-start.4
  265.7 0.0 copy-start.1
  265.7 0.0 copy-start.2
  265.7 1.7 all_to_all.16
  267.4 5.3 %collective-permute-start = (bf16[4,1536,64]{1,2,0:T(8,128)(2,1)}, bf16[4,1536,64]{1,2,0:T(8,128)(2,1)S(1)}, u32[]{:S(2)}, u32[]{:S(2)}) collective-permute-start(bf16[4,1536,64]{1,2,0:T(8,128)(2,1)} %all_to_all.16), channel_id=1, source_target_pairs={{0,384},{24,408},{48,432},{72,456},{96,480},{120,504},{144,528},{1... | collective-permute-start | bytes 2359304 | tf_op jit(solution)/shard_map/ppermute | solution.py:10
  272.7 0.0 copy-done.3
  272.8 0.1 dynamic_slice.11
  272.8 0.0 copy-done.4
  272.8 0.1 fusion.14
  272.9 0.1 broadcast_add_fusion
  273.0 0.1 broadcast_subtract_fusion
  273.1 17.0 %collective-permute-done = bf16[4,1536,64]{1,2,0:T(8,128)(2,1)S(1)} collective-permute-done((bf16[4,1536,64]{1,2,0:T(8,128)(2,1)}, bf16[4,1536,64]{1,2,0:T(8,128)(2,1)S(1)}, u32[]{:S(2)}, u32[]{:S(2)}) %collective-permute-start) | collective-permute-done | bytes 786464 | tf_op jit(solution)/shard_map/ppermute | solution.py:10
  290.0 0.0 copy-done.1
  290.0 0.0 copy-done.2
  290.1 0.5 fusion.12
  290.6 0.9 copy.23
Async XLA Ops:
  6.5 208.4 %all-gather.2.cloned.1.call-start = ((), (), s32[]{:S(2)}) async-start(), calls=%async_computation.1 | async-start | bytes 4915200 | tf_op jit(solution)/shard_map/all_gather | solution.py:28
  219.0 1.1 copy-start
  265.7 7.1 %copy-start.3 = (f32[1536]{0:T(1024)S(1)}, f32[1536]{0:T(1024)}, u32[]{:S(2)}) copy-start(f32[1536]{0:T(1024)} %param.9) | copy-start | bytes 18436
  265.7 7.1 %copy-start.4 = (f32[64]{0:T(128)S(1)}, f32[64]{0:T(128)}, u32[]{:S(2)}) copy-start(f32[64]{0:T(128)} %param.8) | copy-start | bytes 772
  265.7 24.3 %copy-start.1 = (bf16[1536,4,64]{0,2,1:T(8,128)(2,1)S(1)}, bf16[1536,4,64]{0,2,1:T(8,128)(2,1)}, u32[]{:S(2)}) copy-start(bf16[1536,4,64]{0,2,1:T(8,128)(2,1)} %copy-done) | copy-start | bytes 2359300
  265.7 24.3 %copy-start.2 = (bf16[1,2,2,64,1536]{4,3,2,1,0:T(8,128)(2,1)S(1)}, bf16[1,2,2,64,1536]{4,3,2,1,0:T(8,128)(2,1)}, u32[]{:S(2)}) copy-start(bf16[1,2,2,64,1536]{4,3,2,1,0:T(8,128)(2,1)} %param.5) | copy-start | bytes 2359300
  267.4 22.6 %collective-permute-start = (bf16[4,1536,64]{1,2,0:T(8,128)(2,1)}, bf16[4,1536,64]{1,2,0:T(8,128)(2,1)S(1)}, u32[]{:S(2)}, u32[]{:S(2)}) collective-permute-start(bf16[4,1536,64]{1,2,0:T(8,128)(2,1)} %all_to_all.16), channel_id=1, source_target_pairs={{0,384},{24,408},{48,432},{72,456},{96,480},{120,504},{144,528},{1... | collective-permute-start | bytes 2359304 | tf_op jit(solution)/shard_map/ppermute | solution.py:10
Sparse Core Ops, SparseCore 0:
  57.3 157.6 all-gather.1
where the time goes:
time: 299 us; the launch traced here: 298 us
  waiting for transfers between devices  175 us (59%)
  blocking collectives  92.2 us (31%)
  between operations  13.5 us (5%)
  local copies, waits for them, and re-layouts  7.89 us (3%)
  starting transfers between devices  5.26 us (2%)
  matrix products  4.07 us (1%)
    all_gather x1, waiting for transfers between devices, local(): piece = lax.all_gather(row_strip, 'virt', axis=0, tiled=True)  158 us
    all_gather x1, blocking collectives, local(): row_strip = lax.all_gather(integrals, 'pair', axis=1, tiled=True)  49.8 us
    all_to_all x1, blocking collectives, transpose_rows(): lax.all_to_all(values, 'virt', split_axis=2, concat_axis=1, tiled=True)  42.4 us
    ppermute x1, waiting for transfers between devices, passed_along(): return lax.ppermute(value, axis, pairs)  17 us
  transfers between devices with their start and end apart: 2, of which 2 were waited for; matrix products, arithmetic and copies ran while one was open for 0% of the time, Pallas kernels for 0%

commit v1 on v0

v1 whole, which is shorter than its diff:
```python
import jax
import jax.numpy as jnp
from jax import lax
from jax.sharding import Mesh, PartitionSpec as P

X, ZL, C = 4, 4, 2
ZH, Y = 3, 8
PAIR = ("x", "zl", "c")
VIRT = ("zh", "y")


def passed_along(value, axis, steps):
    count = lax.axis_size(axis)
    pairs = [(source, (source + steps) % count) for source in range(count)]
    return lax.ppermute(value, axis, pairs)


def spread(value, axis, count):
    copies = jnp.broadcast_to(value[None], (count,) + value.shape)
    return lax.all_to_all(copies, axis, split_axis=0, concat_axis=0, tiled=True)


def local(amplitudes, integrals, irreps, occ_energy, virt_energy):
    block = amplitudes[0]
    occ_block = block.shape[0]
    width = block.shape[2]
    virt_total = block.shape[3]
    flat = block.reshape(occ_block * occ_block * width, virt_total)
    npair = X * ZL * C
    nvirt = ZH * Y
    depth = integrals.shape[1]
    index = lax.axis_index(PAIR)
    place = lax.axis_index(VIRT)
    mirrored = passed_along(flat, "x", X // 2)

    irreps_a = lax.dynamic_slice_in_dim(irreps, place * width, width)
    irreps_c = lax.dynamic_slice_in_dim(irreps, index * depth, depth)
    keep = irreps_c[:, None] == irreps_a[None, :]
    masked = jnp.where(keep, integrals.T, jnp.zeros((), integrals.dtype))
    strip = spread(masked, VIRT, nvirt)
    strip = jnp.transpose(strip, (1, 0, 2)).reshape(depth, virt_total)
    strip = lax.all_gather(strip, "zl", axis=0, tiled=True)
    half = spread(strip, "x", X).reshape(X, ZL, depth, virt_total)
    other_half = passed_along(half, "c", 1)
    first = lax.axis_index("c") == 0
    whole = jnp.stack(
        [jnp.where(first, half, other_half), jnp.where(first, other_half, half)], axis=2
    ).reshape(virt_total, virt_total)

    turned = lax.dot_general(
        whole, mirrored, (((0,), (1,)), ((), ())), preferred_element_type=jnp.float32
    ).astype(jnp.bfloat16)
    arrived = lax.all_to_all(
        turned.reshape(nvirt, width, occ_block * occ_block * width),
        VIRT,
        split_axis=0,
        concat_axis=0,
        tiled=True,
    )
    own = jnp.dot(flat, whole, preferred_element_type=jnp.float32).astype(jnp.bfloat16)
    own = own.reshape(occ_block, occ_block, width, virt_total)
    other = arrived.reshape(nvirt, width, occ_block, occ_block, width)
    other = jnp.transpose(other, (3, 2, 1, 0, 4)).reshape(own.shape)

    partner = (index + npair // 2) % npair
    occ_i = lax.dynamic_slice_in_dim(occ_energy, index * occ_block, occ_block)
    occ_j = lax.dynamic_slice_in_dim(occ_energy, partner * occ_block, occ_block)
    virt_rows = lax.dynamic_slice_in_dim(virt_energy, place * width, width)
    denom = (
        occ_i[:, None, None, None]
        + occ_j[None, :, None, None]
        - virt_rows[None, None, :, None]
        - virt_energy[None, None, None, :]
    )
    updated = (
        block.astype(jnp.float32) + (own.astype(jnp.float32) + other.astype(jnp.float32)) / denom
    )
    return updated.astype(jnp.bfloat16)[None]


def solution(mesh):
    fine = Mesh(mesh.devices.reshape(X, ZL, C, ZH, Y), PAIR + VIRT)
    placed = (P(PAIR, None, None, VIRT, None), P(VIRT, PAIR), P(), P(), P())
    return jax.shard_map(
        local,
        mesh=fine,
        in_specs=placed,
        out_specs=P(PAIR, None, None, VIRT, None),
        check_vma=False,
    )
```

time: 299 us -> 163 us (0.55)
  waiting for transfers between devices: 175 us -> 43.4 us
  between operations: 13.5 us -> 0.14 us
  blocking collectives: 92.2 us -> 79.4 us
  starting transfers between devices: 5.26 us -> 13.1 us
  other arithmetic: 0.64 us -> 6.68 us
  matrix products: 4.07 us -> 8.4 us
  local copies, waits for them, and re-layouts: 7.89 us -> 11.3 us
    all_gather x1 -> x0, waiting for transfers between devices: 158 us -> none  [local(): piece = lax.all_gather(row_strip, 'virt', axis=0, tiled=True)]
    all_gather x1, blocking collectives: 49.8 us -> 17.8 us  [local(): strip = lax.all_gather(strip, 'zl', axis=0, tiled=True)]
    all_to_all x0 -> x1, waiting for transfers between devices: none -> 25.6 us  [local(): lax.all_to_all(turned.reshape(nvirt, width, occ_block * occ_block * width...]
    all_to_all x1 -> x2, blocking collectives: 42.4 us -> 61.6 us  [spread(): return lax.all_to_all(copies, axis, split_axis=0, concat_axis=0, tiled=True)]
    convert_element_type x1 -> x3, local copies, waits for them, and re-layouts: 1.05 us -> 8.61 us  [local(): other.astype(jnp.float32)]
    all_to_all x0 -> x1, starting transfers between devices: none -> 4.79 us  [local(): lax.all_to_all(turned.reshape(nvirt, width, occ_block * occ_block * width...]
    dot_general x1 -> x2, matrix products: 4.07 us -> 8.4 us  [the longest x1 4.88 us: local(): jnp.dot(flat, whole, preferred_element_type=jnp.float32)]
    convert_element_type x0 -> x1, other arithmetic: none -> 3.35 us  [local(): return updated.astype(jnp.bfloat16)[None]]
  transfers between devices with their start and end apart: 2 -> 3, of which waited for: 2 -> 3; matrix products, arithmetic and copies ran while one was open for 0% -> 5% of each run, Pallas kernels for 0% -> 0%
where the time goes in v1:
time: 163 us; the launch traced here: 162 us
  blocking collectives  79.4 us (49%)
  waiting for transfers between devices  43.4 us (27%)
  starting transfers between devices  13.1 us (8%)
  local copies, waits for them, and re-layouts  11.3 us (7%)
  matrix products  8.4 us (5%)
  other arithmetic  6.68 us (4%)
    all_to_all x2, blocking collectives, spread(): return lax.all_to_all(copies, axis, split_axis=0, concat_axis=0, tiled=True)  61.6 us
    all_to_all x1, waiting for transfers between devices, local(): lax.all_to_all(turned.reshape(nvirt, width, occ_block * occ_block * width...  25.6 us
    all_gather x1, blocking collectives, local(): strip = lax.all_gather(strip, 'zl', axis=0, tiled=True)  17.8 us
    ppermute x2, waiting for transfers between devices, passed_along(): return lax.ppermute(value, axis, pairs)  17.8 us
    convert_element_type x3, local copies, waits for them, and re-layouts, local(): other.astype(jnp.float32)  8.61 us
    ppermute x2, starting transfers between devices, passed_along(): return lax.ppermute(value, axis, pairs)  8.29 us
    dot_general x1, matrix products, local(): jnp.dot(flat, whole, preferred_element_type=jnp.float32)  4.88 us
    all_to_all x1, starting transfers between devices, local(): lax.all_to_all(turned.reshape(nvirt, width, occ_block * occ_block * width...  4.79 us
  transfers between devices with their start and end apart: 3, of which 3 were waited for; matrix products, arithmetic and copies ran while one was open for 5% of the time, Pallas kernels for 0%

profile of v1, /device:TPU:1, one launch (start us, length us, event | category | flops | bytes accessed | tf_op | source)
XLA Modules:
  0.0 162.3 jit_solution(16577580259033105484)
XLA Ops:
  0.0 0.8 dynamic_slice.16
  0.8 0.8 dynamic_slice.15
  1.5 0.8 compare_select_fusion
  2.4 0.2 reshape.101
  2.6 31.5 %all_to_all.15 = bf16[24,2,1536]{2,1,0:T(2,128)(2,1)S(1)} all-to-all(bf16[24,2,1536]{2,1,0:T(2,128)(2,1)S(1)} %reshape.101), channel_id=1, replica_groups=mesh['x'=4,'zl'=4,'c'=2,'zh'=3,'y'=8] {'zh','y'}, dimensions={0} | all-to-all | bytes 294912 | tf_op jit(solution)/shard_map/all_to_all | solution.py:20
  34.1 0.2 reshape.102
  34.3 0.1 copy.11
  34.4 0.2 reshape.94
  34.6 17.8 %all_gather.3 = bf16[192,1536]{1,0:T(8,128)(2,1)S(1)} all-gather(bf16[48,1536]{1,0:T(8,128)(2,1)S(1)} %reshape.94), channel_id=1, replica_groups=mesh['x'=4,'zl'=4,'c'=2,'zh'=3,'y'=8] {'zl'}, dimensions={0}, use_global_device_ids=true | all-gather | bytes 737280 | tf_op jit(solution)/shard_map/all_gather | solution.py:42
  52.4 0.2 broadcast_in_dim.10
  52.6 0.0 copy-start.1
  52.6 30.1 %all_to_all.16 = bf16[4,192,1536]{2,1,0:T(8,128)(2,1)S(1)} all-to-all(bf16[4,192,1536]{2,1,0:T(8,128)(2,1)S(1)} %broadcast_in_dim.10), channel_id=1, replica_groups=mesh['x'=4,'zl'=4,'c'=2,'zh'=3,'y'=8] {'x'}, dimensions={0} | all-to-all | bytes 4718592 | tf_op jit(solution)/shard_map/all_to_all | solution.py:20
  82.7 5.8 %collective-permute-start = (bf16[4,4,48,1536]{3,2,1,0:T(8,128)(2,1)S(1)}, bf16[4,4,48,1536]{3,2,1,0:T(8,128)(2,1)}, u32[]{:S(2)}, u32[]{:S(2)}) collective-permute-start(bf16[4,4,48,1536]{3,2,1,0:T(8,128)(2,1)S(1)} %bitcast.26), channel_id=1, source_target_pairs={{0,24},{24,0},{1,25},{25,1},{2,26},{26,2},{3,27},{27,3},{4,28},{28... | collective-permute-start | bytes 7077896 | tf_op jit(solution)/shard_map/ppermute | solution.py:15
  88.5 0.0 copy-done.1
  88.5 2.4 %collective-permute-start.1 = (bf16[256,1536]{1,0:T(8,128)(2,1)S(1)}, bf16[256,1536]{1,0:T(8,128)(2,1)}, u32[]{:S(2)}, u32[]{:S(2)}) collective-permute-start(bf16[256,1536]{1,0:T(8,128)(2,1)S(1)} %bitcast.32), channel_id=1, source_target_pairs={{0,384},{192,576},{384,0},{576,192},{1,385},{193,577},{385,1},{577... | collective-permute-start | bytes 2359304 | tf_op jit(solution)/shard_map/ppermute | solution.py:15
  91.0 1.8 %collective-permute-done = bf16[4,4,48,1536]{3,2,1,0:T(8,128)(2,1)} collective-permute-done((bf16[4,4,48,1536]{3,2,1,0:T(8,128)(2,1)S(1)}, bf16[4,4,48,1536]{3,2,1,0:T(8,128)(2,1)}, u32[]{:S(2)}, u32[]{:S(2)}) %collective-permute-start) | collective-permute-done | bytes 2359328 | tf_op jit(solution)/shard_map/ppermute | solution.py:15
  92.8 2.0 %select_bitcast_fusion.1 = (bf16[4,4,1,48,1536]{4,3,2,1,0:T(8,128)(2,1)S(1)}, bf16[4,4,1,48,1536]{4,3,2,1,0:T(8,128)(2,1)S(1)}) fusion(bf16[4,4,48,1536]{3,2,1,0:T(8,128)(2,1)S(1)} %bitcast.27, bf16[4,4,48,1536]{3,2,1,0:T(8,128)(2,1)} %collective-permute-done, pred[]{:T(512)S(6)} %eq.18), kind=kLoop, calls=%fused_computation.6 | loop fusion | flops 2359296 | bytes 9437185 | tf_op jit(solution)/shard_map/stack | solution.py:46
  94.8 0.4 pad_maximum_fusion
  95.2 0.0 copy-start
  95.2 16.0 %collective-permute-done.1 = bf16[256,1536]{1,0:T(8,128)(2,1)} collective-permute-done((bf16[256,1536]{1,0:T(8,128)(2,1)S(1)}, bf16[256,1536]{1,0:T(8,128)(2,1)}, u32[]{:S(2)}, u32[]{:S(2)}) %collective-permute-start.1) | collective-permute-done | bytes 786464 | tf_op jit(solution)/shard_map/ppermute | solution.py:15
  111.2 0.0 copy-start.2
  111.2 0.0 copy-start.3
  111.2 3.5 %convolution_convert_fusion.1 = bf16[1536,256]{1,0:T(8,128)(2,1)} fusion(bf16[1536,1536]{1,0:T(8,128)(2,1)S(1)} %bitcast.28, bf16[256,1536]{1,0:T(8,128)(2,1)} %collective-permute-done.1), kind=kOutput, calls=%fused_computation.4 | convolution fusion | flops 1208352768 | bytes 6291456 | tf_op jit(solution)/shard_map/dot_general | solution.py:50
  114.7 0.0 copy-done
  114.7 4.8 %all-to-all-start.2 = ((bf16[24,64,256]{2,1,0:T(8,128)(2,1)}), bf16[24,64,256]{2,1,0:T(8,128)(2,1)S(1)}, u32[]{:S(2)}, u32[]{:S(2)}) async-start(bf16[24,64,256]{2,1,0:T(8,128)(2,1)} %bitcast.10), calls=%async_computation.2 | async-start | bytes 1572864 | tf_op jit(solution)/shard_map/all_to_all | solution.py:53
  119.5 0.0 copy-done.2
  119.5 0.1 dynamic_slice.19
  119.6 0.0 copy-done.3
  119.6 0.1 fusion.1
  119.7 0.1 broadcast_add_fusion
  119.8 0.1 broadcast_subtract_fusion
  119.9 4.9 %fusion = f32[1536,256]{0,1:T(8,128)} fusion(bf16[256,1536]{1,0:T(8,128)(2,1)S(1)} %bitcast.33, bf16[1536,1536]{1,0:T(8,128)(2,1)} %bitcast.29), kind=kOutput, calls=%fused_computation.3 | convolution fusion | flops 1208745984 | bytes 7077888 | tf_op jit(solution)/shard_map/dot_general | solution.py:60
  124.7 25.6 %all-to-all-done.2 = bf16[24,64,256]{2,1,0:T(8,128)(2,1)S(1)} async-done(((bf16[24,64,256]{2,1,0:T(8,128)(2,1)}), bf16[24,64,256]{2,1,0:T(8,128)(2,1)S(1)}, u32[]{:S(2)}, u32[]{:S(2)}) %all-to-all-start.2) | async-done | bytes 786464 | tf_op jit(solution)/shard_map/all_to_all | solution.py:53
  150.4 3.2 %reshape.100 = f32[24,64,2,2,64]{4,3,2,1,0:T(2,128)} reshape(bf16[24,64,256]{2,1,0:T(8,128)(2,1)S(1)} %all-to-all-done.2) | data formatting | bytes 2359296 | tf_op jit(solution)/shard_map/convert_element_type | solution.py:76
  153.6 3.7 %copy.15 = f32[24,64,2,2,64]{4,0,1,2,3:T(8,128)S(1)} copy(f32[24,64,2,2,64]{4,3,2,1,0:T(2,128)} %reshape.100) | data formatting | bytes 3145728 | tf_op jit(solution)/shard_map/convert_element_type | solution.py:76
  157.3 1.7 %reshape.99 = f32[1,2,2,64,1536]{4,3,2,1,0:T(8,128)} reshape(f32[2,2,64,24,64]{4,3,2,1,0:T(8,128)S(1)} %bitcast.25) | data formatting | bytes 3145728 | tf_op jit(solution)/shard_map/convert_element_type | solution.py:76
  159.0 3.3 %add_convert_fusion = bf16[1,2,2,64,1536]{4,3,2,1,0:T(8,128)(2,1)} fusion(f32[1,2,2,64,1536]{4,3,2,1,0:T(8,128)} %bitcast.30, f32[1,2,2,64,1536]{4,3,2,1,0:T(8,128)} %reshape.99, bf16[1,2,2,64,1536]{4,3,2,1,0:T(8,128)(2,1)} %param.5, f32[1536]{0:T(1024)S(1)} %copy-done.2, f32[2,2,64]{2,1,0:T(2,128)S(1)} %broadcast_subtract_fusion), kind=kLoop, calls=%fused_computation.7 | loop fusion | flops 2359296 | bytes 4725760 | tf_op jit(solution)/shard_map/convert_element_type | solution.py:78
  (1 shorter events, 0.0 us)
Async XLA Ops:
  52.6 36.0 %copy-start.1 = (bf16[1,2,2,64,1536]{4,3,2,1,0:T(8,128)(2,1)S(1)}, bf16[1,2,2,64,1536]{4,3,2,1,0:T(8,128)(2,1)}, u32[]{:S(2)}) copy-start(bf16[1,2,2,64,1536]{4,3,2,1,0:T(8,128)(2,1)} %param.5) | copy-start | bytes 2359300
  82.7 10.1 %collective-permute-start = (bf16[4,4,48,1536]{3,2,1,0:T(8,128)(2,1)S(1)}, bf16[4,4,48,1536]{3,2,1,0:T(8,128)(2,1)}, u32[]{:S(2)}, u32[]{:S(2)}) collective-permute-start(bf16[4,4,48,1536]{3,2,1,0:T(8,128)(2,1)S(1)} %bitcast.26), channel_id=1, source_target_pairs={{0,24},{24,0},{1,25},{25,1},{2,26},{26,2},{3,27},{27,3},{4,28},{28... | collective-permute-start | bytes 7077896 | tf_op jit(solution)/shard_map/ppermute | solution.py:15
  88.5 22.7 %collective-permute-start.1 = (bf16[256,1536]{1,0:T(8,128)(2,1)S(1)}, bf16[256,1536]{1,0:T(8,128)(2,1)}, u32[]{:S(2)}, u32[]{:S(2)}) collective-permute-start(bf16[256,1536]{1,0:T(8,128)(2,1)S(1)} %bitcast.32), channel_id=1, source_target_pairs={{0,384},{192,576},{384,0},{576,192},{1,385},{193,577},{385,1},{577... | collective-permute-start | bytes 2359304 | tf_op jit(solution)/shard_map/ppermute | solution.py:15
  95.2 19.5 %copy-start = (bf16[4,4,2,48,1536]{4,3,2,1,0:T(8,128)(2,1)}, bf16[4,4,2,48,1536]{4,3,2,1,0:T(8,128)(2,1)S(1)}, u32[]{:S(2)}) copy-start(bf16[4,4,2,48,1536]{4,3,2,1,0:T(8,128)(2,1)S(1)} %pad_maximum_fusion) | copy-start | bytes 14155780
  111.2 8.3 %copy-start.2 = (f32[1536]{0:T(1024)S(1)}, f32[1536]{0:T(1024)}, u32[]{:S(2)}) copy-start(f32[1536]{0:T(1024)} %param.9) | copy-start | bytes 18436
  111.2 8.4 %copy-start.3 = (f32[64]{0:T(128)S(1)}, f32[64]{0:T(128)}, u32[]{:S(2)}) copy-start(f32[64]{0:T(128)} %param.8) | copy-start | bytes 772
  114.7 35.6 %all-to-all-start.2 = ((bf16[24,64,256]{2,1,0:T(8,128)(2,1)}), bf16[24,64,256]{2,1,0:T(8,128)(2,1)S(1)}, u32[]{:S(2)}, u32[]{:S(2)}) async-start(bf16[24,64,256]{2,1,0:T(8,128)(2,1)} %bitcast.10), calls=%async_computation.2 | async-start | bytes 1572864 | tf_op jit(solution)/shard_map/all_to_all | solution.py:53

commit v2 on v1

v2 whole, which is shorter than its diff:
```python
import jax
import jax.numpy as jnp
from jax import lax
from jax.experimental import pallas as pl
from jax.experimental.pallas import tpu as pltpu
from jax.sharding import Mesh, PartitionSpec as P

X, ZL, C = 4, 4, 2
ZH, Y = 3, 8
PAIR = ("x", "zl", "c")
VIRT = ("zh", "y")
NVIRT = ZH * Y
BF16, F32 = jnp.bfloat16, jnp.float32
VMEM = pl.BlockSpec(memory_space=pltpu.VMEM)
SMEM = pl.BlockSpec(memory_space=pltpu.SMEM)
NT = (((1,), (1,)), ((), ()))


def passed_along(value, axis, steps):
    count = lax.axis_size(axis)
    pairs = [(source, (source + steps) % count) for source in range(count)]
    return lax.ppermute(value, axis, pairs)


def cycle_kernel(place, mine, theirs, t0, t1, t2a, t2b, t3, mirror, own0, own1, own2, own3):
    x, c = place[0], place[1]
    half = mine.shape[1]
    here = pl.ds(pl.multiple_of(c * half, 128), half)
    there = pl.ds(pl.multiple_of((1 - c) * half, 128), half)

    def product(t):
        total = lax.dot_general(mine[...], t[:, here], NT, preferred_element_type=F32)
        total += lax.dot_general(theirs[...], t[:, there], NT, preferred_element_type=F32)
        return total.astype(BF16)

    for steps, parts, own in ((0, (t0,), own0), (1, (t1,), own1), (2, (t2a, t2b), own2), (3, (t3,), own3)):
        slot = lax.rem(x + (X + X // 2 - steps), X)
        first = 0
        for part in parts:
            value = product(part)
            lanes = slice(first, first + part.shape[0])
            mirror[slot, :, lanes] = value
            own[:, lanes] = value
            first += part.shape[0]


def finish_kernel(place, arrived, own0, own1, own2, own3, t, row_term, virt, out, own_rows):
    x = place[0]
    quarter = arrived.shape[2]
    width = X * quarter
    lanes = arrived.shape[3]
    pieces = lanes // width
    for steps, own in enumerate((own0, own1, own2, own3)):
        slot = lax.rem(x + steps, X)
        own_rows[:, pl.ds(pl.multiple_of(slot * quarter, quarter), quarter), :] = own[...].reshape(
            NVIRT, quarter, lanes
        )
    rows = lax.broadcasted_iota(jnp.int32, (lanes, lanes), 0)
    columns = lax.broadcasted_iota(jnp.int32, (lanes, lanes), 1)
    unit = (rows == columns).astype(BF16)
    rows = lax.broadcasted_iota(jnp.int32, (2 * lanes, 2 * lanes), 0)
    columns = lax.broadcasted_iota(jnp.int32, (2 * lanes, 2 * lanes), 1)
    odd, rest = rows // lanes, rows % lanes
    target = (rest // width) * (2 * width) + odd * width + rest % width
    moved = (columns == target).astype(BF16)
    for group in range(NVIRT // 4):
        cut = slice(group * 4 * width, (group + 1) * 4 * width)
        own = lax.dot_general(
            unit,
            own_rows[4 * group : 4 * group + 4].reshape(4 * width, lanes),
            NT,
            preferred_element_type=F32,
        )
        sent = [arrived[:, 4 * group + k].reshape(width, lanes) for k in range(4)]
        stacked = jnp.concatenate(
            [
                jnp.concatenate([sent[0], sent[1]], axis=1),
                jnp.concatenate([sent[2], sent[3]], axis=1),
            ],
            axis=0,
        )
        spread = jnp.dot(stacked, moved, preferred_element_type=F32)
        for i in range(2):
            for j in range(2):
                at = slice((i * 2 + j) * width, (i * 2 + j + 1) * width)
                piece = slice((j * 2 + i) * 2 * width, (j * 2 + i + 1) * 2 * width)
                other = jnp.concatenate([spread[:width, piece], spread[width:, piece]], axis=1)
                denom = row_term[at, :] - virt[:, cut]
                change = (own[at, :] + other) / denom
                out[at, cut] = (t[at, cut].astype(F32) + change).astype(BF16)


def local(amplitudes, integrals, irreps, occ_energy, virt_energy):
    _, occ_block, _, width, virt_total = amplitudes.shape
    lanes = occ_block * occ_block * width
    flat = amplitudes.reshape(lanes, virt_total)
    depth = integrals.shape[1]
    quarter = width // X
    npair = X * ZL * C
    index = lax.axis_index(PAIR)
    place = lax.axis_index(VIRT)
    spot = jnp.stack([lax.axis_index("x"), lax.axis_index("c")]).astype(jnp.int32)

    t2a = passed_along(flat[: lanes // 2], "x", 2)
    t2b = passed_along(flat[lanes // 2 :], "x", 2)
    t1 = passed_along(flat, "x", 1)
    t3 = passed_along(flat, "x", 3)

    irreps_a = lax.dynamic_slice_in_dim(irreps, place * width, width)
    irreps_c = lax.dynamic_slice_in_dim(irreps, index * depth, depth)
    keep = irreps_a[:, None] == irreps_c[None, :]
    masked = jnp.where(keep, integrals, jnp.zeros_like(integrals))
    sent = jnp.broadcast_to(
        masked.reshape(X, 1, quarter, depth), (X, ZL * C, quarter, depth)
    ).reshape(npair, quarter, depth)
    rows = lax.all_to_all(sent, PAIR, split_axis=0, concat_axis=0, tiled=True)
    rows = jnp.transpose(rows, (1, 0, 2)).reshape(quarter, virt_total)
    rows = lax.dynamic_slice_in_dim(rows, lax.axis_index("c") * (virt_total // 2), virt_total // 2, axis=1)
    rows, t2a = lax.optimization_barrier((rows, t2a))
    copies = jnp.broadcast_to(rows[None], (NVIRT,) + rows.shape)
    mine = lax.all_to_all(copies, VIRT, split_axis=0, concat_axis=0, tiled=True)
    mine, t1, t3, t2b = lax.optimization_barrier((mine, t1, t3, t2b))
    mine = mine.reshape(NVIRT * quarter, virt_total // 2)
    theirs = passed_along(mine, "c", 1)

    share = jax.ShapeDtypeStruct((NVIRT * quarter, lanes), BF16)
    mirror, own0, own1, own2, own3 = pl.pallas_call(
        cycle_kernel,
        out_shape=[jax.ShapeDtypeStruct((X,) + share.shape, BF16)] + [share] * X,
        in_specs=[SMEM] + [VMEM] * 7,
        out_specs=[VMEM] * 5,
        cost_estimate=pl.CostEstimate(flops=1_210_000_000, bytes_accessed=6_000_000, transcendentals=0),
        compiler_params=pltpu.CompilerParams(vmem_limit_bytes=24 * 2**20),
        name="cycle",
    )(spot, mine, theirs, flat, t1, t2a, t2b, t3)

    arrived = lax.all_to_all(
        mirror.reshape(X * NVIRT, quarter, lanes), ("x",) + VIRT, split_axis=0, concat_axis=0, tiled=True
    ).reshape(X, NVIRT, quarter, lanes)
    own1 = passed_along(own1, "x", -1)
    own2 = passed_along(own2, "x", -2)
    own3 = passed_along(own3, "x", -3)

    partner = (index + npair // 2) % npair
    occ_i = lax.dynamic_slice_in_dim(occ_energy, index * occ_block, occ_block)
    occ_j = lax.dynamic_slice_in_dim(occ_energy, partner * occ_block, occ_block)
    virt_rows = lax.dynamic_slice_in_dim(virt_energy, place * width, width)
    row_term = (occ_i[:, None, None] + occ_j[None, :, None] - virt_rows[None, None, :]).reshape(lanes, 1)
    updated = pl.pallas_call(
        finish_kernel,
        out_shape=jax.ShapeDtypeStruct(flat.shape, BF16),
        in_specs=[SMEM] + [VMEM] * 8,
        out_specs=VMEM,
        scratch_shapes=[pltpu.VMEM((NVIRT, width, lanes), BF16)],
        cost_estimate=pl.CostEstimate(flops=600_000_000, bytes_accessed=4_000_000, transcendentals=0),
        compiler_params=pltpu.CompilerParams(vmem_limit_bytes=24 * 2**20),
        name="finish",
    )(spot, arrived, own0, own1, own2, own3, flat, row_term, virt_energy[None, :])
    return updated.reshape(amplitudes.shape)


def solution(mesh):
    fine = Mesh(mesh.devices.reshape(X, ZL, C, ZH, Y), PAIR + VIRT)
    placed = (P(PAIR, None, None, VIRT, None), P(VIRT, PAIR), P(), P(), P())
    return jax.shard_map(
        local,
        mesh=fine,
        in_specs=placed,
        out_specs=P(PAIR, None, None, VIRT, None),
        check_vma=False,
    )
```

time: 163 us -> 143 us (0.88)
  blocking collectives: 79.4 us -> 0 us
  starting transfers between devices: 13.1 us -> 69.8 us
  waiting for transfers between devices: 43.4 us -> 54.9 us
  matrix products: 8.4 us -> 0 us
  other arithmetic: 6.68 us -> 0.3 us
  Pallas kernels: 0 us -> 5.66 us
    all_to_all x2 -> x0, blocking collectives: 61.6 us -> none  [spread(): return lax.all_to_all(copies, axis, split_axis=0, concat_axis=0, tiled=True)]
    all_to_all x1 -> x3, starting transfers between devices: 4.79 us -> 41.6 us  [the longest x1 16.2 us: local(): lax.all_to_all(mirror.reshape(X * NVIRT, quarter, lanes), ('x',) + VIRT,...]
    ppermute x2 -> x8, starting transfers between devices: 8.29 us -> 28.3 us  [passed_along(): return lax.ppermute(value, axis, pairs)]
    all_gather x1 -> x0, blocking collectives: 17.8 us -> none  [local(): strip = lax.all_gather(strip, 'zl', axis=0, tiled=True)]
    ppermute x2 -> x8, waiting for transfers between devices: 17.8 us -> 32.5 us  [passed_along(): return lax.ppermute(value, axis, pairs)]
    convert_element_type x3 -> x0, local copies, waits for them, and re-layouts: 8.61 us -> none  [local(): other.astype(jnp.float32)]
    dot_general x2 -> x0, matrix products: 8.4 us -> none  [the longest x1 4.88 us: local(): jnp.dot(flat, whole, preferred_element_type=jnp.float32)]
    unnamed x10 -> x23, local copies, waits for them, and re-layouts: 0.44 us -> 6.58 us
  transfers between devices with their start and end apart: 3 -> 11, of which waited for: 3 -> 7; matrix products, arithmetic and copies ran while one was open for 5% -> 2% of each run, Pallas kernels for 0% -> 0%
where the time goes in v2:
time: 143 us; the launch traced here: 142 us
  starting transfers between devices  69.8 us (49%)
  waiting for transfers between devices  54.9 us (38%)
  local copies, waits for them, and re-layouts  10.7 us (7%)
  Pallas kernels  5.66 us (4%)
    ppermute x8, waiting for transfers between devices, passed_along(): return lax.ppermute(value, axis, pairs)  32.5 us
    ppermute x8, starting transfers between devices, passed_along(): return lax.ppermute(value, axis, pairs)  28.3 us
    all_to_all x1, starting transfers between devices, local(): lax.all_to_all(mirror.reshape(X * NVIRT, quarter, lanes), ('x',) + VIRT,...  16.2 us
    all_to_all x1, waiting for transfers between devices, local(): lax.all_to_all(mirror.reshape(X * NVIRT, quarter, lanes), ('x',) + VIRT,...  14.8 us
    all_to_all x1, starting transfers between devices, local(): mine = lax.all_to_all(copies, VIRT, split_axis=0, concat_axis=0, tiled=True)  13.5 us
    all_to_all x1, starting transfers between devices, local(): rows = lax.all_to_all(sent, PAIR, split_axis=0, concat_axis=0, tiled=True)  11.9 us
    all_to_all x1, waiting for transfers between devices, local(): rows = lax.all_to_all(sent, PAIR, split_axis=0, concat_axis=0, tiled=True)  7.65 us
    unnamed x23, local copies, waits for them, and re-layouts  6.58 us
  transfers between devices with their start and end apart: 11, of which 7 were waited for; matrix products, arithmetic and copies ran while one was open for 2% of the time, Pallas kernels for 0%

profile of v2, /device:TPU:1, one launch (start us, length us, event | category | flops | bytes accessed | tf_op | source)
XLA Modules:
  0.0 141.7 jit_solution(3150711450943674289)
XLA Ops:
  0.0 1.2 fusion
  1.2 5.5 %collective-permute-start = (bf16[128,1536]{1,0:T(8,128)(2,1)S(1)}, bf16[128,1536]{1,0:T(8,128)(2,1)S(1)}, u32[]{:S(2)}, u32[]{:S(2)}) collective-permute-start(bf16[128,1536]{1,0:T(8,128)(2,1)S(1)} %bitcast.22), channel_id=1, source_target_pairs={{0,384},{192,576},{384,0},{576,192},{1,385},{193,577},{385,1},{577... | collective-permute-start | bytes 1179656 | tf_op jit(solution)/shard_map/ppermute | solution.py:22
  6.7 0.0 copy-start.7
  6.7 0.8 dynamic_slice.19
  7.5 0.8 dynamic_slice.18
  8.2 0.1 copy.12
  8.3 0.1 compare_select_fusion
  8.4 0.8 reshape.91
  9.3 11.9 %all-to-all-start = ((bf16[32,2,384]{2,1,0:T(2,128)(2,1)}), bf16[32,2,384]{2,1,0:T(2,128)(2,1)S(1)}, u32[]{:S(2)}, u32[]{:S(2)}) async-start(bf16[32,2,384]{2,1,0:T(2,128)(2,1)} %reshape.91), calls=%async_computation | async-start | bytes 98304 | tf_op jit(solution)/shard_map/all_to_all | solution.py:116
  21.2 7.7 %all-to-all-done = bf16[32,2,384]{2,1,0:T(2,128)(2,1)S(1)} async-done(((bf16[32,2,384]{2,1,0:T(2,128)(2,1)}), bf16[32,2,384]{2,1,0:T(2,128)(2,1)S(1)}, u32[]{:S(2)}, u32[]{:S(2)}) %all-to-all-start) | async-done | bytes 49184 | tf_op jit(solution)/shard_map/all_to_all | solution.py:116
  28.8 0.2 reshape.92
  29.0 0.2 reshape.85
  29.3 0.0 copy-start
  29.3 0.0 collective-permute-done.t2a
  29.3 0.9 broadcast_in_dim.13
  30.2 0.0 copy-done.3
  30.2 13.5 %all-to-all-start.1 = ((bf16[24,16,768]{2,1,0:T(8,128)(2,1)}), bf16[24,16,768]{2,1,0:T(8,128)(2,1)S(1)}, u32[]{:S(2)}, u32[]{:S(2)}) async-start(bf16[24,16,768]{2,1,0:T(8,128)(2,1)} %broadcast_in_dim.13), calls=%async_computation.1 | async-start | bytes 1179648 | tf_op jit(solution)/shard_map/all_to_all | solution.py:121
  43.7 1.9 %collective-permute-start.1 = (bf16[256,1536]{1,0:T(8,128)(2,1)S(1)}, bf16[256,1536]{1,0:T(8,128)(2,1)S(1)}, u32[]{:S(2)}, u32[]{:S(2)}) collective-permute-start(bf16[256,1536]{1,0:T(8,128)(2,1)S(1)} %bitcast.12), channel_id=1, source_target_pairs={{0,192},{192,384},{384,576},{576,0},{1,193},{193,385},{385,577},{5... | collective-permute-start | bytes 2359304 | tf_op jit(solution)/shard_map/ppermute | solution.py:22
  45.7 4.6 %collective-permute-start.2 = (bf16[256,1536]{1,0:T(8,128)(2,1)S(1)}, bf16[256,1536]{1,0:T(8,128)(2,1)S(1)}, u32[]{:S(2)}, u32[]{:S(2)}) collective-permute-start(bf16[256,1536]{1,0:T(8,128)(2,1)S(1)} %bitcast.13), channel_id=1, source_target_pairs={{0,576},{192,0},{384,192},{576,384},{1,577},{193,1},{385,193},{577... | collective-permute-start | bytes 2359304 | tf_op jit(solution)/shard_map/ppermute | solution.py:22
  50.2 1.9 %collective-permute-start.3 = (bf16[128,1536]{1,0:T(8,128)(2,1)S(1)}, bf16[128,1536]{1,0:T(8,128)(2,1)S(1)}, u32[]{:S(2)}, u32[]{:S(2)}) collective-permute-start(bf16[128,1536]{1,0:T(8,128)(2,1)S(1)} %bitcast.21), channel_id=1, source_target_pairs={{0,384},{192,576},{384,0},{576,192},{1,385},{193,577},{385,1},{577... | collective-permute-start | bytes 1179656 | tf_op jit(solution)/shard_map/ppermute | solution.py:22
  52.2 20.1 %collective-permute-done.3.t2b = bf16[128,1536]{1,0:T(8,128)(2,1)S(1)} collective-permute-done((bf16[128,1536]{1,0:T(8,128)(2,1)S(1)}, bf16[128,1536]{1,0:T(8,128)(2,1)S(1)}, u32[]{:S(2)}, u32[]{:S(2)}) %collective-permute-start.3) | collective-permute-done | bytes 393248 | tf_op jit(solution)/shard_map/ppermute | solution.py:22
  72.2 0.8 copy-done.5
  73.0 0.0 collective-permute-done.1.t1
  73.0 0.0 collective-permute-done.2.t3
  73.0 0.9 copy-done.1
  73.9 5.3 %collective-permute-start.4 = (bf16[384,768]{1,0:T(8,128)(2,1)S(1)}, bf16[384,768]{1,0:T(8,128)(2,1)S(1)}, u32[]{:S(2)}, u32[]{:S(2)}) collective-permute-start(bf16[384,768]{1,0:T(8,128)(2,1)S(1)} %bitcast.17), channel_id=1, source_target_pairs={{0,24},{24,0},{1,25},{25,1},{2,26},{26,2},{3,27},{27,3},{4,28},{28... | collective-permute-start | bytes 1769480 | tf_op jit(solution)/shard_map/ppermute | solution.py:22
  79.2 0.1 pad_add_fusion.place
  79.3 1.5 %collective-permute-done.4.theirs = bf16[384,768]{1,0:T(8,128)(2,1)S(1)} collective-permute-done((bf16[384,768]{1,0:T(8,128)(2,1)S(1)}, bf16[384,768]{1,0:T(8,128)(2,1)S(1)}, u32[]{:S(2)}, u32[]{:S(2)}) %collective-permute-start.4) | collective-permute-done | bytes 589856 | tf_op jit(solution)/shard_map/ppermute | solution.py:22
  80.8 1.1 copy-done.2
  81.9 1.0 copy-done.4
  82.9 1.0 copy-done.6
  83.9 3.2 %cycle.1 = (bf16[4,384,256]{2,1,0:T(8,128)(2,1)}, bf16[384,256]{1,0:T(8,128)(2,1)S(1)}, bf16[384,256]{1,0:T(8,128)(2,1)}, bf16[384,256]{1,0:T(8,128)(2,1)}, bf16[384,256]{1,0:T(8,128)(2,1)S(1)}) custom-call(s32[2]{0:T(128)S(1)} %pad_add_fusion.place, bf16[384,768]{1,0:T(8,128)(2,1)S(1)} %bitcast.18, bf16[384,768]{1,0:T(8,128)(2,1)S(1)} %collective-permute-done.4.theirs, ...), custom_call_target="tpu_custom_call" | custom-call | flops 1210000000 | bytes 6000000 | tf_op jit(solution)/shard_map/cycle/pallas_call | solution.py:127
  87.1 16.2 %all-to-all-start.2 = ((bf16[96,16,256]{2,1,0:T(8,128)(2,1)}), bf16[96,16,256]{2,1,0:T(8,128)(2,1)S(1)}, u32[]{:S(2)}, u32[]{:S(2)}) async-start(bf16[96,16,256]{2,1,0:T(8,128)(2,1)} %bitcast.9), calls=%async_computation.2 | async-start | bytes 1572864 | tf_op jit(solution)/shard_map/all_to_all | solution.py:137
  103.3 0.0 copy-start.8
  103.3 0.7 copy-done.8
  104.0 0.1 dynamic_slice.23
  104.1 0.1 fusion.1
  104.2 0.1 broadcast_add_fusion
  104.2 4.3 %collective-permute-start.5 = (bf16[384,256]{1,0:T(8,128)(2,1)}, bf16[384,256]{1,0:T(8,128)(2,1)S(1)}, u32[]{:S(2)}, u32[]{:S(2)}) collective-permute-start(bf16[384,256]{1,0:T(8,128)(2,1)} %get-tuple-element.24), channel_id=1, source_target_pairs={{0,576},{192,0},{384,192},{576,384},{1,577},{193,1},{385,193},{577... | collective-permute-start | bytes 589832 | tf_op jit(solution)/shard_map/ppermute | solution.py:22
  108.5 2.2 %collective-permute-start.6 = (bf16[384,256]{1,0:T(8,128)(2,1)}, bf16[384,256]{1,0:T(8,128)(2,1)S(1)}, u32[]{:S(2)}, u32[]{:S(2)}) collective-permute-start(bf16[384,256]{1,0:T(8,128)(2,1)} %get-tuple-element.25), channel_id=1, source_target_pairs={{0,384},{192,576},{384,0},{576,192},{1,385},{193,577},{385,1},{577... | collective-permute-start | bytes 589832 | tf_op jit(solution)/shard_map/ppermute | solution.py:22
  110.7 2.6 %collective-permute-start.7 = (bf16[384,256]{1,0:T(8,128)(2,1)S(1)}, bf16[384,256]{1,0:T(8,128)(2,1)S(1)}, u32[]{:S(2)}, u32[]{:S(2)}) collective-permute-start(bf16[384,256]{1,0:T(8,128)(2,1)S(1)} %get-tuple-element.26), channel_id=1, source_target_pairs={{0,192},{192,384},{384,576},{576,0},{1,193},{193,385},{385,577},{5... | collective-permute-start | bytes 589832 | tf_op jit(solution)/shard_map/ppermute | solution.py:22
  113.4 0.1 broadcast_subtract_fusion
  113.4 0.1 sub.27.row_term
  113.6 1.0 collective-permute-done.5.own1
  114.5 3.5 %collective-permute-done.6.own2 = bf16[384,256]{1,0:T(8,128)(2,1)S(1)} collective-permute-done((bf16[384,256]{1,0:T(8,128)(2,1)}, bf16[384,256]{1,0:T(8,128)(2,1)S(1)}, u32[]{:S(2)}, u32[]{:S(2)}) %collective-permute-start.6) | collective-permute-done | bytes 196640 | tf_op jit(solution)/shard_map/ppermute | solution.py:22
  118.1 6.4 %collective-permute-done.7.own3 = bf16[384,256]{1,0:T(8,128)(2,1)S(1)} collective-permute-done((bf16[384,256]{1,0:T(8,128)(2,1)S(1)}, bf16[384,256]{1,0:T(8,128)(2,1)S(1)}, u32[]{:S(2)}, u32[]{:S(2)}) %collective-permute-start.7) | collective-permute-done | bytes 196640 | tf_op jit(solution)/shard_map/ppermute | solution.py:22
  124.4 14.8 %all-to-all-done.2 = bf16[96,16,256]{2,1,0:T(8,128)(2,1)S(1)} async-done(((bf16[96,16,256]{2,1,0:T(8,128)(2,1)}), bf16[96,16,256]{2,1,0:T(8,128)(2,1)S(1)}, u32[]{:S(2)}, u32[]{:S(2)}) %all-to-all-start.2) | async-done | bytes 786464 | tf_op jit(solution)/shard_map/all_to_all | solution.py:137
  139.3 2.5 %finish.1 = bf16[256,1536]{1,0:T(8,128)(2,1)} custom-call(s32[2]{0:T(128)S(1)} %pad_add_fusion.place, bf16[4,24,16,256]{3,2,1,0:T(8,128)(2,1)S(1)} %bitcast.16, bf16[384,256]{1,0:T(8,128)(2,1)S(1)} %get-tuple-element.23.own0, bf16[384,256]{1,0:T(8,128)(2,1)S(1)} %collective-permute-done.5.own1, bf16[384,256]{1,0:T(8,128)(2,1)S(1)} %collective-permute-done.6.own2, ...), custom_call_target="tpu_custom_call" | custom-call | flops 600000000 | bytes 4000000 | tf_op jit(solution)/shard_map/finish/pallas_call | solution.py:149
  (15 shorter events, 0.1 us)
Async XLA Ops:
  1.2 28.1 %collective-permute-start = (bf16[128,1536]{1,0:T(8,128)(2,1)S(1)}, bf16[128,1536]{1,0:T(8,128)(2,1)S(1)}, u32[]{:S(2)}, u32[]{:S(2)}) collective-permute-start(bf16[128,1536]{1,0:T(8,128)(2,1)S(1)} %bitcast.22), channel_id=1, source_target_pairs={{0,384},{192,576},{384,0},{576,192},{1,385},{193,577},{385,1},{577... | collective-permute-start | bytes 1179656 | tf_op jit(solution)/shard_map/ppermute | solution.py:22
  6.7 1.6 %copy-start.7 = (bf16[64,48]{0,1:T(8,128)(2,1)S(1)}, bf16[64,48]{0,1:T(8,128)(2,1)}, u32[]{:S(2)}) copy-start(bf16[64,48]{0,1:T(8,128)(2,1)} %param.6) | copy-start | bytes 18436
  9.3 19.6 %all-to-all-start = ((bf16[32,2,384]{2,1,0:T(2,128)(2,1)}), bf16[32,2,384]{2,1,0:T(2,128)(2,1)S(1)}, u32[]{:S(2)}, u32[]{:S(2)}) async-start(bf16[32,2,384]{2,1,0:T(2,128)(2,1)} %reshape.91), calls=%async_computation | async-start | bytes 98304 | tf_op jit(solution)/shard_map/all_to_all | solution.py:116
  29.3 14.5 %copy-start = (bf16[1,2,2,64,1536]{4,3,2,1,0:T(8,128)(2,1)S(1)}, bf16[1,2,2,64,1536]{4,3,2,1,0:T(8,128)(2,1)}, u32[]{:S(2)}) copy-start(bf16[1,2,2,64,1536]{4,3,2,1,0:T(8,128)(2,1)} %param.5) | copy-start | bytes 2359300
  29.3 0.9 copy-start.3
  30.2 43.7 %all-to-all-start.1 = ((bf16[24,16,768]{2,1,0:T(8,128)(2,1)}), bf16[24,16,768]{2,1,0:T(8,128)(2,1)S(1)}, u32[]{:S(2)}, u32[]{:S(2)}) async-start(bf16[24,16,768]{2,1,0:T(8,128)(2,1)} %broadcast_in_dim.13), calls=%async_computation.1 | async-start | bytes 1179648 | tf_op jit(solution)/shard_map/all_to_all | solution.py:121
  43.7 29.3 %collective-permute-start.1 = (bf16[256,1536]{1,0:T(8,128)(2,1)S(1)}, bf16[256,1536]{1,0:T(8,128)(2,1)S(1)}, u32[]{:S(2)}, u32[]{:S(2)}) collective-permute-start(bf16[256,1536]{1,0:T(8,128)(2,1)S(1)} %bitcast.12), channel_id=1, source_target_pairs={{0,192},{192,384},{384,576},{576,0},{1,193},{193,385},{385,577},{5... | collective-permute-start | bytes 2359304 | tf_op jit(solution)/shard_map/ppermute | solution.py:22
  45.7 27.4 %collective-permute-start.2 = (bf16[256,1536]{1,0:T(8,128)(2,1)S(1)}, bf16[256,1536]{1,0:T(8,128)(2,1)S(1)}, u32[]{:S(2)}, u32[]{:S(2)}) collective-permute-start(bf16[256,1536]{1,0:T(8,128)(2,1)S(1)} %bitcast.13), channel_id=1, source_target_pairs={{0,576},{192,0},{384,192},{576,384},{1,577},{193,1},{385,193},{577... | collective-permute-start | bytes 2359304 | tf_op jit(solution)/shard_map/ppermute | solution.py:22
  50.2 22.0 %collective-permute-start.3 = (bf16[128,1536]{1,0:T(8,128)(2,1)S(1)}, bf16[128,1536]{1,0:T(8,128)(2,1)S(1)}, u32[]{:S(2)}, u32[]{:S(2)}) collective-permute-start(bf16[128,1536]{1,0:T(8,128)(2,1)S(1)} %bitcast.21), channel_id=1, source_target_pairs={{0,384},{192,576},{384,0},{576,192},{1,385},{193,577},{385,1},{577... | collective-permute-start | bytes 1179656 | tf_op jit(solution)/shard_map/ppermute | solution.py:22
  72.2 0.8 copy-start.5
  73.0 0.9 copy-start.1
  73.9 6.9 %collective-permute-start.4 = (bf16[384,768]{1,0:T(8,128)(2,1)S(1)}, bf16[384,768]{1,0:T(8,128)(2,1)S(1)}, u32[]{:S(2)}, u32[]{:S(2)}) collective-permute-start(bf16[384,768]{1,0:T(8,128)(2,1)S(1)} %bitcast.17), channel_id=1, source_target_pairs={{0,24},{24,0},{1,25},{25,1},{2,26},{26,2},{3,27},{27,3},{4,28},{28... | collective-permute-start | bytes 1769480 | tf_op jit(solution)/shard_map/ppermute | solution.py:22
  80.8 1.1 copy-start.2
  81.9 1.0 copy-start.4
  82.9 1.0 copy-start.6
  87.1 17.0 %copy-start.9 = (f32[64]{0:T(128)S(1)}, f32[64]{0:T(128)}, u32[]{:S(2)}) copy-start(f32[64]{0:T(128)} %param.8) | copy-start | bytes 772
  87.1 52.1 %all-to-all-start.2 = ((bf16[96,16,256]{2,1,0:T(8,128)(2,1)}), bf16[96,16,256]{2,1,0:T(8,128)(2,1)S(1)}, u32[]{:S(2)}, u32[]{:S(2)}) async-start(bf16[96,16,256]{2,1,0:T(8,128)(2,1)} %bitcast.9), calls=%async_computation.2 | async-start | bytes 1572864 | tf_op jit(solution)/shard_map/all_to_all | solution.py:137
  103.3 0.7 copy-start.8
  104.2 10.3 %collective-permute-start.5 = (bf16[384,256]{1,0:T(8,128)(2,1)}, bf16[384,256]{1,0:T(8,128)(2,1)S(1)}, u32[]{:S(2)}, u32[]{:S(2)}) collective-permute-start(bf16[384,256]{1,0:T(8,128)(2,1)} %get-tuple-element.24), channel_id=1, source_target_pairs={{0,576},{192,0},{384,192},{576,384},{1,577},{193,1},{385,193},{577... | collective-permute-start | bytes 589832 | tf_op jit(solution)/shard_map/ppermute | solution.py:22
  108.5 9.5 %collective-permute-start.6 = (bf16[384,256]{1,0:T(8,128)(2,1)}, bf16[384,256]{1,0:T(8,128)(2,1)S(1)}, u32[]{:S(2)}, u32[]{:S(2)}) collective-permute-start(bf16[384,256]{1,0:T(8,128)(2,1)} %get-tuple-element.25), channel_id=1, source_target_pairs={{0,384},{192,576},{384,0},{576,192},{1,385},{193,577},{385,1},{577... | collective-permute-start | bytes 589832 | tf_op jit(solution)/shard_map/ppermute | solution.py:22
  110.7 13.8 %collective-permute-start.7 = (bf16[384,256]{1,0:T(8,128)(2,1)S(1)}, bf16[384,256]{1,0:T(8,128)(2,1)S(1)}, u32[]{:S(2)}, u32[]{:S(2)}) collective-permute-start(bf16[384,256]{1,0:T(8,128)(2,1)S(1)} %get-tuple-element.26), channel_id=1, source_target_pairs={{0,192},{192,384},{384,576},{576,0},{1,193},{193,385},{385,577},{5... | collective-permute-start | bytes 589832 | tf_op jit(solution)/shard_map/ppermute | solution.py:22

commit v3 on v2

--- a/solution.py
+++ b/solution.py
@@ -25,6 +25,7 @@
 def cycle_kernel(place, mine, theirs, t0, t1, t2a, t2b, t3, mirror, own0, own1, own2, own3):
     x, c = place[0], place[1]
     half = mine.shape[1]
+    quarter = mirror.shape[1] // X
     here = pl.ds(pl.multiple_of(c * half, 128), half)
     there = pl.ds(pl.multiple_of((1 - c) * half, 128), half)
 
@@ -39,16 +40,17 @@
         for part in parts:
             value = product(part)
             lanes = slice(first, first + part.shape[0])
-            mirror[slot, :, lanes] = value
+            mirror[:, pl.ds(pl.multiple_of(slot * quarter, quarter), quarter), lanes] = value.reshape(
+                NVIRT, quarter, part.shape[0]
+            )
             own[:, lanes] = value
             first += part.shape[0]
 
 
 def finish_kernel(place, arrived, own0, own1, own2, own3, t, row_term, virt, out, own_rows):
     x = place[0]
-    quarter = arrived.shape[2]
-    width = X * quarter
-    lanes = arrived.shape[3]
+    width, lanes = arrived.shape[1:]
+    quarter = width // X
     pieces = lanes // width
     for steps, own in enumerate((own0, own1, own2, own3)):
         slot = lax.rem(x + steps, X)
@@ -71,7 +73,7 @@
             NT,
             preferred_element_type=F32,
         )
-        sent = [arrived[:, 4 * group + k].reshape(width, lanes) for k in range(4)]
+        sent = [arrived[4 * group + k] for k in range(4)]
         stacked = jnp.concatenate(
             [
                 jnp.concatenate([sent[0], sent[1]], axis=1),
@@ -101,8 +103,6 @@
     place = lax.axis_index(VIRT)
     spot = jnp.stack([lax.axis_index("x"), lax.axis_index("c")]).astype(jnp.int32)
 
-    t2a = passed_along(flat[: lanes // 2], "x", 2)
-    t2b = passed_along(flat[lanes // 2 :], "x", 2)
     t1 = passed_along(flat, "x", 1)
     t3 = passed_along(flat, "x", 3)
 
@@ -116,27 +116,29 @@
     rows = lax.all_to_all(sent, PAIR, split_axis=0, concat_axis=0, tiled=True)
     rows = jnp.transpose(rows, (1, 0, 2)).reshape(quarter, virt_total)
     rows = lax.dynamic_slice_in_dim(rows, lax.axis_index("c") * (virt_total // 2), virt_total // 2, axis=1)
-    rows, t2a = lax.optimization_barrier((rows, t2a))
+    rows, t1, t3 = lax.optimization_barrier((rows, t1, t3))
+    t2a = passed_along(t1[: lanes // 2], "x", 1)
+    t2b = passed_along(t3[lanes // 2 :], "x", 3)
     copies = jnp.broadcast_to(rows[None], (NVIRT,) + rows.shape)
     mine = lax.all_to_all(copies, VIRT, split_axis=0, concat_axis=0, tiled=True)
-    mine, t1, t3, t2b = lax.optimization_barrier((mine, t1, t3, t2b))
+    mine, t2a, t2b = lax.optimization_barrier((mine, t2a, t2b))
     mine = mine.reshape(NVIRT * quarter, virt_total // 2)
     theirs = passed_along(mine, "c", 1)
 
     share = jax.ShapeDtypeStruct((NVIRT * quarter, lanes), BF16)
     mirror, own0, own1, own2, own3 = pl.pallas_call(
         cycle_kernel,
-        out_shape=[jax.ShapeDtypeStruct((X,) + share.shape, BF16)] + [share] * X,
+        out_shape=[jax.ShapeDtypeStruct((NVIRT, width, lanes), BF16)] + [share] * X,
         in_specs=[SMEM] + [VMEM] * 7,
         out_specs=[VMEM] * 5,
         cost_estimate=pl.CostEstimate(flops=1_210_000_000, bytes_accessed=6_000_000, transcendentals=0),
-        compiler_params=pltpu.CompilerParams(vmem_limit_bytes=24 * 2**20),
+        compiler_params=pltpu.CompilerParams(vmem_limit_bytes=12 * 2**20),
         name="cycle",
     )(spot, mine, theirs, flat, t1, t2a, t2b, t3)
 
     arrived = lax.all_to_all(
-        mirror.reshape(X * NVIRT, quarter, lanes), ("x",) + VIRT, split_axis=0, concat_axis=0, tiled=True
-    ).reshape(X, NVIRT, quarter, lanes)
+        mirror.reshape(NVIRT * X, quarter, lanes), VIRT + ("x",), split_axis=0, concat_axis=0, tiled=True
+    ).reshape(NVIRT, width, lanes)
     own1 = passed_along(own1, "x", -1)
     own2 = passed_along(own2, "x", -2)
     own3 = passed_along(own3, "x", -3)
@@ -153,7 +155,7 @@
         out_specs=VMEM,
         scratch_shapes=[pltpu.VMEM((NVIRT, width, lanes), BF16)],
         cost_estimate=pl.CostEstimate(flops=600_000_000, bytes_accessed=4_000_000, transcendentals=0),
-        compiler_params=pltpu.CompilerParams(vmem_limit_bytes=24 * 2**20),
+        compiler_params=pltpu.CompilerParams(vmem_limit_bytes=12 * 2**20),
         name="finish",
     )(spot, arrived, own0, own1, own2, own3, flat, row_term, virt_energy[None, :])
     return updated.reshape(amplitudes.shape)

time: 143 us -> 130 us (0.909)
  the two profiles are of different devices: /device:TPU:1 before, /device:TPU:192 now
where the time goes in v3:
time: 130 us
  starting transfers between devices  63.5 us (49%)
  waiting for transfers between devices  49.7 us (38%)
  local copies, waits for them, and re-layouts  10.3 us (8%)
  Pallas kernels  5.53 us (4%)
    ppermute x8, starting transfers between devices, passed_along(): return lax.ppermute(value, axis, pairs)  26.1 us
    ppermute x8, waiting for transfers between devices, passed_along(): return lax.ppermute(value, axis, pairs)  18.8 us
    all_to_all x1, starting transfers between devices, local(): mine = lax.all_to_all(copies, VIRT, split_axis=0, concat_axis=0, tiled=True)  16.6 us
    all_to_all x1, waiting for transfers between devices, local(): lax.all_to_all(mirror.reshape(NVIRT * X, quarter, lanes), VIRT + ('x',),...  15.3 us
    all_to_all x1, waiting for transfers between devices, local(): mine = lax.all_to_all(copies, VIRT, split_axis=0, concat_axis=0, tiled=True)  10.7 us
    all_to_all x1, starting transfers between devices, local(): rows = lax.all_to_all(sent, PAIR, split_axis=0, concat_axis=0, tiled=True)  10.4 us
    all_to_all x1, starting transfers between devices, local(): lax.all_to_all(mirror.reshape(NVIRT * X, quarter, lanes), VIRT + ('x',),...  10.3 us
    unnamed x31, local copies, waits for them, and re-layouts  7.29 us
  transfers between devices with their start and end apart: 11, of which 9 were waited for; matrix products, arithmetic and copies ran while one was open for 3% of the time, Pallas kernels for 0%

profile of v3, /device:TPU:192, one launch (start us, length us, event | category | flops | bytes accessed | tf_op | source)
XLA Modules:
  0.0 129.6 jit_solution(1786256004657962059)
XLA Ops:
  0.0 3.4 %collective-permute-start = (bf16[256,1536]{1,0:T(8,128)(2,1)}, bf16[256,1536]{1,0:T(8,128)(2,1)S(1)}, u32[]{:S(2)}, u32[]{:S(2)}) collective-permute-start(bf16[256,1536]{1,0:T(8,128)(2,1)} %bitcast.11), channel_id=1, source_target_pairs={{0,192},{192,384},{384,576},{576,0},{1,193},{193,385},{385,577},{5... | collective-permute-start | bytes 2359304 | tf_op jit(solution)/shard_map/ppermute | solution.py:22
  3.4 3.7 %collective-permute-start.1 = (bf16[256,1536]{1,0:T(8,128)(2,1)}, bf16[256,1536]{1,0:T(8,128)(2,1)S(1)}, u32[]{:S(2)}, u32[]{:S(2)}) collective-permute-start(bf16[256,1536]{1,0:T(8,128)(2,1)} %bitcast.12), channel_id=1, source_target_pairs={{0,576},{192,0},{384,192},{576,384},{1,577},{193,1},{385,193},{577... | collective-permute-start | bytes 2359304 | tf_op jit(solution)/shard_map/ppermute | solution.py:22
  7.1 0.8 dynamic_slice.19
  7.9 0.8 dynamic_slice.18
  8.6 0.1 copy.12
  8.7 0.1 compare_select_fusion
  8.8 0.8 reshape.89
  9.7 10.4 %all-to-all-start = ((bf16[32,2,384]{2,1,0:T(2,128)(2,1)}), bf16[32,2,384]{2,1,0:T(2,128)(2,1)S(1)}, u32[]{:S(2)}, u32[]{:S(2)}) async-start(bf16[32,2,384]{2,1,0:T(2,128)(2,1)} %reshape.89), calls=%async_computation | async-start | bytes 98304 | tf_op jit(solution)/shard_map/all_to_all | solution.py:116
  20.1 5.0 %all-to-all-done = bf16[32,2,384]{2,1,0:T(2,128)(2,1)S(1)} async-done(((bf16[32,2,384]{2,1,0:T(2,128)(2,1)}), bf16[32,2,384]{2,1,0:T(2,128)(2,1)S(1)}, u32[]{:S(2)}, u32[]{:S(2)}) %all-to-all-start) | async-done | bytes 49184 | tf_op jit(solution)/shard_map/all_to_all | solution.py:116
  25.1 0.2 reshape.90
  25.3 0.2 reshape.83
  25.5 0.0 collective-permute-done.t1
  25.5 0.0 collective-permute-done.1.t3
  25.5 0.9 broadcast_in_dim.13
  26.4 16.6 %all-to-all-start.1 = ((bf16[24,16,768]{2,1,0:T(8,128)(2,1)}), bf16[24,16,768]{2,1,0:T(8,128)(2,1)S(1)}, u32[]{:S(2)}, u32[]{:S(2)}) async-start(bf16[24,16,768]{2,1,0:T(8,128)(2,1)} %broadcast_in_dim.13), calls=%async_computation.1 | async-start | bytes 1179648 | tf_op jit(solution)/shard_map/all_to_all | solution.py:123
  43.0 0.0 copy-start
  43.1 4.2 %collective-permute-start.2 = (bf16[128,1536]{1,0:T(8,128)(2,1)S(1)}, bf16[128,1536]{1,0:T(8,128)(2,1)S(1)}, u32[]{:S(2)}, u32[]{:S(2)}) collective-permute-start(bf16[128,1536]{1,0:T(8,128)(2,1)S(1)} %slice.6), channel_id=1, source_target_pairs={{0,192},{192,384},{384,576},{576,0},{1,193},{193,385},{385,577},{5... | collective-permute-start | bytes 1179656 | tf_op jit(solution)/shard_map/ppermute | solution.py:22
  47.3 3.0 %collective-permute-start.3 = (bf16[128,1536]{1,0:T(8,128)(2,1)S(1)}, bf16[128,1536]{1,0:T(8,128)(2,1)S(1)}, u32[]{:S(2)}, u32[]{:S(2)}) collective-permute-start(bf16[128,1536]{1,0:T(8,128)(2,1)S(1)} %slice.7), channel_id=1, source_target_pairs={{0,576},{192,0},{384,192},{576,384},{1,577},{193,1},{385,193},{577... | collective-permute-start | bytes 1179656 | tf_op jit(solution)/shard_map/ppermute | solution.py:22
  50.3 6.9 %collective-permute-done.2.t2a = bf16[128,1536]{1,0:T(8,128)(2,1)S(1)} collective-permute-done((bf16[128,1536]{1,0:T(8,128)(2,1)S(1)}, bf16[128,1536]{1,0:T(8,128)(2,1)S(1)}, u32[]{:S(2)}, u32[]{:S(2)}) %collective-permute-start.2) | collective-permute-done | bytes 393248 | tf_op jit(solution)/shard_map/ppermute | solution.py:22
  57.2 0.8 copy-done.1
  58.0 1.5 %collective-permute-done.3.t2b = bf16[128,1536]{1,0:T(8,128)(2,1)S(1)} collective-permute-done((bf16[128,1536]{1,0:T(8,128)(2,1)S(1)}, bf16[128,1536]{1,0:T(8,128)(2,1)S(1)}, u32[]{:S(2)}, u32[]{:S(2)}) %collective-permute-start.3) | collective-permute-done | bytes 393248 | tf_op jit(solution)/shard_map/ppermute | solution.py:22
  59.5 0.7 copy-done.3
  60.2 10.7 %all-to-all-done.1 = bf16[24,16,768]{2,1,0:T(8,128)(2,1)S(1)} async-done(((bf16[24,16,768]{2,1,0:T(8,128)(2,1)}), bf16[24,16,768]{2,1,0:T(8,128)(2,1)S(1)}, u32[]{:S(2)}, u32[]{:S(2)}) %all-to-all-start.1) | async-done | bytes 589856 | tf_op jit(solution)/shard_map/all_to_all | solution.py:123
  70.9 1.9 %collective-permute-start.4 = (bf16[384,768]{1,0:T(8,128)(2,1)S(1)}, bf16[384,768]{1,0:T(8,128)(2,1)S(1)}, u32[]{:S(2)}, u32[]{:S(2)}) collective-permute-start(bf16[384,768]{1,0:T(8,128)(2,1)S(1)} %bitcast.15), channel_id=1, source_target_pairs={{0,24},{24,0},{1,25},{25,1},{2,26},{26,2},{3,27},{27,3},{4,28},{28... | collective-permute-start | bytes 1769480 | tf_op jit(solution)/shard_map/ppermute | solution.py:22
  72.8 0.1 pad_add_fusion.place
  72.9 1.9 %collective-permute-done.4.theirs = bf16[384,768]{1,0:T(8,128)(2,1)S(1)} collective-permute-done((bf16[384,768]{1,0:T(8,128)(2,1)S(1)}, bf16[384,768]{1,0:T(8,128)(2,1)S(1)}, u32[]{:S(2)}, u32[]{:S(2)}) %collective-permute-start.4) | collective-permute-done | bytes 589856 | tf_op jit(solution)/shard_map/ppermute | solution.py:22
  74.8 1.0 copy-done.2
  75.8 1.0 copy-done.4
  76.8 3.1 %cycle.1 = (bf16[24,64,256]{2,1,0:T(8,128)(2,1)}, bf16[384,256]{1,0:T(8,128)(2,1)S(1)}, bf16[384,256]{1,0:T(8,128)(2,1)S(1)}, bf16[384,256]{1,0:T(8,128)(2,1)S(1)}, bf16[384,256]{1,0:T(8,128)(2,1)S(1)}) custom-call(s32[2]{0:T(128)S(1)} %pad_add_fusion.place, bf16[384,768]{1,0:T(8,128)(2,1)S(1)} %bitcast.16, ...), custom_call_target="tpu_custom_call" | custom-call | flops 1210000000 | bytes 6000000 | tf_op jit(solution)/shard_map/cycle/pallas_call | solution.py:129
  79.9 0.7 copy-done.5
  80.6 0.7 copy-done.7
  81.2 0.7 copy-done.9
  81.9 10.3 %all-to-all-start.2 = ((bf16[96,16,256]{2,1,0:T(8,128)(2,1)}), bf16[96,16,256]{2,1,0:T(8,128)(2,1)S(1)}, u32[]{:S(2)}, u32[]{:S(2)}) async-start(bf16[96,16,256]{2,1,0:T(8,128)(2,1)} %bitcast.7), calls=%async_computation.2 | async-start | bytes 1572864 | tf_op jit(solution)/shard_map/all_to_all | solution.py:139
  92.3 0.0 copy-start.12
  92.3 0.7 copy-done.12
  93.0 0.1 dynamic_slice.23
  93.0 0.1 fusion
  93.1 0.1 broadcast_add_fusion
  93.2 4.5 %collective-permute-start.5 = (bf16[384,256]{1,0:T(8,128)(2,1)S(1)}, bf16[384,256]{1,0:T(8,128)(2,1)S(1)}, u32[]{:S(2)}, u32[]{:S(2)}) collective-permute-start(bf16[384,256]{1,0:T(8,128)(2,1)S(1)} %copy-done.10), channel_id=1, source_target_pairs={{0,576},{192,0},{384,192},{576,384},{1,577},{193,1},{385,193},{577... | collective-permute-start | bytes 589832 | tf_op jit(solution)/shard_map/ppermute | solution.py:22
  97.7 2.8 %collective-permute-start.6 = (bf16[384,256]{1,0:T(8,128)(2,1)S(1)}, bf16[384,256]{1,0:T(8,128)(2,1)S(1)}, u32[]{:S(2)}, u32[]{:S(2)}) collective-permute-start(bf16[384,256]{1,0:T(8,128)(2,1)S(1)} %copy-done.8), channel_id=1, source_target_pairs={{0,384},{192,576},{384,0},{576,192},{1,385},{193,577},{385,1},{577... | collective-permute-start | bytes 589832 | tf_op jit(solution)/shard_map/ppermute | solution.py:22
  100.5 2.8 %collective-permute-start.7 = (bf16[384,256]{1,0:T(8,128)(2,1)S(1)}, bf16[384,256]{1,0:T(8,128)(2,1)S(1)}, u32[]{:S(2)}, u32[]{:S(2)}) collective-permute-start(bf16[384,256]{1,0:T(8,128)(2,1)S(1)} %copy-done.6), channel_id=1, source_target_pairs={{0,192},{192,384},{384,576},{576,0},{1,193},{193,385},{385,577},{5... | collective-permute-start | bytes 589832 | tf_op jit(solution)/shard_map/ppermute | solution.py:22
  103.2 0.1 broadcast_subtract_fusion
  103.3 0.1 sub.27.row_term
  103.5 3.3 %collective-permute-done.5.own1 = bf16[384,256]{1,0:T(8,128)(2,1)S(1)} collective-permute-done((bf16[384,256]{1,0:T(8,128)(2,1)S(1)}, bf16[384,256]{1,0:T(8,128)(2,1)S(1)}, u32[]{:S(2)}, u32[]{:S(2)}) %collective-permute-start.5) | collective-permute-done | bytes 196640 | tf_op jit(solution)/shard_map/ppermute | solution.py:22
  106.8 2.5 %collective-permute-done.6.own2 = bf16[384,256]{1,0:T(8,128)(2,1)S(1)} collective-permute-done((bf16[384,256]{1,0:T(8,128)(2,1)S(1)}, bf16[384,256]{1,0:T(8,128)(2,1)S(1)}, u32[]{:S(2)}, u32[]{:S(2)}) %collective-permute-start.6) | collective-permute-done | bytes 196640 | tf_op jit(solution)/shard_map/ppermute | solution.py:22
  109.3 2.7 %collective-permute-done.7.own3 = bf16[384,256]{1,0:T(8,128)(2,1)S(1)} collective-permute-done((bf16[384,256]{1,0:T(8,128)(2,1)S(1)}, bf16[384,256]{1,0:T(8,128)(2,1)S(1)}, u32[]{:S(2)}, u32[]{:S(2)}) %collective-permute-start.7) | collective-permute-done | bytes 196640 | tf_op jit(solution)/shard_map/ppermute | solution.py:22
  112.0 15.3 %all-to-all-done.2 = bf16[96,16,256]{2,1,0:T(8,128)(2,1)S(1)} async-done(((bf16[96,16,256]{2,1,0:T(8,128)(2,1)}), bf16[96,16,256]{2,1,0:T(8,128)(2,1)S(1)}, u32[]{:S(2)}, u32[]{:S(2)}) %all-to-all-start.2) | async-done | bytes 786464 | tf_op jit(solution)/shard_map/all_to_all | solution.py:139
  127.2 2.4 %finish.1 = bf16[256,1536]{1,0:T(8,128)(2,1)} custom-call(s32[2]{0:T(128)S(1)} %pad_add_fusion.place, bf16[24,64,256]{2,1,0:T(8,128)(2,1)S(1)} %bitcast.10, bf16[384,256]{1,0:T(8,128)(2,1)S(1)} %get-tuple-element.23.own0, bf16[384,256]{1,0:T(8,128)(2,1)S(1)} %collective-permute-done.5.own1, bf16[384,256]{1,0:T(8,128)(2,1)S(1)} %collective-permute-done.6.own2, ...), custom_call_target="tpu_custom_call" | custom-call | flops 600000000 | bytes 4000000 | tf_op jit(solution)/shard_map/finish/pallas_call | solution.py:151
  (24 shorter events, 0.2 us)
Async XLA Ops:
  0.0 25.5 %collective-permute-start = (bf16[256,1536]{1,0:T(8,128)(2,1)}, bf16[256,1536]{1,0:T(8,128)(2,1)S(1)}, u32[]{:S(2)}, u32[]{:S(2)}) collective-permute-start(bf16[256,1536]{1,0:T(8,128)(2,1)} %bitcast.11), channel_id=1, source_target_pairs={{0,192},{192,384},{384,576},{576,0},{1,193},{193,385},{385,577},{5... | collective-permute-start | bytes 2359304 | tf_op jit(solution)/shard_map/ppermute | solution.py:22
  3.4 22.1 %collective-permute-start.1 = (bf16[256,1536]{1,0:T(8,128)(2,1)}, bf16[256,1536]{1,0:T(8,128)(2,1)S(1)}, u32[]{:S(2)}, u32[]{:S(2)}) collective-permute-start(bf16[256,1536]{1,0:T(8,128)(2,1)} %bitcast.12), channel_id=1, source_target_pairs={{0,576},{192,0},{384,192},{576,384},{1,577},{193,1},{385,193},{577... | collective-permute-start | bytes 2359304 | tf_op jit(solution)/shard_map/ppermute | solution.py:22
  7.1 1.6 %copy-start.11 = (bf16[64,48]{0,1:T(8,128)(2,1)S(1)}, bf16[64,48]{0,1:T(8,128)(2,1)}, u32[]{:S(2)}) copy-start(bf16[64,48]{0,1:T(8,128)(2,1)} %param.6) | copy-start | bytes 18436
  9.7 15.4 %all-to-all-start = ((bf16[32,2,384]{2,1,0:T(2,128)(2,1)}), bf16[32,2,384]{2,1,0:T(2,128)(2,1)S(1)}, u32[]{:S(2)}, u32[]{:S(2)}) async-start(bf16[32,2,384]{2,1,0:T(2,128)(2,1)} %reshape.89), calls=%async_computation | async-start | bytes 98304 | tf_op jit(solution)/shard_map/all_to_all | solution.py:116
  26.4 44.5 %all-to-all-start.1 = ((bf16[24,16,768]{2,1,0:T(8,128)(2,1)}), bf16[24,16,768]{2,1,0:T(8,128)(2,1)S(1)}, u32[]{:S(2)}, u32[]{:S(2)}) async-start(bf16[24,16,768]{2,1,0:T(8,128)(2,1)} %broadcast_in_dim.13), calls=%async_computation.1 | async-start | bytes 1179648 | tf_op jit(solution)/shard_map/all_to_all | solution.py:123
  43.0 31.7 %copy-start = (bf16[1,2,2,64,1536]{4,3,2,1,0:T(8,128)(2,1)S(1)}, bf16[1,2,2,64,1536]{4,3,2,1,0:T(8,128)(2,1)}, u32[]{:S(2)}) copy-start(bf16[1,2,2,64,1536]{4,3,2,1,0:T(8,128)(2,1)} %param.5) | copy-start | bytes 2359300
  43.1 14.1 %collective-permute-start.2 = (bf16[128,1536]{1,0:T(8,128)(2,1)S(1)}, bf16[128,1536]{1,0:T(8,128)(2,1)S(1)}, u32[]{:S(2)}, u32[]{:S(2)}) collective-permute-start(bf16[128,1536]{1,0:T(8,128)(2,1)S(1)} %slice.6), channel_id=1, source_target_pairs={{0,192},{192,384},{384,576},{576,0},{1,193},{193,385},{385,577},{5... | collective-permute-start | bytes 1179656 | tf_op jit(solution)/shard_map/ppermute | solution.py:22
  47.3 12.1 %collective-permute-start.3 = (bf16[128,1536]{1,0:T(8,128)(2,1)S(1)}, bf16[128,1536]{1,0:T(8,128)(2,1)S(1)}, u32[]{:S(2)}, u32[]{:S(2)}) collective-permute-start(bf16[128,1536]{1,0:T(8,128)(2,1)S(1)} %slice.7), channel_id=1, source_target_pairs={{0,576},{192,0},{384,192},{576,384},{1,577},{193,1},{385,193},{577... | collective-permute-start | bytes 1179656 | tf_op jit(solution)/shard_map/ppermute | solution.py:22
  57.2 0.8 copy-start.1
  59.5 0.8 copy-start.3
  70.9 3.9 %collective-permute-start.4 = (bf16[384,768]{1,0:T(8,128)(2,1)S(1)}, bf16[384,768]{1,0:T(8,128)(2,1)S(1)}, u32[]{:S(2)}, u32[]{:S(2)}) collective-permute-start(bf16[384,768]{1,0:T(8,128)(2,1)S(1)} %bitcast.15), channel_id=1, source_target_pairs={{0,24},{24,0},{1,25},{25,1},{2,26},{26,2},{3,27},{27,3},{4,28},{28... | collective-permute-start | bytes 1769480 | tf_op jit(solution)/shard_map/ppermute | solution.py:22
  74.8 1.0 copy-start.2
  75.8 1.0 copy-start.4
  79.9 0.7 copy-start.5
  80.6 0.7 copy-start.7
  81.2 0.7 copy-start.9
  81.9 11.1 %copy-start.13 = (f32[64]{0:T(128)S(1)}, f32[64]{0:T(128)}, u32[]{:S(2)}) copy-start(f32[64]{0:T(128)} %param.8) | copy-start | bytes 772
  81.9 11.3 %copy-start.10 = (bf16[384,256]{1,0:T(8,128)(2,1)S(1)}, bf16[384,256]{1,0:T(8,128)(2,1)}, u32[]{:S(2)}) copy-start(bf16[384,256]{1,0:T(8,128)(2,1)} %copy-done.9) | copy-start | bytes 589828
  81.9 15.7 %copy-start.8 = (bf16[384,256]{1,0:T(8,128)(2,1)S(1)}, bf16[384,256]{1,0:T(8,128)(2,1)}, u32[]{:S(2)}) copy-start(bf16[384,256]{1,0:T(8,128)(2,1)} %copy-done.7) | copy-start | bytes 589828
  81.9 18.5 %copy-start.6 = (bf16[384,256]{1,0:T(8,128)(2,1)S(1)}, bf16[384,256]{1,0:T(8,128)(2,1)}, u32[]{:S(2)}) copy-start(bf16[384,256]{1,0:T(8,128)(2,1)} %copy-done.5) | copy-start | bytes 589828
  81.9 45.3 %all-to-all-start.2 = ((bf16[96,16,256]{2,1,0:T(8,128)(2,1)}), bf16[96,16,256]{2,1,0:T(8,128)(2,1)S(1)}, u32[]{:S(2)}, u32[]{:S(2)}) async-start(bf16[96,16,256]{2,1,0:T(8,128)(2,1)} %bitcast.7), calls=%async_computation.2 | async-start | bytes 1572864 | tf_op jit(solution)/shard_map/all_to_all | solution.py:139
  92.3 0.7 copy-start.12
  93.2 13.6 %collective-permute-start.5 = (bf16[384,256]{1,0:T(8,128)(2,1)S(1)}, bf16[384,256]{1,0:T(8,128)(2,1)S(1)}, u32[]{:S(2)}, u32[]{:S(2)}) collective-permute-start(bf16[384,256]{1,0:T(8,128)(2,1)S(1)} %copy-done.10), channel_id=1, source_target_pairs={{0,576},{192,0},{384,192},{576,384},{1,577},{193,1},{385,193},{577... | collective-permute-start | bytes 589832 | tf_op jit(solution)/shard_map/ppermute | solution.py:22
  97.7 11.6 %collective-permute-start.6 = (bf16[384,256]{1,0:T(8,128)(2,1)S(1)}, bf16[384,256]{1,0:T(8,128)(2,1)S(1)}, u32[]{:S(2)}, u32[]{:S(2)}) collective-permute-start(bf16[384,256]{1,0:T(8,128)(2,1)S(1)} %copy-done.8), channel_id=1, source_target_pairs={{0,384},{192,576},{384,0},{576,192},{1,385},{193,577},{385,1},{577... | collective-permute-start | bytes 589832 | tf_op jit(solution)/shard_map/ppermute | solution.py:22
  100.5 11.5 %collective-permute-start.7 = (bf16[384,256]{1,0:T(8,128)(2,1)S(1)}, bf16[384,256]{1,0:T(8,128)(2,1)S(1)}, u32[]{:S(2)}, u32[]{:S(2)}) collective-permute-start(bf16[384,256]{1,0:T(8,128)(2,1)S(1)} %copy-done.6), channel_id=1, source_target_pairs={{0,192},{192,384},{384,576},{576,0},{1,193},{193,385},{385,577},{5... | collective-permute-start | bytes 589832 | tf_op jit(solution)/shard_map/ppermute | solution.py:22

commit v4 on v3

--- a/solution.py
+++ b/solution.py
@@ -1,3 +1,5 @@
+import functools
+
 import jax
 import jax.numpy as jnp
 from jax import lax
@@ -13,6 +15,7 @@
 BF16, F32 = jnp.bfloat16, jnp.float32
 VMEM = pl.BlockSpec(memory_space=pltpu.VMEM)
 SMEM = pl.BlockSpec(memory_space=pltpu.SMEM)
+HBM = pl.BlockSpec(memory_space=pltpu.HBM)
 NT = (((1,), (1,)), ((), ()))
 
 
@@ -22,29 +25,84 @@
     return lax.ppermute(value, axis, pairs)
 
 
-def cycle_kernel(place, mine, theirs, t0, t1, t2a, t2b, t3, mirror, own0, own1, own2, own3):
+def mask_kernel(place, irreps, rows, out):
+    total = irreps.shape[1]
+    lanes = rows.shape[1]
+    quarter = out.shape[1]
+    copies = out.shape[0] // X
+    labels = jnp.broadcast_to(irreps[...], (8, total))
+    of_row = pltpu.roll(labels, lax.rem(total - place[2], total), 1)[:1, :lanes].astype(F32)
+    of_column = pltpu.roll(labels, lax.rem(total - place[3], total), 1)[:1, :lanes].astype(F32)
+    of_row = jnp.transpose(jnp.broadcast_to(of_row, (lanes, lanes)))[: rows.shape[0]]
+    masked = jnp.where(of_row == of_column, rows[...].astype(F32), 0.0).astype(BF16)
+    for share in range(X):
+        piece = masked[share * quarter : (share + 1) * quarter]
+        for copy in range(copies):
+            out[share * copies + copy] = piece
+
+
+def gather_kernel(place, pieces, out, depth):
+    c = place[1]
+    quarter = pieces.shape[1]
+    count = pieces.shape[0] // 2
+    lane = lax.broadcasted_iota(jnp.int32, (quarter, 128), 1)
+    tiles = [jnp.zeros((quarter, 128), F32) for _ in range(out.shape[2] // 128)]
+    for number in range(count):
+        tile, start = divmod(number * depth, 128)
+        piece = pltpu.roll(pieces[c * count + number].astype(F32), start, 1)
+        if start + depth <= 128:
+            tiles[tile] += piece
+        else:
+            tiles[tile] += jnp.where(lane >= start, piece, 0.0)
+            tiles[tile + 1] += jnp.where(lane < start, piece, 0.0)
+    half = jnp.concatenate(tiles, axis=1).astype(BF16)
+    for copy in range(NVIRT):
+        out[copy] = half
+
+
+def cycle_kernel(
+    place, mine, theirs, t0, t1, t2a, t2b, t3, mirror, own0, own1, own2, own3, held, done, in_sems, out_sems
+):
     x, c = place[0], place[1]
     half = mine.shape[1]
     quarter = mirror.shape[1] // X
+    rows = t2a.shape[0]
     here = pl.ds(pl.multiple_of(c * half, 128), half)
     there = pl.ds(pl.multiple_of((1 - c) * half, 128), half)
-
-    def product(t):
-        total = lax.dot_general(mine[...], t[:, here], NT, preferred_element_type=F32)
-        total += lax.dot_general(theirs[...], t[:, there], NT, preferred_element_type=F32)
-        return total.astype(BF16)
-
-    for steps, parts, own in ((0, (t0,), own0), (1, (t1,), own1), (2, (t2a, t2b), own2), (3, (t3,), own3)):
+    loads = [
+        pltpu.make_async_copy(source, target, in_sems.at[number])
+        for number, (source, target) in enumerate(
+            (
+                (t0, held.at[0]),
+                (t1, held.at[1]),
+                (t3, held.at[3]),
+                (t2a, held.at[2, pl.ds(0, rows)]),
+                (t2b, held.at[2, pl.ds(rows, rows)]),
+            )
+        )
+    ]
+    for load in loads:
+        load.start()
+    stores = []
+    for steps, needed, own in (
+        (0, loads[:1], own0),
+        (1, loads[1:2], own1),
+        (3, loads[2:3], own3),
+        (2, loads[3:], own2),
+    ):
+        for load in needed:
+            load.wait()
+        total = lax.dot_general(mine[...], held[steps, :, here], NT, preferred_element_type=F32)
+        total += lax.dot_general(theirs[...], held[steps, :, there], NT, preferred_element_type=F32)
         slot = lax.rem(x + (X + X // 2 - steps), X)
-        first = 0
-        for part in parts:
-            value = product(part)
-            lanes = slice(first, first + part.shape[0])
-            mirror[:, pl.ds(pl.multiple_of(slot * quarter, quarter), quarter), lanes] = value.reshape(
-                NVIRT, quarter, part.shape[0]
-            )
-            own[:, lanes] = value
-            first += part.shape[0]
+        done[steps] = total.astype(BF16).reshape(done.shape[1:])
+        target = mirror.at[:, pl.ds(pl.multiple_of(slot * quarter, quarter), quarter), :]
+        for which, place_of in enumerate((own, target)):
+            store = pltpu.make_async_copy(done.at[steps], place_of, out_sems.at[steps, which])
+            store.start()
+            stores.append(store)
+    for store in stores:
+        store.wait()
 
 
 def finish_kernel(place, arrived, own0, own1, own2, own3, t, row_term, virt, out, own_rows):
@@ -54,9 +112,7 @@
     pieces = lanes // width
     for steps, own in enumerate((own0, own1, own2, own3)):
         slot = lax.rem(x + steps, X)
-        own_rows[:, pl.ds(pl.multiple_of(slot * quarter, quarter), quarter), :] = own[...].reshape(
-            NVIRT, quarter, lanes
-        )
+        own_rows[:, pl.ds(pl.multiple_of(slot * quarter, quarter), quarter), :] = own[...]
     rows = lax.broadcasted_iota(jnp.int32, (lanes, lanes), 0)
     columns = lax.broadcasted_iota(jnp.int32, (lanes, lanes), 1)
     unit = (rows == columns).astype(BF16)
@@ -101,36 +157,50 @@
     npair = X * ZL * C
     index = lax.axis_index(PAIR)
     place = lax.axis_index(VIRT)
-    spot = jnp.stack([lax.axis_index("x"), lax.axis_index("c")]).astype(jnp.int32)
+    spot = jnp.stack(
+        [lax.axis_index("x"), lax.axis_index("c"), place * width, index * depth]
+    ).astype(jnp.int32)
 
     t1 = passed_along(flat, "x", 1)
     t3 = passed_along(flat, "x", 3)
 
-    irreps_a = lax.dynamic_slice_in_dim(irreps, place * width, width)
-    irreps_c = lax.dynamic_slice_in_dim(irreps, index * depth, depth)
-    keep = irreps_a[:, None] == irreps_c[None, :]
-    masked = jnp.where(keep, integrals, jnp.zeros_like(integrals))
-    sent = jnp.broadcast_to(
-        masked.reshape(X, 1, quarter, depth), (X, ZL * C, quarter, depth)
-    ).reshape(npair, quarter, depth)
-    rows = lax.all_to_all(sent, PAIR, split_axis=0, concat_axis=0, tiled=True)
-    rows = jnp.transpose(rows, (1, 0, 2)).reshape(quarter, virt_total)
-    rows = lax.dynamic_slice_in_dim(rows, lax.axis_index("c") * (virt_total // 2), virt_total // 2, axis=1)
-    rows, t1, t3 = lax.optimization_barrier((rows, t1, t3))
+    sent = pl.pallas_call(
+        mask_kernel,
+        out_shape=jax.ShapeDtypeStruct((npair, quarter, 128), BF16),
+        in_specs=[SMEM, VMEM, VMEM],
+        out_specs=VMEM,
+        cost_estimate=pl.CostEstimate(flops=100_000, bytes_accessed=150_000, transcendentals=0),
+        name="mask",
+    )(spot, irreps[None, :], jnp.pad(integrals, ((0, 0), (0, 128 - depth))))
+    pieces = lax.all_to_all(sent, PAIR, split_axis=0, concat_axis=0, tiled=True)
+    pieces, t1, t3 = lax.optimization_barrier((pieces, t1, t3))
+    copies = pl.pallas_call(
+        functools.partial(gather_kernel, depth=depth),
+        out_shape=jax.ShapeDtypeStruct((NVIRT, quarter, virt_total // 2), BF16),
+        in_specs=[SMEM, VMEM],
+        out_specs=VMEM,
+        cost_estimate=pl.CostEstimate(flops=100_000, bytes_accessed=700_000, transcendentals=0),
+        name="gather",
+    )(spot, pieces)
     t2a = passed_along(t1[: lanes // 2], "x", 1)
     t2b = passed_along(t3[lanes // 2 :], "x", 3)
-    copies = jnp.broadcast_to(rows[None], (NVIRT,) + rows.shape)
     mine = lax.all_to_all(copies, VIRT, split_axis=0, concat_axis=0, tiled=True)
     mine, t2a, t2b = lax.optimization_barrier((mine, t2a, t2b))
     mine = mine.reshape(NVIRT * quarter, virt_total // 2)
     theirs = passed_along(mine, "c", 1)
 
-    share = jax.ShapeDtypeStruct((NVIRT * quarter, lanes), BF16)
+    share = jax.ShapeDtypeStruct((NVIRT, quarter, lanes), BF16)
     mirror, own0, own1, own2, own3 = pl.pallas_call(
         cycle_kernel,
         out_shape=[jax.ShapeDtypeStruct((NVIRT, width, lanes), BF16)] + [share] * X,
-        in_specs=[SMEM] + [VMEM] * 7,
-        out_specs=[VMEM] * 5,
+        in_specs=[SMEM] + [VMEM] * 2 + [HBM] * 5,
+        out_specs=[HBM] * 5,
+        scratch_shapes=[
+            pltpu.VMEM((X, lanes, virt_total), BF16),
+            pltpu.VMEM((X,) + share.shape, BF16),
+            pltpu.SemaphoreType.DMA((5,)),
+            pltpu.SemaphoreType.DMA((X, 2)),
+        ],
         cost_estimate=pl.CostEstimate(flops=1_210_000_000, bytes_accessed=6_000_000, transcendentals=0),
         compiler_params=pltpu.CompilerParams(vmem_limit_bytes=12 * 2**20),
         name="cycle",

time: 130 us -> 135 us (1.038)
  blocking collectives: 0 us -> 17.3 us
  starting transfers between devices: 63.5 us -> 50.2 us
  Pallas kernels: 5.53 us -> 11.9 us
  waiting for transfers between devices: 49.7 us -> 44.4 us
    all_to_all x0 -> x1, blocking collectives: none -> 17.3 us  [local(): pieces = lax.all_to_all(sent, PAIR, split_axis=0, concat_axis=0, tiled=True)]
    all_to_all x1 -> x0, starting transfers between devices: 10.4 us -> none  [local(): rows = lax.all_to_all(sent, PAIR, split_axis=0, concat_axis=0, tiled=True)]
    all_to_all x1 -> x0, waiting for transfers between devices: 5.03 us -> none  [local(): rows = lax.all_to_all(sent, PAIR, split_axis=0, concat_axis=0, tiled=True)]
    pallas_call x0 -> x2, Pallas kernels: none -> 3.43 us  [the longest x1 1.85 us: local(): pl.pallas_call(functools.partial(gather_kernel, depth=depth), out_shape=j...]
    all_to_all x1, starting transfers between devices: 16.6 us -> 13.3 us  [local(): mine = lax.all_to_all(copies, VIRT, split_axis=0, concat_axis=0, tiled=True)]
    pallas_call x1, Pallas kernels: 3.14 us -> 6.01 us  [local(): pl.pallas_call(cycle_kernel, out_shape=[jax.ShapeDtypeStruct((NVIRT, widt...]
    dynamic_slice x3 -> x0, local copies, waits for them, and re-layouts: 1.55 us -> none  [the longest x1 0.78 us: local(): irreps_c = lax.dynamic_slice_in_dim(irreps, index * depth, depth)]
    unnamed x31 -> x33, local copies, waits for them, and re-layouts: 7.29 us -> 7.6 us
  transfers between devices with their start and end apart: 11 -> 10, of which waited for: 9 -> 8; matrix products, arithmetic and copies ran while one was open for 3% -> 2% of each run, Pallas kernels for 0% -> 1%
where the time goes in v4:
time: 135 us; the launch traced here: 134 us
  starting transfers between devices  50.2 us (37%)
  waiting for transfers between devices  44.4 us (33%)
  blocking collectives  17.3 us (13%)
  Pallas kernels  11.9 us (9%)
  local copies, waits for them, and re-layouts  9.14 us (7%)
    ppermute x8, starting transfers between devices, passed_along(): return lax.ppermute(value, axis, pairs)  26.1 us
    ppermute x8, waiting for transfers between devices, passed_along(): return lax.ppermute(value, axis, pairs)  18.9 us
    all_to_all x1, blocking collectives, local(): pieces = lax.all_to_all(sent, PAIR, split_axis=0, concat_axis=0, tiled=True)  17.3 us
    all_to_all x1, waiting for transfers between devices, local(): lax.all_to_all(mirror.reshape(NVIRT * X, quarter, lanes), VIRT + ('x',),...  15.2 us
    all_to_all x1, starting transfers between devices, local(): mine = lax.all_to_all(copies, VIRT, split_axis=0, concat_axis=0, tiled=True)  13.3 us
    all_to_all x1, starting transfers between devices, local(): lax.all_to_all(mirror.reshape(NVIRT * X, quarter, lanes), VIRT + ('x',),...  10.8 us
    all_to_all x1, waiting for transfers between devices, local(): mine = lax.all_to_all(copies, VIRT, split_axis=0, concat_axis=0, tiled=True)  10.2 us
    unnamed x33, local copies, waits for them, and re-layouts  7.6 us
  transfers between devices with their start and end apart: 10, of which 8 were waited for; matrix products, arithmetic and copies ran while one was open for 2% of the time, Pallas kernels for 1%

profile of v4, /device:TPU:192, one launch (start us, length us, event | category | flops | bytes accessed | tf_op | source)
XLA Modules:
  0.0 134.0 jit_solution(10444057408269338406)
XLA Ops:
  0.0 3.4 %collective-permute-start = (bf16[256,1536]{1,0:T(8,128)(2,1)}, bf16[256,1536]{1,0:T(8,128)(2,1)S(1)}, u32[]{:S(2)}, u32[]{:S(2)}) collective-permute-start(bf16[256,1536]{1,0:T(8,128)(2,1)} %bitcast.10), channel_id=1, source_target_pairs={{0,192},{192,384},{384,576},{576,0},{1,193},{193,385},{385,577},{5... | collective-permute-start | bytes 2359304 | tf_op jit(solution)/shard_map/ppermute | solution.py:25
  3.4 3.7 %collective-permute-start.1 = (bf16[256,1536]{1,0:T(8,128)(2,1)}, bf16[256,1536]{1,0:T(8,128)(2,1)S(1)}, u32[]{:S(2)}, u32[]{:S(2)}) collective-permute-start(bf16[256,1536]{1,0:T(8,128)(2,1)} %bitcast.11), channel_id=1, source_target_pairs={{0,576},{192,0},{384,192},{576,384},{1,577},{193,1},{385,193},{577... | collective-permute-start | bytes 2359304 | tf_op jit(solution)/shard_map/ppermute | solution.py:25
  7.1 0.7 copy-done.12
  7.8 0.1 copy.7
  7.9 0.6 copy-done.13
  8.5 0.6 broadcast_in_dim.4.irreps
  9.1 0.7 pad_add_fusion.place
  9.7 0.6 pad.4.rows
  10.3 1.6 %mask.1 = bf16[32,16,128]{2,1,0:T(8,128)(2,1)} custom-call(s32[4]{0:T(128)} %pad_add_fusion.place, s32[1,1536]{1,0:T(1,128)} %broadcast_in_dim.4.irreps, bf16[64,128]{1,0:T(8,128)(2,1)} %pad.4.rows), custom_call_target="tpu_custom_call" | custom-call | flops 100000 | bytes 150000 | tf_op jit(solution)/shard_map/mask/pallas_call | solution.py:167
  11.9 17.3 %all_to_all.15.pieces = bf16[32,16,128]{2,1,0:T(8,128)(2,1)} all-to-all(bf16[32,16,128]{2,1,0:T(8,128)(2,1)} %mask.1), channel_id=1, replica_groups=mesh['x'=4,'zl'=4,'c'=2,'zh'=3,'y'=8] {'x','zl','c'}, dimensions={0} | all-to-all | bytes 262144 | tf_op jit(solution)/shard_map/all_to_all | solution.py:175
  29.3 0.0 collective-permute-done.t1
  29.3 0.0 collective-permute-done.1.t3
  29.3 1.9 %gather.1 = bf16[24,16,768]{2,1,0:T(8,128)(2,1)} custom-call(s32[4]{0:T(128)} %pad_add_fusion.place, bf16[32,16,128]{2,1,0:T(8,128)(2,1)} %all_to_all.15.pieces), custom_call_target="tpu_custom_call" | custom-call | flops 100000 | bytes 700000 | tf_op jit(solution)/shard_map/gather/pallas_call | solution.py:177
  31.1 13.3 %all-to-all-start.1 = ((bf16[24,16,768]{2,1,0:T(8,128)(2,1)}), bf16[24,16,768]{2,1,0:T(8,128)(2,1)S(1)}, u32[]{:S(2)}, u32[]{:S(2)}) async-start(bf16[24,16,768]{2,1,0:T(8,128)(2,1)} %gather.1), calls=%async_computation.1 | async-start | bytes 1179648 | tf_op jit(solution)/shard_map/all_to_all | solution.py:187
  44.5 0.0 copy-start
  44.5 4.3 %collective-permute-start.2 = (bf16[128,1536]{1,0:T(8,128)(2,1)S(1)}, bf16[128,1536]{1,0:T(8,128)(2,1)S(1)}, u32[]{:S(2)}, u32[]{:S(2)}) collective-permute-start(bf16[128,1536]{1,0:T(8,128)(2,1)S(1)} %slice.6), channel_id=1, source_target_pairs={{0,192},{192,384},{384,576},{576,0},{1,193},{193,385},{385,577},{5... | collective-permute-start | bytes 1179656 | tf_op jit(solution)/shard_map/ppermute | solution.py:25
  48.9 2.9 %collective-permute-start.3 = (bf16[128,1536]{1,0:T(8,128)(2,1)S(1)}, bf16[128,1536]{1,0:T(8,128)(2,1)S(1)}, u32[]{:S(2)}, u32[]{:S(2)}) collective-permute-start(bf16[128,1536]{1,0:T(8,128)(2,1)S(1)} %slice.7), channel_id=1, source_target_pairs={{0,576},{192,0},{384,192},{576,384},{1,577},{193,1},{385,193},{577... | collective-permute-start | bytes 1179656 | tf_op jit(solution)/shard_map/ppermute | solution.py:25
  51.8 6.9 %collective-permute-done.2.t2a = bf16[128,1536]{1,0:T(8,128)(2,1)S(1)} collective-permute-done((bf16[128,1536]{1,0:T(8,128)(2,1)S(1)}, bf16[128,1536]{1,0:T(8,128)(2,1)S(1)}, u32[]{:S(2)}, u32[]{:S(2)}) %collective-permute-start.2) | collective-permute-done | bytes 393248 | tf_op jit(solution)/shard_map/ppermute | solution.py:25
  58.7 0.8 copy-done.2
  59.5 1.5 %collective-permute-done.3.t2b = bf16[128,1536]{1,0:T(8,128)(2,1)S(1)} collective-permute-done((bf16[128,1536]{1,0:T(8,128)(2,1)S(1)}, bf16[128,1536]{1,0:T(8,128)(2,1)S(1)}, u32[]{:S(2)}, u32[]{:S(2)}) %collective-permute-start.3) | collective-permute-done | bytes 393248 | tf_op jit(solution)/shard_map/ppermute | solution.py:25
  61.0 0.7 copy-done.4
  61.7 10.2 %all-to-all-done.1 = bf16[24,16,768]{2,1,0:T(8,128)(2,1)S(1)} async-done(((bf16[24,16,768]{2,1,0:T(8,128)(2,1)}), bf16[24,16,768]{2,1,0:T(8,128)(2,1)S(1)}, u32[]{:S(2)}, u32[]{:S(2)}) %all-to-all-start.1) | async-done | bytes 589856 | tf_op jit(solution)/shard_map/all_to_all | solution.py:187
  71.9 1.9 %collective-permute-start.4 = (bf16[384,768]{1,0:T(8,128)(2,1)S(1)}, bf16[384,768]{1,0:T(8,128)(2,1)S(1)}, u32[]{:S(2)}, u32[]{:S(2)}) collective-permute-start(bf16[384,768]{1,0:T(8,128)(2,1)S(1)} %bitcast.14), channel_id=1, source_target_pairs={{0,24},{24,0},{1,25},{25,1},{2,26},{26,2},{3,27},{27,3},{4,28},{28... | collective-permute-start | bytes 1769480 | tf_op jit(solution)/shard_map/ppermute | solution.py:25
  73.9 2.0 %collective-permute-done.4.theirs = bf16[384,768]{1,0:T(8,128)(2,1)S(1)} collective-permute-done((bf16[384,768]{1,0:T(8,128)(2,1)S(1)}, bf16[384,768]{1,0:T(8,128)(2,1)S(1)}, u32[]{:S(2)}, u32[]{:S(2)}) %collective-permute-start.4) | collective-permute-done | bytes 589856 | tf_op jit(solution)/shard_map/ppermute | solution.py:25
  75.8 1.0 copy-done.3
  76.8 1.0 copy-done.5
  77.8 6.0 %cycle.1 = (bf16[24,64,256]{2,1,0:T(8,128)(2,1)}, bf16[24,16,256]{2,1,0:T(8,128)(2,1)S(1)}, bf16[24,16,256]{2,1,0:T(8,128)(2,1)S(1)}, bf16[24,16,256]{2,1,0:T(8,128)(2,1)S(1)}, bf16[24,16,256]{2,1,0:T(8,128)(2,1)S(1)}) custom-call(s32[4]{0:T(128)S(1)} %copy-done.1, bf16[384,768]{1,0:T(8,128)(2,1)S(1)} %bitcast.15, ...), custom_call_target="tpu_custom_call" | custom-call | flops 1210000000 | bytes 6000000 | tf_op jit(solution)/shard_map/cycle/pallas_call | solution.py:193
  83.8 0.0 copy-start.6
  83.9 0.7 copy-done.6
  84.5 0.7 copy-done.8
  85.2 0.7 copy-done.10
  85.9 10.8 %all-to-all-start.2 = ((bf16[96,16,256]{2,1,0:T(8,128)(2,1)}), bf16[96,16,256]{2,1,0:T(8,128)(2,1)S(1)}, u32[]{:S(2)}, u32[]{:S(2)}) async-start(bf16[96,16,256]{2,1,0:T(8,128)(2,1)} %bitcast.6), calls=%async_computation.2 | async-start | bytes 1572864 | tf_op jit(solution)/shard_map/all_to_all | solution.py:209
  96.7 0.0 copy-start.14
  96.7 0.7 copy-done.14
  97.4 0.1 dynamic_slice.11
  97.5 0.1 fusion
  97.5 0.1 broadcast_add_fusion
  97.6 4.5 %collective-permute-start.5 = (bf16[24,16,256]{2,1,0:T(8,128)(2,1)S(1)}, bf16[24,16,256]{2,1,0:T(8,128)(2,1)S(1)}, u32[]{:S(2)}, u32[]{:S(2)}) collective-permute-start(bf16[24,16,256]{2,1,0:T(8,128)(2,1)S(1)} %copy-done.11), channel_id=1, source_target_pairs={{0,576},{192,0},{384,192},{576,384},{1,577},{193,1},{385,193},{577... | collective-permute-start | bytes 589832 | tf_op jit(solution)/shard_map/ppermute | solution.py:25
  102.1 2.8 %collective-permute-start.6 = (bf16[24,16,256]{2,1,0:T(8,128)(2,1)S(1)}, bf16[24,16,256]{2,1,0:T(8,128)(2,1)S(1)}, u32[]{:S(2)}, u32[]{:S(2)}) collective-permute-start(bf16[24,16,256]{2,1,0:T(8,128)(2,1)S(1)} %copy-done.9), channel_id=1, source_target_pairs={{0,384},{192,576},{384,0},{576,192},{1,385},{193,577},{385,1},{577... | collective-permute-start | bytes 589832 | tf_op jit(solution)/shard_map/ppermute | solution.py:25
  104.9 0.0 copy-done.7
  104.9 2.8 %collective-permute-start.7 = (bf16[24,16,256]{2,1,0:T(8,128)(2,1)S(1)}, bf16[24,16,256]{2,1,0:T(8,128)(2,1)S(1)}, u32[]{:S(2)}, u32[]{:S(2)}) collective-permute-start(bf16[24,16,256]{2,1,0:T(8,128)(2,1)S(1)} %copy-done.7), channel_id=1, source_target_pairs={{0,192},{192,384},{384,576},{576,0},{1,193},{193,385},{385,577},{5... | collective-permute-start | bytes 589832 | tf_op jit(solution)/shard_map/ppermute | solution.py:25
  107.6 0.1 broadcast_subtract_fusion
  107.7 0.1 sub.27.row_term
  107.9 3.3 %collective-permute-done.5.own1 = bf16[24,16,256]{2,1,0:T(8,128)(2,1)S(1)} collective-permute-done((bf16[24,16,256]{2,1,0:T(8,128)(2,1)S(1)}, bf16[24,16,256]{2,1,0:T(8,128)(2,1)S(1)}, u32[]{:S(2)}, u32[]{:S(2)}) %collective-permute-start.5) | collective-permute-done | bytes 196640 | tf_op jit(solution)/shard_map/ppermute | solution.py:25
  111.2 2.5 %collective-permute-done.6.own2 = bf16[24,16,256]{2,1,0:T(8,128)(2,1)S(1)} collective-permute-done((bf16[24,16,256]{2,1,0:T(8,128)(2,1)S(1)}, bf16[24,16,256]{2,1,0:T(8,128)(2,1)S(1)}, u32[]{:S(2)}, u32[]{:S(2)}) %collective-permute-start.6) | collective-permute-done | bytes 196640 | tf_op jit(solution)/shard_map/ppermute | solution.py:25
  113.7 2.7 %collective-permute-done.7.own3 = bf16[24,16,256]{2,1,0:T(8,128)(2,1)S(1)} collective-permute-done((bf16[24,16,256]{2,1,0:T(8,128)(2,1)S(1)}, bf16[24,16,256]{2,1,0:T(8,128)(2,1)S(1)}, u32[]{:S(2)}, u32[]{:S(2)}) %collective-permute-start.7) | collective-permute-done | bytes 196640 | tf_op jit(solution)/shard_map/ppermute | solution.py:25
  116.4 15.2 %all-to-all-done.2 = bf16[96,16,256]{2,1,0:T(8,128)(2,1)S(1)} async-done(((bf16[96,16,256]{2,1,0:T(8,128)(2,1)}), bf16[96,16,256]{2,1,0:T(8,128)(2,1)S(1)}, u32[]{:S(2)}, u32[]{:S(2)}) %all-to-all-start.2) | async-done | bytes 786464 | tf_op jit(solution)/shard_map/all_to_all | solution.py:209
  131.6 2.5 %finish.1 = bf16[256,1536]{1,0:T(8,128)(2,1)} custom-call(s32[4]{0:T(128)S(1)} %copy-done.1, bf16[24,64,256]{2,1,0:T(8,128)(2,1)S(1)} %bitcast.9, bf16[24,16,256]{2,1,0:T(8,128)(2,1)S(1)} %get-tuple-element.23.own0, bf16[24,16,256]{2,1,0:T(8,128)(2,1)S(1)} %collective-permute-done.5.own1, bf16[24,16,256]{2,1,0:T(8,128)(2,1)S(1)} %collective-permute-done.6.own2, ...), custom_call_target="tpu_custom_call" | custom-call | flops 600000000 | bytes 4000000 | tf_op jit(solution)/shard_map/finish/pallas_call | solution.py:221
  (21 shorter events, 0.1 us)
Async XLA Ops:
  0.0 29.3 %collective-permute-start = (bf16[256,1536]{1,0:T(8,128)(2,1)}, bf16[256,1536]{1,0:T(8,128)(2,1)S(1)}, u32[]{:S(2)}, u32[]{:S(2)}) collective-permute-start(bf16[256,1536]{1,0:T(8,128)(2,1)} %bitcast.10), channel_id=1, source_target_pairs={{0,192},{192,384},{384,576},{576,0},{1,193},{193,385},{385,577},{5... | collective-permute-start | bytes 2359304 | tf_op jit(solution)/shard_map/ppermute | solution.py:25
  3.4 25.9 %collective-permute-start.1 = (bf16[256,1536]{1,0:T(8,128)(2,1)}, bf16[256,1536]{1,0:T(8,128)(2,1)S(1)}, u32[]{:S(2)}, u32[]{:S(2)}) collective-permute-start(bf16[256,1536]{1,0:T(8,128)(2,1)} %bitcast.11), channel_id=1, source_target_pairs={{0,576},{192,0},{384,192},{576,384},{1,577},{193,1},{385,193},{577... | collective-permute-start | bytes 2359304 | tf_op jit(solution)/shard_map/ppermute | solution.py:25
  7.1 0.7 copy-start.12
  7.8 0.7 copy-start.13
  31.1 40.8 %all-to-all-start.1 = ((bf16[24,16,768]{2,1,0:T(8,128)(2,1)}), bf16[24,16,768]{2,1,0:T(8,128)(2,1)S(1)}, u32[]{:S(2)}, u32[]{:S(2)}) async-start(bf16[24,16,768]{2,1,0:T(8,128)(2,1)} %gather.1), calls=%async_computation.1 | async-start | bytes 1179648 | tf_op jit(solution)/shard_map/all_to_all | solution.py:187
  44.5 31.3 %copy-start = (bf16[1,2,2,64,1536]{4,3,2,1,0:T(8,128)(2,1)S(1)}, bf16[1,2,2,64,1536]{4,3,2,1,0:T(8,128)(2,1)}, u32[]{:S(2)}) copy-start(bf16[1,2,2,64,1536]{4,3,2,1,0:T(8,128)(2,1)} %param.5) | copy-start | bytes 2359300
  44.5 14.2 %collective-permute-start.2 = (bf16[128,1536]{1,0:T(8,128)(2,1)S(1)}, bf16[128,1536]{1,0:T(8,128)(2,1)S(1)}, u32[]{:S(2)}, u32[]{:S(2)}) collective-permute-start(bf16[128,1536]{1,0:T(8,128)(2,1)S(1)} %slice.6), channel_id=1, source_target_pairs={{0,192},{192,384},{384,576},{576,0},{1,193},{193,385},{385,577},{5... | collective-permute-start | bytes 1179656 | tf_op jit(solution)/shard_map/ppermute | solution.py:25
  48.9 27.0 %copy-start.1 = (s32[4]{0:T(128)S(1)}, s32[4]{0:T(128)}, u32[]{:S(2)}) copy-start(s32[4]{0:T(128)} %pad_add_fusion.place) | copy-start | bytes 52
  48.9 12.1 %collective-permute-start.3 = (bf16[128,1536]{1,0:T(8,128)(2,1)S(1)}, bf16[128,1536]{1,0:T(8,128)(2,1)S(1)}, u32[]{:S(2)}, u32[]{:S(2)}) collective-permute-start(bf16[128,1536]{1,0:T(8,128)(2,1)S(1)} %slice.7), channel_id=1, source_target_pairs={{0,576},{192,0},{384,192},{576,384},{1,577},{193,1},{385,193},{577... | collective-permute-start | bytes 1179656 | tf_op jit(solution)/shard_map/ppermute | solution.py:25
  58.7 0.8 copy-start.2
  61.0 0.8 copy-start.4
  71.9 3.9 %collective-permute-start.4 = (bf16[384,768]{1,0:T(8,128)(2,1)S(1)}, bf16[384,768]{1,0:T(8,128)(2,1)S(1)}, u32[]{:S(2)}, u32[]{:S(2)}) collective-permute-start(bf16[384,768]{1,0:T(8,128)(2,1)S(1)} %bitcast.14), channel_id=1, source_target_pairs={{0,24},{24,0},{1,25},{25,1},{2,26},{26,2},{3,27},{27,3},{4,28},{28... | collective-permute-start | bytes 1769480 | tf_op jit(solution)/shard_map/ppermute | solution.py:25
  75.8 1.0 copy-start.3
  76.8 1.0 copy-start.5
  83.8 0.7 copy-start.6
  84.5 0.7 copy-start.8
  85.2 0.7 copy-start.10
  85.9 11.6 %copy-start.15 = (f32[64]{0:T(128)S(1)}, f32[64]{0:T(128)}, u32[]{:S(2)}) copy-start(f32[64]{0:T(128)} %param.8) | copy-start | bytes 772
  85.9 11.7 %copy-start.11 = (bf16[24,16,256]{2,1,0:T(8,128)(2,1)S(1)}, bf16[24,16,256]{2,1,0:T(8,128)(2,1)}, u32[]{:S(2)}) copy-start(bf16[24,16,256]{2,1,0:T(8,128)(2,1)} %copy-done.10) | copy-start | bytes 589828
  85.9 16.2 %copy-start.9 = (bf16[24,16,256]{2,1,0:T(8,128)(2,1)S(1)}, bf16[24,16,256]{2,1,0:T(8,128)(2,1)}, u32[]{:S(2)}) copy-start(bf16[24,16,256]{2,1,0:T(8,128)(2,1)} %copy-done.8) | copy-start | bytes 589828
  85.9 19.0 %copy-start.7 = (bf16[24,16,256]{2,1,0:T(8,128)(2,1)S(1)}, bf16[24,16,256]{2,1,0:T(8,128)(2,1)}, u32[]{:S(2)}) copy-start(bf16[24,16,256]{2,1,0:T(8,128)(2,1)} %copy-done.6) | copy-start | bytes 589828
  85.9 45.7 %all-to-all-start.2 = ((bf16[96,16,256]{2,1,0:T(8,128)(2,1)}), bf16[96,16,256]{2,1,0:T(8,128)(2,1)S(1)}, u32[]{:S(2)}, u32[]{:S(2)}) async-start(bf16[96,16,256]{2,1,0:T(8,128)(2,1)} %bitcast.6), calls=%async_computation.2 | async-start | bytes 1572864 | tf_op jit(solution)/shard_map/all_to_all | solution.py:209
  96.7 0.7 copy-start.14
  97.6 13.6 %collective-permute-start.5 = (bf16[24,16,256]{2,1,0:T(8,128)(2,1)S(1)}, bf16[24,16,256]{2,1,0:T(8,128)(2,1)S(1)}, u32[]{:S(2)}, u32[]{:S(2)}) collective-permute-start(bf16[24,16,256]{2,1,0:T(8,128)(2,1)S(1)} %copy-done.11), channel_id=1, source_target_pairs={{0,576},{192,0},{384,192},{576,384},{1,577},{193,1},{385,193},{577... | collective-permute-start | bytes 589832 | tf_op jit(solution)/shard_map/ppermute | solution.py:25
  102.1 11.6 %collective-permute-start.6 = (bf16[24,16,256]{2,1,0:T(8,128)(2,1)S(1)}, bf16[24,16,256]{2,1,0:T(8,128)(2,1)S(1)}, u32[]{:S(2)}, u32[]{:S(2)}) collective-permute-start(bf16[24,16,256]{2,1,0:T(8,128)(2,1)S(1)} %copy-done.9), channel_id=1, source_target_pairs={{0,384},{192,576},{384,0},{576,192},{1,385},{193,577},{385,1},{577... | collective-permute-start | bytes 589832 | tf_op jit(solution)/shard_map/ppermute | solution.py:25
  104.9 11.5 %collective-permute-start.7 = (bf16[24,16,256]{2,1,0:T(8,128)(2,1)S(1)}, bf16[24,16,256]{2,1,0:T(8,128)(2,1)S(1)}, u32[]{:S(2)}, u32[]{:S(2)}) collective-permute-start(bf16[24,16,256]{2,1,0:T(8,128)(2,1)S(1)} %copy-done.7), channel_id=1, source_target_pairs={{0,192},{192,384},{384,576},{576,0},{1,193},{193,385},{385,577},{5... | collective-permute-start | bytes 589832 | tf_op jit(solution)/shard_map/ppermute | solution.py:25

commit v5 on v3

--- a/solution.py
+++ b/solution.py
@@ -22,29 +22,54 @@
     return lax.ppermute(value, axis, pairs)
 
 
-def cycle_kernel(place, mine, theirs, t0, t1, t2a, t2b, t3, mirror, own0, own1, own2, own3):
+def unit_matrix(size):
+    rows = lax.broadcasted_iota(jnp.int32, (size, size), 0)
+    return (rows == lax.broadcasted_iota(jnp.int32, (size, size), 1)).astype(BF16)
+
+
+def spread(value, axis, count):
+    copies = jnp.broadcast_to(value[None], (count,) + value.shape)
+    return lax.all_to_all(copies, axis, split_axis=0, concat_axis=0, tiled=True)
+
+
+def turn_kernel(labels_c, labels_a, pieces, out):
+    depth = pieces.shape[2]
+    quarter = pieces.shape[1] // X
+    unit = unit_matrix(depth)
+    for share in range(X):
+        rows = pieces[:, share * quarter : (share + 1) * quarter, :].reshape(NVIRT * quarter, depth)
+        turned = lax.dot_general(unit, rows, NT, preferred_element_type=F32)
+        keep = labels_c[...] == labels_a[share : share + 1, :]
+        masked = jnp.where(keep, turned, 0.0).astype(BF16)
+        for copy in range(ZL):
+            out[share * ZL + copy] = masked
+
+
+def cycle_kernel(
+    place, mine, theirs, t0, t1, t2a, t2b, t2c, t2d, t3, mirror, own0, own1, own2, own3, turned, held, t2
+):
     x, c = place[0], place[1]
-    half = mine.shape[1]
     quarter = mirror.shape[1] // X
-    here = pl.ds(pl.multiple_of(c * half, 128), half)
-    there = pl.ds(pl.multiple_of((1 - c) * half, 128), half)
-
-    def product(t):
-        total = lax.dot_general(mine[...], t[:, here], NT, preferred_element_type=F32)
-        total += lax.dot_general(theirs[...], t[:, there], NT, preferred_element_type=F32)
-        return total.astype(BF16)
-
-    for steps, parts, own in ((0, (t0,), own0), (1, (t1,), own1), (2, (t2a, t2b), own2), (3, (t3,), own3)):
+    count, depth, size = mine.shape
+    for number in range(count):
+        here = pl.multiple_of((2 * number + c) * depth, 16)
+        there = pl.multiple_of((2 * number + 1 - c) * depth, 16)
+        turned[pl.ds(here, depth), :] = mine[number]
+        turned[pl.ds(there, depth), :] = theirs[number]
+    unit = unit_matrix(size)
+    for first in range(0, turned.shape[0], size):
+        part = lax.dot_general(unit, turned[first : first + size, :], NT, preferred_element_type=F32)
+        held[:, first : first + size] = part.astype(BF16)
+    rows = t2a.shape[0]
+    for number, part in enumerate((t2a, t2b, t2c, t2d)):
+        t2[number * rows : (number + 1) * rows, :] = part[...]
+    for steps, (t, own) in enumerate(((t0, own0), (t1, own1), (t2, own2), (t3, own3))):
         slot = lax.rem(x + (X + X // 2 - steps), X)
-        first = 0
-        for part in parts:
-            value = product(part)
-            lanes = slice(first, first + part.shape[0])
-            mirror[:, pl.ds(pl.multiple_of(slot * quarter, quarter), quarter), lanes] = value.reshape(
-                NVIRT, quarter, part.shape[0]
-            )
-            own[:, lanes] = value
-            first += part.shape[0]
+        value = lax.dot_general(held[...], t[...], NT, preferred_element_type=F32).astype(BF16)
+        mirror[:, pl.ds(pl.multiple_of(slot * quarter, quarter), quarter), :] = value.reshape(
+            NVIRT, quarter, value.shape[1]
+        )
+        own[...] = value
 
 
 def finish_kernel(place, arrived, own0, own1, own2, own3, t, row_term, virt, out, own_rows):
@@ -106,35 +131,43 @@
     t1 = passed_along(flat, "x", 1)
     t3 = passed_along(flat, "x", 3)
 
-    irreps_a = lax.dynamic_slice_in_dim(irreps, place * width, width)
-    irreps_c = lax.dynamic_slice_in_dim(irreps, index * depth, depth)
-    keep = irreps_a[:, None] == irreps_c[None, :]
-    masked = jnp.where(keep, integrals, jnp.zeros_like(integrals))
-    sent = jnp.broadcast_to(
-        masked.reshape(X, 1, quarter, depth), (X, ZL * C, quarter, depth)
-    ).reshape(npair, quarter, depth)
-    rows = lax.all_to_all(sent, PAIR, split_axis=0, concat_axis=0, tiled=True)
-    rows = jnp.transpose(rows, (1, 0, 2)).reshape(quarter, virt_total)
-    rows = lax.dynamic_slice_in_dim(rows, lax.axis_index("c") * (virt_total // 2), virt_total // 2, axis=1)
-    rows, t1, t3 = lax.optimization_barrier((rows, t1, t3))
-    t2a = passed_along(t1[: lanes // 2], "x", 1)
-    t2b = passed_along(t3[lanes // 2 :], "x", 3)
-    copies = jnp.broadcast_to(rows[None], (NVIRT,) + rows.shape)
-    mine = lax.all_to_all(copies, VIRT, split_axis=0, concat_axis=0, tiled=True)
-    mine, t2a, t2b = lax.optimization_barrier((mine, t2a, t2b))
-    mine = mine.reshape(NVIRT * quarter, virt_total // 2)
+    pieces = spread(integrals, VIRT, NVIRT)
+    labels_c = lax.dynamic_slice_in_dim(irreps, index * depth, depth)[:, None]
+    labels_a = jnp.transpose(irreps.reshape(NVIRT, X, quarter), (1, 0, 2)).reshape(X, NVIRT * quarter)
+    part = lanes // 4
+    t2a = passed_along(t1[:part], "x", 1)
+    t2d = passed_along(t3[3 * part :], "x", 3)
+    pieces, t1, t3, t2a, t2d = lax.optimization_barrier((pieces, t1, t3, t2a, t2d))
+    t2b = passed_along(t1[part : 2 * part], "x", 1)
+    t2c = passed_along(t3[2 * part : 3 * part], "x", 3)
+    sent = pl.pallas_call(
+        turn_kernel,
+        out_shape=jax.ShapeDtypeStruct((X * ZL, depth, NVIRT * quarter), BF16),
+        in_specs=[VMEM] * 3,
+        out_specs=VMEM,
+        cost_estimate=pl.CostEstimate(flops=10_000_000, bytes_accessed=1_000_000, transcendentals=0),
+        compiler_params=pltpu.CompilerParams(vmem_limit_bytes=12 * 2**20),
+        name="turn",
+    )(labels_c, labels_a, pieces)
+    mine = lax.all_to_all(sent, ("x", "zl"), split_axis=0, concat_axis=0, tiled=True)
+    mine, t2b, t2c = lax.optimization_barrier((mine, t2b, t2c))
     theirs = passed_along(mine, "c", 1)
 
     share = jax.ShapeDtypeStruct((NVIRT * quarter, lanes), BF16)
     mirror, own0, own1, own2, own3 = pl.pallas_call(
         cycle_kernel,
         out_shape=[jax.ShapeDtypeStruct((NVIRT, width, lanes), BF16)] + [share] * X,
-        in_specs=[SMEM] + [VMEM] * 7,
+        in_specs=[SMEM] + [VMEM] * 9,
         out_specs=[VMEM] * 5,
+        scratch_shapes=[
+            pltpu.VMEM((virt_total, NVIRT * quarter), BF16),
+            pltpu.VMEM((NVIRT * quarter, virt_total), BF16),
+            pltpu.VMEM(flat.shape, BF16),
+        ],
         cost_estimate=pl.CostEstimate(flops=1_210_000_000, bytes_accessed=6_000_000, transcendentals=0),
-        compiler_params=pltpu.CompilerParams(vmem_limit_bytes=12 * 2**20),
+        compiler_params=pltpu.CompilerParams(vmem_limit_bytes=56 * 2**20),
         name="cycle",
-    )(spot, mine, theirs, flat, t1, t2a, t2b, t3)
+    )(spot, mine, theirs, flat, t1, t2a, t2b, t2c, t2d, t3)
 
     arrived = lax.all_to_all(
         mirror.reshape(NVIRT * X, quarter, lanes), VIRT + ("x",), split_axis=0, concat_axis=0, tiled=True

time: 130 us -> 128 us (0.985)
  the two profiles are of different devices: /device:TPU:192 before, /device:TPU:1 now
where the time goes in v5:
time: 128 us
  starting transfers between devices  73.1 us (57%)
  waiting for transfers between devices  39.5 us (31%)
  Pallas kernels  9.14 us (7%)
  local copies, waits for them, and re-layouts  4.71 us (4%)
    ppermute x10, starting transfers between devices, passed_along(): return lax.ppermute(value, axis, pairs)  33.3 us
    all_to_all x1, starting transfers between devices, spread(): return lax.all_to_all(copies, axis, split_axis=0, concat_axis=0, tiled=True)  19.3 us
    ppermute x10, waiting for transfers between devices, passed_along(): return lax.ppermute(value, axis, pairs)  17.8 us
    all_to_all x1, starting transfers between devices, local(): lax.all_to_all(mirror.reshape(NVIRT * X, quarter, lanes), VIRT + ('x',),...  13.4 us
    all_to_all x1, waiting for transfers between devices, local(): lax.all_to_all(mirror.reshape(NVIRT * X, quarter, lanes), VIRT + ('x',),...  12.7 us
    all_to_all x1, starting transfers between devices, local(): lax.all_to_all(sent, ('x', 'zl'), split_axis=0, concat_axis=0, tiled=True)  6.95 us
    pallas_call x1, Pallas kernels, local(): pl.pallas_call(cycle_kernel, out_shape=[jax.ShapeDtypeStruct((NVIRT, widt...  5.54 us
    all_to_all x1, waiting for transfers between devices, local(): lax.all_to_all(sent, ('x', 'zl'), split_axis=0, concat_axis=0, tiled=True)  4.85 us
  transfers between devices with their start and end apart: 13, of which 9 were waited for; matrix products, arithmetic and copies ran while one was open for 2% of the time, Pallas kernels for 0%

profile of v5, /device:TPU:1, one launch (start us, length us, event | category | flops | bytes accessed | tf_op | source)
XLA Modules:
  0.0 127.5 jit_solution(18001487417947316507)
XLA Ops:
  0.0 4.1 %collective-permute-start = (bf16[256,1536]{1,0:T(8,128)(2,1)}, bf16[256,1536]{1,0:T(8,128)(2,1)S(1)}, u32[]{:S(2)}, u32[]{:S(2)}) collective-permute-start(bf16[256,1536]{1,0:T(8,128)(2,1)} %bitcast.13), channel_id=1, source_target_pairs={{0,192},{192,384},{384,576},{576,0},{1,193},{193,385},{385,577},{5... | collective-permute-start | bytes 2359304 | tf_op jit(solution)/shard_map/ppermute | solution.py:22
  4.1 3.2 %collective-permute-start.1 = (bf16[256,1536]{1,0:T(8,128)(2,1)}, bf16[256,1536]{1,0:T(8,128)(2,1)S(1)}, u32[]{:S(2)}, u32[]{:S(2)}) collective-permute-start(bf16[256,1536]{1,0:T(8,128)(2,1)} %bitcast.14), channel_id=1, source_target_pairs={{0,576},{192,0},{384,192},{576,384},{1,577},{193,1},{385,193},{577... | collective-permute-start | bytes 2359304 | tf_op jit(solution)/shard_map/ppermute | solution.py:22
  7.3 0.9 reshape.81
  8.2 19.3 %all-to-all-start = ((bf16[24,2,1536]{2,1,0:T(2,128)(2,1)}), bf16[24,2,1536]{2,1,0:T(2,128)(2,1)S(1)}, u32[]{:S(2)}, u32[]{:S(2)}) async-start(bf16[24,2,1536]{2,1,0:T(2,128)(2,1)} %reshape.81), calls=%async_computation | async-start | bytes 294912 | tf_op jit(solution)/shard_map/all_to_all | solution.py:32
  27.6 0.0 collective-permute-done.t1
  27.6 0.0 copy-start.5
  27.6 1.9 %collective-permute-start.2 = (bf16[64,1536]{1,0:T(8,128)(2,1)S(1)}, bf16[64,1536]{1,0:T(8,128)(2,1)S(1)}, u32[]{:S(2)}, u32[]{:S(2)}) collective-permute-start(bf16[64,1536]{1,0:T(8,128)(2,1)S(1)} %slice.16), channel_id=1, source_target_pairs={{0,192},{192,384},{384,576},{576,0},{1,193},{193,385},{385,577},{5... | collective-permute-start | bytes 589832 | tf_op jit(solution)/shard_map/ppermute | solution.py:22
  29.5 0.0 collective-permute-done.1.t3
  29.6 4.6 %collective-permute-start.3 = (bf16[64,1536]{1,0:T(8,128)(2,1)S(1)}, bf16[64,1536]{1,0:T(8,128)(2,1)S(1)}, u32[]{:S(2)}, u32[]{:S(2)}) collective-permute-start(bf16[64,1536]{1,0:T(8,128)(2,1)S(1)} %slice.17), channel_id=1, source_target_pairs={{0,576},{192,0},{384,192},{576,384},{1,577},{193,1},{385,193},{577... | collective-permute-start | bytes 589832 | tf_op jit(solution)/shard_map/ppermute | solution.py:22
  34.2 0.0 copy-start.7
  34.2 0.7 copy-done.7
  34.9 0.1 reshape.75
  35.0 0.1 dynamic-slice_bitcast_fusion
  35.1 0.1 copy.13.labels_c
  35.2 0.1 reshape.76.labels_a
  35.2 4.1 %all-to-all-done = bf16[24,2,1536]{2,1,0:T(2,128)(2,1)S(1)} async-done(((bf16[24,2,1536]{2,1,0:T(2,128)(2,1)}), bf16[24,2,1536]{2,1,0:T(2,128)(2,1)S(1)}, u32[]{:S(2)}, u32[]{:S(2)}) %all-to-all-start) | async-done | bytes 147488 | tf_op jit(solution)/shard_map/all_to_all | solution.py:32
  39.3 0.2 reshape.82
  39.6 0.2 copy.14.pieces
  39.8 0.4 copy-done.13
  40.2 0.1 copy-done.15
  40.3 1.1 turn.1
  41.4 7.0 %all-to-all-start.1 = ((bf16[16,48,384]{2,1,0:T(8,128)(2,1)}), bf16[16,48,384]{2,1,0:T(8,128)(2,1)S(1)}, u32[]{:S(2)}, u32[]{:S(2)}) async-start(bf16[16,48,384]{2,1,0:T(8,128)(2,1)} %turn.1), calls=%async_computation.1 | async-start | bytes 1179648 | tf_op jit(solution)/shard_map/all_to_all | solution.py:152
  48.4 3.3 %collective-permute-start.4 = (bf16[64,1536]{1,0:T(8,128)(2,1)S(1)}, bf16[64,1536]{1,0:T(8,128)(2,1)S(1)}, u32[]{:S(2)}, u32[]{:S(2)}) collective-permute-start(bf16[64,1536]{1,0:T(8,128)(2,1)S(1)} %slice.14), channel_id=1, source_target_pairs={{0,192},{192,384},{384,576},{576,0},{1,193},{193,385},{385,577},{5... | collective-permute-start | bytes 589832 | tf_op jit(solution)/shard_map/ppermute | solution.py:22
  51.7 3.2 %collective-permute-start.5 = (bf16[64,1536]{1,0:T(8,128)(2,1)S(1)}, bf16[64,1536]{1,0:T(8,128)(2,1)S(1)}, u32[]{:S(2)}, u32[]{:S(2)}) collective-permute-start(bf16[64,1536]{1,0:T(8,128)(2,1)S(1)} %slice.15), channel_id=1, source_target_pairs={{0,576},{192,0},{384,192},{576,384},{1,577},{193,1},{385,193},{577... | collective-permute-start | bytes 589832 | tf_op jit(solution)/shard_map/ppermute | solution.py:22
  55.0 4.9 %collective-permute-done.4.t2b = bf16[64,1536]{1,0:T(8,128)(2,1)S(1)} collective-permute-done((bf16[64,1536]{1,0:T(8,128)(2,1)S(1)}, bf16[64,1536]{1,0:T(8,128)(2,1)S(1)}, u32[]{:S(2)}, u32[]{:S(2)}) %collective-permute-start.4) | collective-permute-done | bytes 196640 | tf_op jit(solution)/shard_map/ppermute | solution.py:22
  59.9 0.2 collective-permute-done.5.t2c
  60.1 4.8 %all-to-all-done.1.mine = bf16[16,48,384]{2,1,0:T(8,128)(2,1)S(1)} async-done(((bf16[16,48,384]{2,1,0:T(8,128)(2,1)}), bf16[16,48,384]{2,1,0:T(8,128)(2,1)S(1)}, u32[]{:S(2)}, u32[]{:S(2)}) %all-to-all-start.1) | async-done | bytes 589856 | tf_op jit(solution)/shard_map/all_to_all | solution.py:152
  64.9 4.2 %collective-permute-start.6 = (bf16[16,48,384]{2,1,0:T(8,128)(2,1)S(1)}, bf16[16,48,384]{2,1,0:T(8,128)(2,1)S(1)}, u32[]{:S(2)}, u32[]{:S(2)}) collective-permute-start(bf16[16,48,384]{2,1,0:T(8,128)(2,1)S(1)} %all-to-all-done.1.mine), channel_id=1, source_target_pairs={{0,24},{24,0},{1,25},{25,1},{2,26},{26,2},{3,27},{27,3},{4,28},{28... | collective-permute-start | bytes 1769480 | tf_op jit(solution)/shard_map/ppermute | solution.py:22
  69.2 0.6 pad_add_fusion.place
  69.7 1.1 collective-permute-done.6.theirs
  70.8 0.8 copy-done.10
  71.6 5.5 %cycle.1 = (bf16[24,64,256]{2,1,0:T(8,128)(2,1)}, bf16[384,256]{1,0:T(8,128)(2,1)}, bf16[384,256]{1,0:T(8,128)(2,1)}, bf16[384,256]{1,0:T(8,128)(2,1)}, bf16[384,256]{1,0:T(8,128)(2,1)}) custom-call(s32[2]{0:T(128)} %pad_add_fusion.place, bf16[16,48,384]{2,1,0:T(8,128)(2,1)} %copy-done.4, bf16[16,48,384]{2,1,0:T(8,128)(2,1)} %copy-done.10, ...), custom_call_target="tpu_custom_call" | custom-call | flops 1210000000 | bytes 6000000 | tf_op jit(solution)/shard_map/cycle/pallas_call | solution.py:157
  77.2 0.0 copy-start.1
  77.2 13.4 %all-to-all-start.2 = ((bf16[96,16,256]{2,1,0:T(8,128)(2,1)}), bf16[96,16,256]{2,1,0:T(8,128)(2,1)S(1)}, u32[]{:S(2)}, u32[]{:S(2)}) async-start(bf16[96,16,256]{2,1,0:T(8,128)(2,1)} %bitcast.18), calls=%async_computation.2 | async-start | bytes 1572864 | tf_op jit(solution)/shard_map/all_to_all | solution.py:172
  90.7 0.1 dynamic_slice.15
  90.8 0.1 fusion
  90.9 0.1 broadcast_add_fusion
  90.9 3.9 %collective-permute-start.7 = (bf16[384,256]{1,0:T(8,128)(2,1)S(1)}, bf16[384,256]{1,0:T(8,128)(2,1)S(1)}, u32[]{:S(2)}, u32[]{:S(2)}) collective-permute-start(bf16[384,256]{1,0:T(8,128)(2,1)S(1)} %copy-done.14), channel_id=1, source_target_pairs={{0,576},{192,0},{384,192},{576,384},{1,577},{193,1},{385,193},{577... | collective-permute-start | bytes 589832 | tf_op jit(solution)/shard_map/ppermute | solution.py:22
  94.9 2.5 %collective-permute-start.8 = (bf16[384,256]{1,0:T(8,128)(2,1)S(1)}, bf16[384,256]{1,0:T(8,128)(2,1)S(1)}, u32[]{:S(2)}, u32[]{:S(2)}) collective-permute-start(bf16[384,256]{1,0:T(8,128)(2,1)S(1)} %copy-done.12), channel_id=1, source_target_pairs={{0,384},{192,576},{384,0},{576,192},{1,385},{193,577},{385,1},{577... | collective-permute-start | bytes 589832 | tf_op jit(solution)/shard_map/ppermute | solution.py:22
  97.4 2.5 %collective-permute-start.9 = (bf16[384,256]{1,0:T(8,128)(2,1)S(1)}, bf16[384,256]{1,0:T(8,128)(2,1)S(1)}, u32[]{:S(2)}, u32[]{:S(2)}) collective-permute-start(bf16[384,256]{1,0:T(8,128)(2,1)S(1)} %copy-done.11), channel_id=1, source_target_pairs={{0,192},{192,384},{384,576},{576,0},{1,193},{193,385},{385,577},{5... | collective-permute-start | bytes 589832 | tf_op jit(solution)/shard_map/ppermute | solution.py:22
  99.9 0.1 broadcast_subtract_fusion
  99.9 0.1 sub.27.row_term
  100.1 1.1 collective-permute-done.7.own1
  101.2 4.4 %collective-permute-done.8.own2 = bf16[384,256]{1,0:T(8,128)(2,1)S(1)} collective-permute-done((bf16[384,256]{1,0:T(8,128)(2,1)S(1)}, bf16[384,256]{1,0:T(8,128)(2,1)S(1)}, u32[]{:S(2)}, u32[]{:S(2)}) %collective-permute-start.8) | collective-permute-done | bytes 196640 | tf_op jit(solution)/shard_map/ppermute | solution.py:22
  105.6 6.2 %collective-permute-done.9.own3 = bf16[384,256]{1,0:T(8,128)(2,1)S(1)} collective-permute-done((bf16[384,256]{1,0:T(8,128)(2,1)S(1)}, bf16[384,256]{1,0:T(8,128)(2,1)S(1)}, u32[]{:S(2)}, u32[]{:S(2)}) %collective-permute-start.9) | collective-permute-done | bytes 196640 | tf_op jit(solution)/shard_map/ppermute | solution.py:22
  111.8 12.7 %all-to-all-done.2 = bf16[96,16,256]{2,1,0:T(8,128)(2,1)S(1)} async-done(((bf16[96,16,256]{2,1,0:T(8,128)(2,1)}), bf16[96,16,256]{2,1,0:T(8,128)(2,1)S(1)}, u32[]{:S(2)}, u32[]{:S(2)}) %all-to-all-start.2) | async-done | bytes 786464 | tf_op jit(solution)/shard_map/all_to_all | solution.py:172
  124.5 0.6 copy-done.3
  125.0 2.5 %finish.1 = bf16[256,1536]{1,0:T(8,128)(2,1)} custom-call(s32[2]{0:T(128)S(1)} %copy-done.3, bf16[24,64,256]{2,1,0:T(8,128)(2,1)S(1)} %bitcast.12, bf16[384,256]{1,0:T(8,128)(2,1)S(1)} %copy-done.2, bf16[384,256]{1,0:T(8,128)(2,1)S(1)} %collective-permute-done.7.own1, bf16[384,256]{1,0:T(8,128)(2,1)S(1)} %collective-permute-done.8.own2, ...), custom_call_target="tpu_custom_call" | custom-call | flops 600000000 | bytes 4000000 | tf_op jit(solution)/shard_map/finish/pallas_call | solution.py:184
  (37 shorter events, 0.2 us)
Async XLA Ops:
  0.0 7.3 %copy-start = (bf16[64,48]{0,1:T(8,128)(2,1)S(1)}, bf16[64,48]{0,1:T(8,128)(2,1)}, u32[]{:S(2)}) copy-start(bf16[64,48]{0,1:T(8,128)(2,1)} %param.6) | copy-start | bytes 18436
  0.0 27.6 %collective-permute-start = (bf16[256,1536]{1,0:T(8,128)(2,1)}, bf16[256,1536]{1,0:T(8,128)(2,1)S(1)}, u32[]{:S(2)}, u32[]{:S(2)}) collective-permute-start(bf16[256,1536]{1,0:T(8,128)(2,1)} %bitcast.13), channel_id=1, source_target_pairs={{0,192},{192,384},{384,576},{576,0},{1,193},{193,385},{385,577},{5... | collective-permute-start | bytes 2359304 | tf_op jit(solution)/shard_map/ppermute | solution.py:22
  4.1 25.5 %collective-permute-start.1 = (bf16[256,1536]{1,0:T(8,128)(2,1)}, bf16[256,1536]{1,0:T(8,128)(2,1)S(1)}, u32[]{:S(2)}, u32[]{:S(2)}) collective-permute-start(bf16[256,1536]{1,0:T(8,128)(2,1)} %bitcast.14), channel_id=1, source_target_pairs={{0,576},{192,0},{384,192},{576,384},{1,577},{193,1},{385,193},{577... | collective-permute-start | bytes 2359304 | tf_op jit(solution)/shard_map/ppermute | solution.py:22
  8.2 31.1 %all-to-all-start = ((bf16[24,2,1536]{2,1,0:T(2,128)(2,1)}), bf16[24,2,1536]{2,1,0:T(2,128)(2,1)S(1)}, u32[]{:S(2)}, u32[]{:S(2)}) async-start(bf16[24,2,1536]{2,1,0:T(2,128)(2,1)} %reshape.81), calls=%async_computation | async-start | bytes 294912 | tf_op jit(solution)/shard_map/all_to_all | solution.py:32
  27.6 20.8 %copy-start.5 = (bf16[256,1536]{1,0:T(8,128)(2,1)}, bf16[256,1536]{1,0:T(8,128)(2,1)S(1)}, u32[]{:S(2)}) copy-start(bf16[256,1536]{1,0:T(8,128)(2,1)S(1)} %collective-permute-done.t1) | copy-start | bytes 2359300
  27.6 11.9 %collective-permute-start.2 = (bf16[64,1536]{1,0:T(8,128)(2,1)S(1)}, bf16[64,1536]{1,0:T(8,128)(2,1)S(1)}, u32[]{:S(2)}, u32[]{:S(2)}) collective-permute-start(bf16[64,1536]{1,0:T(8,128)(2,1)S(1)} %slice.16), channel_id=1, source_target_pairs={{0,192},{192,384},{384,576},{576,0},{1,193},{193,385},{385,577},{5... | collective-permute-start | bytes 589832 | tf_op jit(solution)/shard_map/ppermute | solution.py:22
  29.6 22.2 %copy-start.6 = (bf16[256,1536]{1,0:T(8,128)(2,1)}, bf16[256,1536]{1,0:T(8,128)(2,1)S(1)}, u32[]{:S(2)}) copy-start(bf16[256,1536]{1,0:T(8,128)(2,1)S(1)} %collective-permute-done.1.t3) | copy-start | bytes 2359300
  29.6 10.0 %collective-permute-start.3 = (bf16[64,1536]{1,0:T(8,128)(2,1)S(1)}, bf16[64,1536]{1,0:T(8,128)(2,1)S(1)}, u32[]{:S(2)}, u32[]{:S(2)}) collective-permute-start(bf16[64,1536]{1,0:T(8,128)(2,1)S(1)} %slice.17), channel_id=1, source_target_pairs={{0,576},{192,0},{384,192},{576,384},{1,577},{193,1},{385,193},{577... | collective-permute-start | bytes 589832 | tf_op jit(solution)/shard_map/ppermute | solution.py:22
  34.2 0.7 copy-start.7
  39.6 0.7 copy-start.13
  39.6 0.7 copy-start.15
  41.4 23.5 %all-to-all-start.1 = ((bf16[16,48,384]{2,1,0:T(8,128)(2,1)}), bf16[16,48,384]{2,1,0:T(8,128)(2,1)S(1)}, u32[]{:S(2)}, u32[]{:S(2)}) async-start(bf16[16,48,384]{2,1,0:T(8,128)(2,1)} %turn.1), calls=%async_computation.1 | async-start | bytes 1179648 | tf_op jit(solution)/shard_map/all_to_all | solution.py:152
  48.4 11.4 %collective-permute-start.4 = (bf16[64,1536]{1,0:T(8,128)(2,1)S(1)}, bf16[64,1536]{1,0:T(8,128)(2,1)S(1)}, u32[]{:S(2)}, u32[]{:S(2)}) collective-permute-start(bf16[64,1536]{1,0:T(8,128)(2,1)S(1)} %slice.14), channel_id=1, source_target_pairs={{0,192},{192,384},{384,576},{576,0},{1,193},{193,385},{385,577},{5... | collective-permute-start | bytes 589832 | tf_op jit(solution)/shard_map/ppermute | solution.py:22
  51.7 8.3 %collective-permute-start.5 = (bf16[64,1536]{1,0:T(8,128)(2,1)S(1)}, bf16[64,1536]{1,0:T(8,128)(2,1)S(1)}, u32[]{:S(2)}, u32[]{:S(2)}) collective-permute-start(bf16[64,1536]{1,0:T(8,128)(2,1)S(1)} %slice.15), channel_id=1, source_target_pairs={{0,576},{192,0},{384,192},{576,384},{1,577},{193,1},{385,193},{577... | collective-permute-start | bytes 589832 | tf_op jit(solution)/shard_map/ppermute | solution.py:22
  59.9 10.9 %copy-start.16 = (bf16[64,1536]{1,0:T(8,128)(2,1)}, bf16[64,1536]{1,0:T(8,128)(2,1)S(1)}, u32[]{:S(2)}) copy-start(bf16[64,1536]{1,0:T(8,128)(2,1)S(1)} %collective-permute-done.4.t2b) | copy-start | bytes 589828
  60.1 10.7 %copy-start.17 = (bf16[64,1536]{1,0:T(8,128)(2,1)}, bf16[64,1536]{1,0:T(8,128)(2,1)S(1)}, u32[]{:S(2)}) copy-start(bf16[64,1536]{1,0:T(8,128)(2,1)S(1)} %collective-permute-done.5.t2c) | copy-start | bytes 589828
  64.9 5.9 %copy-start.4 = (bf16[16,48,384]{2,1,0:T(8,128)(2,1)}, bf16[16,48,384]{2,1,0:T(8,128)(2,1)S(1)}, u32[]{:S(2)}) copy-start(bf16[16,48,384]{2,1,0:T(8,128)(2,1)S(1)} %all-to-all-done.1.mine) | copy-start | bytes 1769476
  64.9 5.8 %collective-permute-start.6 = (bf16[16,48,384]{2,1,0:T(8,128)(2,1)S(1)}, bf16[16,48,384]{2,1,0:T(8,128)(2,1)S(1)}, u32[]{:S(2)}, u32[]{:S(2)}) collective-permute-start(bf16[16,48,384]{2,1,0:T(8,128)(2,1)S(1)} %all-to-all-done.1.mine), channel_id=1, source_target_pairs={{0,24},{24,0},{1,25},{25,1},{2,26},{26,2},{3,27},{27,3},{4,28},{28... | collective-permute-start | bytes 1769480 | tf_op jit(solution)/shard_map/ppermute | solution.py:22
  70.8 0.8 copy-start.10
  77.2 13.5 %copy-start.8 = (f32[1536]{0:T(1024)S(1)}, f32[1536]{0:T(1024)}, u32[]{:S(2)}) copy-start(f32[1536]{0:T(1024)} %param.9) | copy-start | bytes 18436
  77.2 13.6 %copy-start.9 = (f32[64]{0:T(128)S(1)}, f32[64]{0:T(128)}, u32[]{:S(2)}) copy-start(f32[64]{0:T(128)} %param.8) | copy-start | bytes 772
  77.2 13.8 %copy-start.14 = (bf16[384,256]{1,0:T(8,128)(2,1)S(1)}, bf16[384,256]{1,0:T(8,128)(2,1)}, u32[]{:S(2)}) copy-start(bf16[384,256]{1,0:T(8,128)(2,1)} %get-tuple-element.28) | copy-start | bytes 589828
  77.2 17.7 %copy-start.12 = (bf16[384,256]{1,0:T(8,128)(2,1)S(1)}, bf16[384,256]{1,0:T(8,128)(2,1)}, u32[]{:S(2)}) copy-start(bf16[384,256]{1,0:T(8,128)(2,1)} %get-tuple-element.29) | copy-start | bytes 589828
  77.2 20.2 %copy-start.11 = (bf16[384,256]{1,0:T(8,128)(2,1)S(1)}, bf16[384,256]{1,0:T(8,128)(2,1)}, u32[]{:S(2)}) copy-start(bf16[384,256]{1,0:T(8,128)(2,1)} %get-tuple-element.30) | copy-start | bytes 589828
  77.2 47.3 %copy-start.1 = (bf16[1,2,2,64,1536]{4,3,2,1,0:T(8,128)(2,1)S(1)}, bf16[1,2,2,64,1536]{4,3,2,1,0:T(8,128)(2,1)}, u32[]{:S(2)}) copy-start(bf16[1,2,2,64,1536]{4,3,2,1,0:T(8,128)(2,1)} %param.5) | copy-start | bytes 2359300
  77.2 47.3 %all-to-all-start.2 = ((bf16[96,16,256]{2,1,0:T(8,128)(2,1)}), bf16[96,16,256]{2,1,0:T(8,128)(2,1)S(1)}, u32[]{:S(2)}, u32[]{:S(2)}) async-start(bf16[96,16,256]{2,1,0:T(8,128)(2,1)} %bitcast.18), calls=%async_computation.2 | async-start | bytes 1572864 | tf_op jit(solution)/shard_map/all_to_all | solution.py:172
  90.6 33.8 %copy-start.2 = (bf16[384,256]{1,0:T(8,128)(2,1)S(1)}, bf16[384,256]{1,0:T(8,128)(2,1)}, u32[]{:S(2)}) copy-start(bf16[384,256]{1,0:T(8,128)(2,1)} %get-tuple-element.27.own0) | copy-start | bytes 589828
  90.9 10.2 %collective-permute-start.7 = (bf16[384,256]{1,0:T(8,128)(2,1)S(1)}, bf16[384,256]{1,0:T(8,128)(2,1)S(1)}, u32[]{:S(2)}, u32[]{:S(2)}) collective-permute-start(bf16[384,256]{1,0:T(8,128)(2,1)S(1)} %copy-done.14), channel_id=1, source_target_pairs={{0,576},{192,0},{384,192},{576,384},{1,577},{193,1},{385,193},{577... | collective-permute-start | bytes 589832 | tf_op jit(solution)/shard_map/ppermute | solution.py:22
  94.9 10.7 %collective-permute-start.8 = (bf16[384,256]{1,0:T(8,128)(2,1)S(1)}, bf16[384,256]{1,0:T(8,128)(2,1)S(1)}, u32[]{:S(2)}, u32[]{:S(2)}) collective-permute-start(bf16[384,256]{1,0:T(8,128)(2,1)S(1)} %copy-done.12), channel_id=1, source_target_pairs={{0,384},{192,576},{384,0},{576,192},{1,385},{193,577},{385,1},{577... | collective-permute-start | bytes 589832 | tf_op jit(solution)/shard_map/ppermute | solution.py:22
  97.4 14.4 %collective-permute-start.9 = (bf16[384,256]{1,0:T(8,128)(2,1)S(1)}, bf16[384,256]{1,0:T(8,128)(2,1)S(1)}, u32[]{:S(2)}, u32[]{:S(2)}) collective-permute-start(bf16[384,256]{1,0:T(8,128)(2,1)S(1)} %copy-done.11), channel_id=1, source_target_pairs={{0,192},{192,384},{384,576},{576,0},{1,193},{193,385},{385,577},{5... | collective-permute-start | bytes 589832 | tf_op jit(solution)/shard_map/ppermute | solution.py:22
  124.5 0.6 copy-start.3

commit v6 on v5

--- a/solution.py
+++ b/solution.py
@@ -12,7 +12,6 @@
 NVIRT = ZH * Y
 BF16, F32 = jnp.bfloat16, jnp.float32
 VMEM = pl.BlockSpec(memory_space=pltpu.VMEM)
-SMEM = pl.BlockSpec(memory_space=pltpu.SMEM)
 NT = (((1,), (1,)), ((), ()))
 
 
@@ -46,9 +45,9 @@
 
 
 def cycle_kernel(
-    place, mine, theirs, t0, t1, t2a, t2b, t2c, t2d, t3, mirror, own0, own1, own2, own3, turned, held, t2
+    mine, theirs, t0, t1, t2a, t2b, t2c, t3, mirror, own0, own1, own2, own3, turned, held, t2
 ):
-    x, c = place[0], place[1]
+    x, c = lax.axis_index("x"), lax.axis_index("c")
     quarter = mirror.shape[1] // X
     count, depth, size = mine.shape
     for number in range(count):
@@ -60,9 +59,10 @@
     for first in range(0, turned.shape[0], size):
         part = lax.dot_general(unit, turned[first : first + size, :], NT, preferred_element_type=F32)
         held[:, first : first + size] = part.astype(BF16)
-    rows = t2a.shape[0]
-    for number, part in enumerate((t2a, t2b, t2c, t2d)):
-        t2[number * rows : (number + 1) * rows, :] = part[...]
+    first = 0
+    for part in (t2a, t2b, t2c):
+        t2[first : first + part.shape[0], :] = part[...]
+        first += part.shape[0]
     for steps, (t, own) in enumerate(((t0, own0), (t1, own1), (t2, own2), (t3, own3))):
         slot = lax.rem(x + (X + X // 2 - steps), X)
         value = lax.dot_general(held[...], t[...], NT, preferred_element_type=F32).astype(BF16)
@@ -72,8 +72,8 @@
         own[...] = value
 
 
-def finish_kernel(place, arrived, own0, own1, own2, own3, t, row_term, virt, out, own_rows):
-    x = place[0]
+def finish_kernel(arrived, own0, own1, own2, own3, t, row_term, virt, out, own_rows):
+    x = lax.axis_index("x")
     width, lanes = arrived.shape[1:]
     quarter = width // X
     pieces = lanes // width
@@ -126,20 +126,17 @@
     npair = X * ZL * C
     index = lax.axis_index(PAIR)
     place = lax.axis_index(VIRT)
-    spot = jnp.stack([lax.axis_index("x"), lax.axis_index("c")]).astype(jnp.int32)
-
     t1 = passed_along(flat, "x", 1)
     t3 = passed_along(flat, "x", 3)
 
     pieces = spread(integrals, VIRT, NVIRT)
     labels_c = lax.dynamic_slice_in_dim(irreps, index * depth, depth)[:, None]
     labels_a = jnp.transpose(irreps.reshape(NVIRT, X, quarter), (1, 0, 2)).reshape(X, NVIRT * quarter)
-    part = lanes // 4
-    t2a = passed_along(t1[:part], "x", 1)
-    t2d = passed_along(t3[3 * part :], "x", 3)
-    pieces, t1, t3, t2a, t2d = lax.optimization_barrier((pieces, t1, t3, t2a, t2d))
-    t2b = passed_along(t1[part : 2 * part], "x", 1)
-    t2c = passed_along(t3[2 * part : 3 * part], "x", 3)
+    early, middle = lanes // 4, lanes * 5 // 8
+    t2a = passed_along(t1[:early], "x", 1)
+    pieces, t1, t3, t2a = lax.optimization_barrier((pieces, t1, t3, t2a))
+    t2c = passed_along(t3[middle:], "x", 3)
+    t2b = passed_along(t1[early:middle], "x", 1)
     sent = pl.pallas_call(
         turn_kernel,
         out_shape=jax.ShapeDtypeStruct((X * ZL, depth, NVIRT * quarter), BF16),
@@ -157,7 +154,7 @@
     mirror, own0, own1, own2, own3 = pl.pallas_call(
         cycle_kernel,
         out_shape=[jax.ShapeDtypeStruct((NVIRT, width, lanes), BF16)] + [share] * X,
-        in_specs=[SMEM] + [VMEM] * 9,
+        in_specs=[VMEM] * 8,
         out_specs=[VMEM] * 5,
         scratch_shapes=[
             pltpu.VMEM((virt_total, NVIRT * quarter), BF16),
@@ -167,7 +164,7 @@
         cost_estimate=pl.CostEstimate(flops=1_210_000_000, bytes_accessed=6_000_000, transcendentals=0),
         compiler_params=pltpu.CompilerParams(vmem_limit_bytes=56 * 2**20),
         name="cycle",
-    )(spot, mine, theirs, flat, t1, t2a, t2b, t2c, t2d, t3)
+    )(mine, theirs, flat, t1, t2a, t2b, t2c, t3)
 
     arrived = lax.all_to_all(
         mirror.reshape(NVIRT * X, quarter, lanes), VIRT + ("x",), split_axis=0, concat_axis=0, tiled=True
@@ -184,13 +181,13 @@
     updated = pl.pallas_call(
         finish_kernel,
         out_shape=jax.ShapeDtypeStruct(flat.shape, BF16),
-        in_specs=[SMEM] + [VMEM] * 8,
+        in_specs=[VMEM] * 8,
         out_specs=VMEM,
         scratch_shapes=[pltpu.VMEM((NVIRT, width, lanes), BF16)],
         cost_estimate=pl.CostEstimate(flops=600_000_000, bytes_accessed=4_000_000, transcendentals=0),
         compiler_params=pltpu.CompilerParams(vmem_limit_bytes=12 * 2**20),
         name="finish",
-    )(spot, arrived, own0, own1, own2, own3, flat, row_term, virt_energy[None, :])
+    )(arrived, own0, own1, own2, own3, flat, row_term, virt_energy[None, :])
     return updated.reshape(amplitudes.shape)
 
 

time: 128 us -> 122 us (0.953)
  the two profiles are of different devices: /device:TPU:1 before, /device:TPU:64 now
where the time goes in v6:
time: 122 us
  starting transfers between devices  65.2 us (53%)
  waiting for transfers between devices  43.8 us (36%)
  Pallas kernels  8.62 us (7%)
  local copies, waits for them, and re-layouts  3.64 us (3%)
    ppermute x9, starting transfers between devices, passed_along(): return lax.ppermute(value, axis, pairs)  28.3 us
    ppermute x9, waiting for transfers between devices, passed_along(): return lax.ppermute(value, axis, pairs)  20.3 us
    all_to_all x1, starting transfers between devices, spread(): return lax.all_to_all(copies, axis, split_axis=0, concat_axis=0, tiled=True)  18.5 us
    all_to_all x1, waiting for transfers between devices, local(): lax.all_to_all(mirror.reshape(NVIRT * X, quarter, lanes), VIRT + ('x',),...  13.3 us
    all_to_all x1, starting transfers between devices, local(): lax.all_to_all(mirror.reshape(NVIRT * X, quarter, lanes), VIRT + ('x',),...  11.1 us
    all_to_all x1, waiting for transfers between devices, spread(): return lax.all_to_all(copies, axis, split_axis=0, concat_axis=0, tiled=True)  10.2 us
    all_to_all x1, starting transfers between devices, local(): lax.all_to_all(sent, ('x', 'zl'), split_axis=0, concat_axis=0, tiled=True)  7.24 us
    pallas_call x1, Pallas kernels, local(): pl.pallas_call(cycle_kernel, out_shape=[jax.ShapeDtypeStruct((NVIRT, widt...  5.52 us
  transfers between devices with their start and end apart: 12, of which 7 were waited for; matrix products, arithmetic and copies ran while one was open for 2% of the time, Pallas kernels for 0%

profile of v6, /device:TPU:64, one launch (start us, length us, event | category | flops | bytes accessed | tf_op | source)
XLA Modules:
  0.0 121.7 jit_solution(3448503899278373656)
XLA Ops:
  0.0 3.5 %collective-permute-start = (bf16[256,1536]{1,0:T(8,128)(2,1)}, bf16[256,1536]{1,0:T(8,128)(2,1)S(1)}, u32[]{:S(2)}, u32[]{:S(2)}) collective-permute-start(bf16[256,1536]{1,0:T(8,128)(2,1)} %bitcast.11), channel_id=1, source_target_pairs={{0,192},{192,384},{384,576},{576,0},{1,193},{193,385},{385,577},{5... | collective-permute-start | bytes 2359304 | tf_op jit(solution)/shard_map/ppermute | solution.py:21
  3.5 3.7 %collective-permute-start.1 = (bf16[256,1536]{1,0:T(8,128)(2,1)}, bf16[256,1536]{1,0:T(8,128)(2,1)S(1)}, u32[]{:S(2)}, u32[]{:S(2)}) collective-permute-start(bf16[256,1536]{1,0:T(8,128)(2,1)} %bitcast.12), channel_id=1, source_target_pairs={{0,576},{192,0},{384,192},{576,384},{1,577},{193,1},{385,193},{577... | collective-permute-start | bytes 2359304 | tf_op jit(solution)/shard_map/ppermute | solution.py:21
  7.3 0.9 reshape.81
  8.1 18.5 %all-to-all-start = ((bf16[24,2,1536]{2,1,0:T(2,128)(2,1)}), bf16[24,2,1536]{2,1,0:T(2,128)(2,1)S(1)}, u32[]{:S(2)}, u32[]{:S(2)}) async-start(bf16[24,2,1536]{2,1,0:T(2,128)(2,1)} %reshape.81), calls=%async_computation | async-start | bytes 294912 | tf_op jit(solution)/shard_map/all_to_all | solution.py:31
  26.7 0.0 collective-permute-done.t1
  26.7 0.0 copy-start.4
  26.7 2.2 %collective-permute-start.2 = (bf16[64,1536]{1,0:T(8,128)(2,1)S(1)}, bf16[64,1536]{1,0:T(8,128)(2,1)S(1)}, u32[]{:S(2)}, u32[]{:S(2)}) collective-permute-start(bf16[64,1536]{1,0:T(8,128)(2,1)S(1)} %slice.12), channel_id=1, source_target_pairs={{0,192},{192,384},{384,576},{576,0},{1,193},{193,385},{385,577},{5... | collective-permute-start | bytes 589832 | tf_op jit(solution)/shard_map/ppermute | solution.py:21
  28.9 0.0 copy-start.6
  28.9 0.7 copy-done.6
  29.6 0.1 reshape.75
  29.7 0.1 dynamic-slice_bitcast_fusion
  29.8 0.1 copy.13.labels_c
  29.9 0.1 reshape.76.labels_a
  30.0 10.2 %all-to-all-done = bf16[24,2,1536]{2,1,0:T(2,128)(2,1)S(1)} async-done(((bf16[24,2,1536]{2,1,0:T(2,128)(2,1)}), bf16[24,2,1536]{2,1,0:T(2,128)(2,1)S(1)}, u32[]{:S(2)}, u32[]{:S(2)}) %all-to-all-start) | async-done | bytes 147488 | tf_op jit(solution)/shard_map/all_to_all | solution.py:31
  40.2 0.2 reshape.82
  40.4 0.0 collective-permute-done.1.t3
  40.4 0.0 copy-start.5
  40.4 0.0 collective-permute-done.2.t2a
  40.4 0.2 copy.14.pieces
  40.7 1.1 turn.1
  41.8 7.2 %all-to-all-start.1 = ((bf16[16,48,384]{2,1,0:T(8,128)(2,1)}), bf16[16,48,384]{2,1,0:T(8,128)(2,1)S(1)}, u32[]{:S(2)}, u32[]{:S(2)}) async-start(bf16[16,48,384]{2,1,0:T(8,128)(2,1)} %turn.1), calls=%async_computation.1 | async-start | bytes 1179648 | tf_op jit(solution)/shard_map/all_to_all | solution.py:149
  49.1 3.4 %collective-permute-start.3 = (bf16[96,1536]{1,0:T(8,128)(2,1)S(1)}, bf16[96,1536]{1,0:T(8,128)(2,1)S(1)}, u32[]{:S(2)}, u32[]{:S(2)}) collective-permute-start(bf16[96,1536]{1,0:T(8,128)(2,1)S(1)} %slice.10), channel_id=1, source_target_pairs={{0,192},{192,384},{384,576},{576,0},{1,193},{193,385},{385,577},{5... | collective-permute-start | bytes 884744 | tf_op jit(solution)/shard_map/ppermute | solution.py:21
  52.5 3.7 %collective-permute-start.4 = (bf16[96,1536]{1,0:T(8,128)(2,1)S(1)}, bf16[96,1536]{1,0:T(8,128)(2,1)S(1)}, u32[]{:S(2)}, u32[]{:S(2)}) collective-permute-start(bf16[96,1536]{1,0:T(8,128)(2,1)S(1)} %slice.11), channel_id=1, source_target_pairs={{0,576},{192,0},{384,192},{576,384},{1,577},{193,1},{385,193},{577... | collective-permute-start | bytes 884744 | tf_op jit(solution)/shard_map/ppermute | solution.py:21
  56.2 7.6 %collective-permute-done.3.t2b = bf16[96,1536]{1,0:T(8,128)(2,1)S(1)} collective-permute-done((bf16[96,1536]{1,0:T(8,128)(2,1)S(1)}, bf16[96,1536]{1,0:T(8,128)(2,1)S(1)}, u32[]{:S(2)}, u32[]{:S(2)}) %collective-permute-start.3) | collective-permute-done | bytes 294944 | tf_op jit(solution)/shard_map/ppermute | solution.py:21
  63.8 0.0 collective-permute-done.4.t2c
  63.8 0.0 all-to-all-done.1.mine
  63.8 1.9 %collective-permute-start.5 = (bf16[16,48,384]{2,1,0:T(8,128)(2,1)S(1)}, bf16[16,48,384]{2,1,0:T(8,128)(2,1)S(1)}, u32[]{:S(2)}, u32[]{:S(2)}) collective-permute-start(bf16[16,48,384]{2,1,0:T(8,128)(2,1)S(1)} %all-to-all-done.1.mine), channel_id=1, source_target_pairs={{0,24},{24,0},{1,25},{25,1},{2,26},{26,2},{3,27},{27,3},{4,28},{28... | collective-permute-start | bytes 1769480 | tf_op jit(solution)/shard_map/ppermute | solution.py:21
  65.7 2.0 %collective-permute-done.5.theirs = bf16[16,48,384]{2,1,0:T(8,128)(2,1)S(1)} collective-permute-done((bf16[16,48,384]{2,1,0:T(8,128)(2,1)S(1)}, bf16[16,48,384]{2,1,0:T(8,128)(2,1)S(1)}, u32[]{:S(2)}, u32[]{:S(2)}) %collective-permute-start.5) | collective-permute-done | bytes 589856 | tf_op jit(solution)/shard_map/ppermute | solution.py:21
  67.7 0.0 copy-done.11
  67.7 0.8 copy-done.9
  68.5 5.5 %cycle.1 = (bf16[24,64,256]{2,1,0:T(8,128)(2,1)}, bf16[384,256]{1,0:T(8,128)(2,1)}, bf16[384,256]{1,0:T(8,128)(2,1)}, bf16[384,256]{1,0:T(8,128)(2,1)}, bf16[384,256]{1,0:T(8,128)(2,1)}) custom-call(bf16[16,48,384]{2,1,0:T(8,128)(2,1)} %copy-done.3, bf16[16,48,384]{2,1,0:T(8,128)(2,1)} %copy-done.9, bf16[256,1536]{1,0:T(8,128)(2,1)} %bitcast.13, ...), custom_call_target="tpu_custom_call" | custom-call | flops 1210000000 | bytes 6000000 | tf_op jit(solution)/shard_map/cycle/pallas_call | solution.py:154
  74.1 0.0 copy-start.1
  74.1 11.1 %all-to-all-start.2 = ((bf16[96,16,256]{2,1,0:T(8,128)(2,1)}), bf16[96,16,256]{2,1,0:T(8,128)(2,1)S(1)}, u32[]{:S(2)}, u32[]{:S(2)}) async-start(bf16[96,16,256]{2,1,0:T(8,128)(2,1)} %bitcast.16), calls=%async_computation.2 | async-start | bytes 1572864 | tf_op jit(solution)/shard_map/all_to_all | solution.py:169
  85.2 0.0 copy-start.2
  85.2 0.1 dynamic_slice.15
  85.3 0.1 fusion
  85.4 0.1 broadcast_add_fusion
  85.5 4.5 %collective-permute-start.6 = (bf16[384,256]{1,0:T(8,128)(2,1)S(1)}, bf16[384,256]{1,0:T(8,128)(2,1)S(1)}, u32[]{:S(2)}, u32[]{:S(2)}) collective-permute-start(bf16[384,256]{1,0:T(8,128)(2,1)S(1)} %copy-done.14), channel_id=1, source_target_pairs={{0,576},{192,0},{384,192},{576,384},{1,577},{193,1},{385,193},{577... | collective-permute-start | bytes 589832 | tf_op jit(solution)/shard_map/ppermute | solution.py:21
  89.9 0.0 copy-done.13
  90.0 2.8 %collective-permute-start.7 = (bf16[384,256]{1,0:T(8,128)(2,1)S(1)}, bf16[384,256]{1,0:T(8,128)(2,1)S(1)}, u32[]{:S(2)}, u32[]{:S(2)}) collective-permute-start(bf16[384,256]{1,0:T(8,128)(2,1)S(1)} %copy-done.13), channel_id=1, source_target_pairs={{0,384},{192,576},{384,0},{576,192},{1,385},{193,577},{385,1},{577... | collective-permute-start | bytes 589832 | tf_op jit(solution)/shard_map/ppermute | solution.py:21
  92.7 2.8 %collective-permute-start.8 = (bf16[384,256]{1,0:T(8,128)(2,1)S(1)}, bf16[384,256]{1,0:T(8,128)(2,1)S(1)}, u32[]{:S(2)}, u32[]{:S(2)}) collective-permute-start(bf16[384,256]{1,0:T(8,128)(2,1)S(1)} %copy-done.12), channel_id=1, source_target_pairs={{0,192},{192,384},{384,576},{576,0},{1,193},{193,385},{385,577},{5... | collective-permute-start | bytes 589832 | tf_op jit(solution)/shard_map/ppermute | solution.py:21
  95.5 0.1 broadcast_subtract_fusion
  95.6 0.1 sub.27.row_term
  95.7 4.8 %collective-permute-done.6.own1 = bf16[384,256]{1,0:T(8,128)(2,1)S(1)} collective-permute-done((bf16[384,256]{1,0:T(8,128)(2,1)S(1)}, bf16[384,256]{1,0:T(8,128)(2,1)S(1)}, u32[]{:S(2)}, u32[]{:S(2)}) %collective-permute-start.6) | collective-permute-done | bytes 196640 | tf_op jit(solution)/shard_map/ppermute | solution.py:21
  100.5 1.4 %collective-permute-done.7.own2 = bf16[384,256]{1,0:T(8,128)(2,1)S(1)} collective-permute-done((bf16[384,256]{1,0:T(8,128)(2,1)S(1)}, bf16[384,256]{1,0:T(8,128)(2,1)S(1)}, u32[]{:S(2)}, u32[]{:S(2)}) %collective-permute-start.7) | collective-permute-done | bytes 196640 | tf_op jit(solution)/shard_map/ppermute | solution.py:21
  101.9 4.6 %collective-permute-done.8.own3 = bf16[384,256]{1,0:T(8,128)(2,1)S(1)} collective-permute-done((bf16[384,256]{1,0:T(8,128)(2,1)S(1)}, bf16[384,256]{1,0:T(8,128)(2,1)S(1)}, u32[]{:S(2)}, u32[]{:S(2)}) %collective-permute-start.8) | collective-permute-done | bytes 196640 | tf_op jit(solution)/shard_map/ppermute | solution.py:21
  106.5 13.3 %all-to-all-done.2 = bf16[96,16,256]{2,1,0:T(8,128)(2,1)S(1)} async-done(((bf16[96,16,256]{2,1,0:T(8,128)(2,1)}), bf16[96,16,256]{2,1,0:T(8,128)(2,1)S(1)}, u32[]{:S(2)}, u32[]{:S(2)}) %all-to-all-start.2) | async-done | bytes 786464 | tf_op jit(solution)/shard_map/all_to_all | solution.py:169
  119.8 2.0 %finish.1 = bf16[256,1536]{1,0:T(8,128)(2,1)} custom-call(bf16[24,64,256]{2,1,0:T(8,128)(2,1)S(1)} %bitcast.10, bf16[384,256]{1,0:T(8,128)(2,1)S(1)} %copy-done.2, bf16[384,256]{1,0:T(8,128)(2,1)S(1)} %collective-permute-done.6.own1, bf16[384,256]{1,0:T(8,128)(2,1)S(1)} %collective-permute-done.7.own2, bf16[384,256]{1,0:T(8,128)(2,1)S(1)} %collective-permute-done.8.own3, ...), custom_call_target="tpu_custom_call" | custom-call | flops 600000000 | bytes 4000000 | tf_op jit(solution)/shard_map/finish/pallas_call | solution.py:181
  (29 shorter events, 0.2 us)
Async XLA Ops:
  0.0 7.2 %copy-start = (bf16[64,48]{0,1:T(8,128)(2,1)S(1)}, bf16[64,48]{0,1:T(8,128)(2,1)}, u32[]{:S(2)}) copy-start(bf16[64,48]{0,1:T(8,128)(2,1)} %param.6) | copy-start | bytes 18436
  0.0 26.7 %collective-permute-start = (bf16[256,1536]{1,0:T(8,128)(2,1)}, bf16[256,1536]{1,0:T(8,128)(2,1)S(1)}, u32[]{:S(2)}, u32[]{:S(2)}) collective-permute-start(bf16[256,1536]{1,0:T(8,128)(2,1)} %bitcast.11), channel_id=1, source_target_pairs={{0,192},{192,384},{384,576},{576,0},{1,193},{193,385},{385,577},{5... | collective-permute-start | bytes 2359304 | tf_op jit(solution)/shard_map/ppermute | solution.py:21
  3.5 36.9 %collective-permute-start.1 = (bf16[256,1536]{1,0:T(8,128)(2,1)}, bf16[256,1536]{1,0:T(8,128)(2,1)S(1)}, u32[]{:S(2)}, u32[]{:S(2)}) collective-permute-start(bf16[256,1536]{1,0:T(8,128)(2,1)} %bitcast.12), channel_id=1, source_target_pairs={{0,576},{192,0},{384,192},{576,384},{1,577},{193,1},{385,193},{577... | collective-permute-start | bytes 2359304 | tf_op jit(solution)/shard_map/ppermute | solution.py:21
  8.1 32.0 %all-to-all-start = ((bf16[24,2,1536]{2,1,0:T(2,128)(2,1)}), bf16[24,2,1536]{2,1,0:T(2,128)(2,1)S(1)}, u32[]{:S(2)}, u32[]{:S(2)}) async-start(bf16[24,2,1536]{2,1,0:T(2,128)(2,1)} %reshape.81), calls=%async_computation | async-start | bytes 294912 | tf_op jit(solution)/shard_map/all_to_all | solution.py:31
  26.7 22.4 %copy-start.4 = (bf16[256,1536]{1,0:T(8,128)(2,1)}, bf16[256,1536]{1,0:T(8,128)(2,1)S(1)}, u32[]{:S(2)}) copy-start(bf16[256,1536]{1,0:T(8,128)(2,1)S(1)} %collective-permute-done.t1) | copy-start | bytes 2359300
  26.7 13.7 %collective-permute-start.2 = (bf16[64,1536]{1,0:T(8,128)(2,1)S(1)}, bf16[64,1536]{1,0:T(8,128)(2,1)S(1)}, u32[]{:S(2)}, u32[]{:S(2)}) collective-permute-start(bf16[64,1536]{1,0:T(8,128)(2,1)S(1)} %slice.12), channel_id=1, source_target_pairs={{0,192},{192,384},{384,576},{576,0},{1,193},{193,385},{385,577},{5... | collective-permute-start | bytes 589832 | tf_op jit(solution)/shard_map/ppermute | solution.py:21
  28.9 0.7 copy-start.6
  40.4 12.1 %copy-start.5 = (bf16[256,1536]{1,0:T(8,128)(2,1)}, bf16[256,1536]{1,0:T(8,128)(2,1)S(1)}, u32[]{:S(2)}) copy-start(bf16[256,1536]{1,0:T(8,128)(2,1)S(1)} %collective-permute-done.1.t3) | copy-start | bytes 2359300
  40.4 1.4 %copy-start.15 = (bf16[64,1536]{1,0:T(8,128)(2,1)}, bf16[64,1536]{1,0:T(8,128)(2,1)S(1)}, u32[]{:S(2)}) copy-start(bf16[64,1536]{1,0:T(8,128)(2,1)S(1)} %collective-permute-done.2.t2a) | copy-start | bytes 589828
  41.8 21.9 %all-to-all-start.1 = ((bf16[16,48,384]{2,1,0:T(8,128)(2,1)}), bf16[16,48,384]{2,1,0:T(8,128)(2,1)S(1)}, u32[]{:S(2)}, u32[]{:S(2)}) async-start(bf16[16,48,384]{2,1,0:T(8,128)(2,1)} %turn.1), calls=%async_computation.1 | async-start | bytes 1179648 | tf_op jit(solution)/shard_map/all_to_all | solution.py:149
  49.1 14.7 %collective-permute-start.3 = (bf16[96,1536]{1,0:T(8,128)(2,1)S(1)}, bf16[96,1536]{1,0:T(8,128)(2,1)S(1)}, u32[]{:S(2)}, u32[]{:S(2)}) collective-permute-start(bf16[96,1536]{1,0:T(8,128)(2,1)S(1)} %slice.10), channel_id=1, source_target_pairs={{0,192},{192,384},{384,576},{576,0},{1,193},{193,385},{385,577},{5... | collective-permute-start | bytes 884744 | tf_op jit(solution)/shard_map/ppermute | solution.py:21
  52.5 11.3 %collective-permute-start.4 = (bf16[96,1536]{1,0:T(8,128)(2,1)S(1)}, bf16[96,1536]{1,0:T(8,128)(2,1)S(1)}, u32[]{:S(2)}, u32[]{:S(2)}) collective-permute-start(bf16[96,1536]{1,0:T(8,128)(2,1)S(1)} %slice.11), channel_id=1, source_target_pairs={{0,576},{192,0},{384,192},{576,384},{1,577},{193,1},{385,193},{577... | collective-permute-start | bytes 884744 | tf_op jit(solution)/shard_map/ppermute | solution.py:21
  63.8 3.9 %copy-start.10 = (bf16[96,1536]{1,0:T(8,128)(2,1)}, bf16[96,1536]{1,0:T(8,128)(2,1)S(1)}, u32[]{:S(2)}) copy-start(bf16[96,1536]{1,0:T(8,128)(2,1)S(1)} %collective-permute-done.3.t2b) | copy-start | bytes 884740
  63.8 3.9 %copy-start.11 = (bf16[96,1536]{1,0:T(8,128)(2,1)}, bf16[96,1536]{1,0:T(8,128)(2,1)S(1)}, u32[]{:S(2)}) copy-start(bf16[96,1536]{1,0:T(8,128)(2,1)S(1)} %collective-permute-done.4.t2c) | copy-start | bytes 884740
  63.8 3.9 %copy-start.3 = (bf16[16,48,384]{2,1,0:T(8,128)(2,1)}, bf16[16,48,384]{2,1,0:T(8,128)(2,1)S(1)}, u32[]{:S(2)}) copy-start(bf16[16,48,384]{2,1,0:T(8,128)(2,1)S(1)} %all-to-all-done.1.mine) | copy-start | bytes 1769476
  63.8 3.9 %collective-permute-start.5 = (bf16[16,48,384]{2,1,0:T(8,128)(2,1)S(1)}, bf16[16,48,384]{2,1,0:T(8,128)(2,1)S(1)}, u32[]{:S(2)}, u32[]{:S(2)}) collective-permute-start(bf16[16,48,384]{2,1,0:T(8,128)(2,1)S(1)} %all-to-all-done.1.mine), channel_id=1, source_target_pairs={{0,24},{24,0},{1,25},{25,1},{2,26},{26,2},{3,27},{27,3},{4,28},{28... | collective-permute-start | bytes 1769480 | tf_op jit(solution)/shard_map/ppermute | solution.py:21
  67.7 0.8 copy-start.9
  74.0 11.2 %copy-start.7 = (f32[1536]{0:T(1024)S(1)}, f32[1536]{0:T(1024)}, u32[]{:S(2)}) copy-start(f32[1536]{0:T(1024)} %param.9) | copy-start | bytes 18436
  74.0 11.3 %copy-start.8 = (f32[64]{0:T(128)S(1)}, f32[64]{0:T(128)}, u32[]{:S(2)}) copy-start(f32[64]{0:T(128)} %param.8) | copy-start | bytes 772
  74.0 11.4 %copy-start.14 = (bf16[384,256]{1,0:T(8,128)(2,1)S(1)}, bf16[384,256]{1,0:T(8,128)(2,1)}, u32[]{:S(2)}) copy-start(bf16[384,256]{1,0:T(8,128)(2,1)} %get-tuple-element.26) | copy-start | bytes 589828
  74.0 15.9 %copy-start.13 = (bf16[384,256]{1,0:T(8,128)(2,1)S(1)}, bf16[384,256]{1,0:T(8,128)(2,1)}, u32[]{:S(2)}) copy-start(bf16[384,256]{1,0:T(8,128)(2,1)} %get-tuple-element.27) | copy-start | bytes 589828
  74.0 18.7 %copy-start.12 = (bf16[384,256]{1,0:T(8,128)(2,1)S(1)}, bf16[384,256]{1,0:T(8,128)(2,1)}, u32[]{:S(2)}) copy-start(bf16[384,256]{1,0:T(8,128)(2,1)} %get-tuple-element.28) | copy-start | bytes 589828
  74.1 45.7 %copy-start.1 = (bf16[1,2,2,64,1536]{4,3,2,1,0:T(8,128)(2,1)S(1)}, bf16[1,2,2,64,1536]{4,3,2,1,0:T(8,128)(2,1)}, u32[]{:S(2)}) copy-start(bf16[1,2,2,64,1536]{4,3,2,1,0:T(8,128)(2,1)} %param.5) | copy-start | bytes 2359300
  74.1 45.7 %all-to-all-start.2 = ((bf16[96,16,256]{2,1,0:T(8,128)(2,1)}), bf16[96,16,256]{2,1,0:T(8,128)(2,1)S(1)}, u32[]{:S(2)}, u32[]{:S(2)}) async-start(bf16[96,16,256]{2,1,0:T(8,128)(2,1)} %bitcast.16), calls=%async_computation.2 | async-start | bytes 1572864 | tf_op jit(solution)/shard_map/all_to_all | solution.py:169
  85.2 34.6 %copy-start.2 = (bf16[384,256]{1,0:T(8,128)(2,1)S(1)}, bf16[384,256]{1,0:T(8,128)(2,1)}, u32[]{:S(2)}) copy-start(bf16[384,256]{1,0:T(8,128)(2,1)} %get-tuple-element.25.own0) | copy-start | bytes 589828
  85.5 15.1 %collective-permute-start.6 = (bf16[384,256]{1,0:T(8,128)(2,1)S(1)}, bf16[384,256]{1,0:T(8,128)(2,1)S(1)}, u32[]{:S(2)}, u32[]{:S(2)}) collective-permute-start(bf16[384,256]{1,0:T(8,128)(2,1)S(1)} %copy-done.14), channel_id=1, source_target_pairs={{0,576},{192,0},{384,192},{576,384},{1,577},{193,1},{385,193},{577... | collective-permute-start | bytes 589832 | tf_op jit(solution)/shard_map/ppermute | solution.py:21
  90.0 12.0 %collective-permute-start.7 = (bf16[384,256]{1,0:T(8,128)(2,1)S(1)}, bf16[384,256]{1,0:T(8,128)(2,1)S(1)}, u32[]{:S(2)}, u32[]{:S(2)}) collective-permute-start(bf16[384,256]{1,0:T(8,128)(2,1)S(1)} %copy-done.13), channel_id=1, source_target_pairs={{0,384},{192,576},{384,0},{576,192},{1,385},{193,577},{385,1},{577... | collective-permute-start | bytes 589832 | tf_op jit(solution)/shard_map/ppermute | solution.py:21
  92.7 13.7 %collective-permute-start.8 = (bf16[384,256]{1,0:T(8,128)(2,1)S(1)}, bf16[384,256]{1,0:T(8,128)(2,1)S(1)}, u32[]{:S(2)}, u32[]{:S(2)}) collective-permute-start(bf16[384,256]{1,0:T(8,128)(2,1)S(1)} %copy-done.12), channel_id=1, source_target_pairs={{0,192},{192,384},{384,576},{576,0},{1,193},{193,385},{385,577},{5... | collective-permute-start | bytes 589832 | tf_op jit(solution)/shard_map/ppermute | solution.py:21

commit v7 on v6

--- a/solution.py
+++ b/solution.py
@@ -132,7 +132,7 @@
     pieces = spread(integrals, VIRT, NVIRT)
     labels_c = lax.dynamic_slice_in_dim(irreps, index * depth, depth)[:, None]
     labels_a = jnp.transpose(irreps.reshape(NVIRT, X, quarter), (1, 0, 2)).reshape(X, NVIRT * quarter)
-    early, middle = lanes // 4, lanes * 5 // 8
+    early, middle = lanes // 8, lanes * 9 // 16
     t2a = passed_along(t1[:early], "x", 1)
     pieces, t1, t3, t2a = lax.optimization_barrier((pieces, t1, t3, t2a))
     t2c = passed_along(t3[middle:], "x", 3)

time: 122 us -> 123 us (level)
  no operation moved by 1% of the time
where the time goes in v7:
time: 123 us; the launch traced here: 122 us
  starting transfers between devices  64 us (52%)
  waiting for transfers between devices  44.8 us (36%)
  Pallas kernels  8.6 us (7%)
  local copies, waits for them, and re-layouts  4.07 us (3%)
    ppermute x9, starting transfers between devices, passed_along(): return lax.ppermute(value, axis, pairs)  28.3 us
    ppermute x9, waiting for transfers between devices, passed_along(): return lax.ppermute(value, axis, pairs)  21.4 us
    all_to_all x1, starting transfers between devices, spread(): return lax.all_to_all(copies, axis, split_axis=0, concat_axis=0, tiled=True)  18.5 us
    all_to_all x1, waiting for transfers between devices, local(): lax.all_to_all(mirror.reshape(NVIRT * X, quarter, lanes), VIRT + ('x',),...  13.2 us
    all_to_all x1, waiting for transfers between devices, spread(): return lax.all_to_all(copies, axis, split_axis=0, concat_axis=0, tiled=True)  10.2 us
    all_to_all x1, starting transfers between devices, local(): lax.all_to_all(mirror.reshape(NVIRT * X, quarter, lanes), VIRT + ('x',),...  9.89 us
    all_to_all x1, starting transfers between devices, local(): lax.all_to_all(sent, ('x', 'zl'), split_axis=0, concat_axis=0, tiled=True)  7.24 us
    pallas_call x1, Pallas kernels, local(): pl.pallas_call(cycle_kernel, out_shape=[jax.ShapeDtypeStruct((NVIRT, widt...  5.51 us
  transfers between devices with their start and end apart: 12, of which 7 were waited for; matrix products, arithmetic and copies ran while one was open for 2% of the time, Pallas kernels for 0%

profile of v7, /device:TPU:64, one launch (start us, length us, event | category | flops | bytes accessed | tf_op | source)
XLA Modules:
  0.0 122.0 jit_solution(9161625621341899962)
XLA Ops:
  0.0 3.5 %collective-permute-start = (bf16[256,1536]{1,0:T(8,128)(2,1)}, bf16[256,1536]{1,0:T(8,128)(2,1)S(1)}, u32[]{:S(2)}, u32[]{:S(2)}) collective-permute-start(bf16[256,1536]{1,0:T(8,128)(2,1)} %bitcast.11), channel_id=1, source_target_pairs={{0,192},{192,384},{384,576},{576,0},{1,193},{193,385},{385,577},{5... | collective-permute-start | bytes 2359304 | tf_op jit(solution)/shard_map/ppermute | solution.py:21
  3.5 3.7 %collective-permute-start.1 = (bf16[256,1536]{1,0:T(8,128)(2,1)}, bf16[256,1536]{1,0:T(8,128)(2,1)S(1)}, u32[]{:S(2)}, u32[]{:S(2)}) collective-permute-start(bf16[256,1536]{1,0:T(8,128)(2,1)} %bitcast.12), channel_id=1, source_target_pairs={{0,576},{192,0},{384,192},{576,384},{1,577},{193,1},{385,193},{577... | collective-permute-start | bytes 2359304 | tf_op jit(solution)/shard_map/ppermute | solution.py:21
  7.3 0.9 reshape.81
  8.1 18.5 %all-to-all-start = ((bf16[24,2,1536]{2,1,0:T(2,128)(2,1)}), bf16[24,2,1536]{2,1,0:T(2,128)(2,1)S(1)}, u32[]{:S(2)}, u32[]{:S(2)}) async-start(bf16[24,2,1536]{2,1,0:T(2,128)(2,1)} %reshape.81), calls=%async_computation | async-start | bytes 294912 | tf_op jit(solution)/shard_map/all_to_all | solution.py:31
  26.7 0.0 copy-start.6
  26.7 0.7 copy-done.6
  27.4 0.1 reshape.75
  27.5 0.0 collective-permute-done.t1
  27.5 0.0 copy-start.4
  27.5 2.2 %collective-permute-start.2 = (bf16[32,1536]{1,0:T(8,128)(2,1)S(1)}, bf16[32,1536]{1,0:T(8,128)(2,1)S(1)}, u32[]{:S(2)}, u32[]{:S(2)}) collective-permute-start(bf16[32,1536]{1,0:T(8,128)(2,1)S(1)} %slice.12), channel_id=1, source_target_pairs={{0,192},{192,384},{384,576},{576,0},{1,193},{193,385},{385,577},{5... | collective-permute-start | bytes 294920 | tf_op jit(solution)/shard_map/ppermute | solution.py:21
  29.7 0.1 dynamic-slice_bitcast_fusion
  29.8 0.1 copy.13.labels_c
  29.9 0.1 reshape.76.labels_a
  30.0 10.2 %all-to-all-done = bf16[24,2,1536]{2,1,0:T(2,128)(2,1)S(1)} async-done(((bf16[24,2,1536]{2,1,0:T(2,128)(2,1)}), bf16[24,2,1536]{2,1,0:T(2,128)(2,1)S(1)}, u32[]{:S(2)}, u32[]{:S(2)}) %all-to-all-start) | async-done | bytes 147488 | tf_op jit(solution)/shard_map/all_to_all | solution.py:31
  40.2 0.2 reshape.82
  40.4 0.0 collective-permute-done.1.t3
  40.4 0.0 copy-start.5
  40.4 0.0 collective-permute-done.2.t2a
  40.4 0.2 copy.14.pieces
  40.7 0.4 copy-done.15
  41.1 1.1 turn.1
  42.2 7.2 %all-to-all-start.1 = ((bf16[16,48,384]{2,1,0:T(8,128)(2,1)}), bf16[16,48,384]{2,1,0:T(8,128)(2,1)S(1)}, u32[]{:S(2)}, u32[]{:S(2)}) async-start(bf16[16,48,384]{2,1,0:T(8,128)(2,1)} %turn.1), calls=%async_computation.1 | async-start | bytes 1179648 | tf_op jit(solution)/shard_map/all_to_all | solution.py:149
  49.5 0.0 copy-done.4
  49.5 3.4 %collective-permute-start.3 = (bf16[112,1536]{1,0:T(8,128)(2,1)S(1)}, bf16[112,1536]{1,0:T(8,128)(2,1)S(1)}, u32[]{:S(2)}, u32[]{:S(2)}) collective-permute-start(bf16[112,1536]{1,0:T(8,128)(2,1)S(1)} %slice.10), channel_id=1, source_target_pairs={{0,192},{192,384},{384,576},{576,0},{1,193},{193,385},{385,577},{5... | collective-permute-start | bytes 1032200 | tf_op jit(solution)/shard_map/ppermute | solution.py:21
  52.9 0.0 copy-done.5
  52.9 3.7 %collective-permute-start.4 = (bf16[112,1536]{1,0:T(8,128)(2,1)S(1)}, bf16[112,1536]{1,0:T(8,128)(2,1)S(1)}, u32[]{:S(2)}, u32[]{:S(2)}) collective-permute-start(bf16[112,1536]{1,0:T(8,128)(2,1)S(1)} %slice.11), channel_id=1, source_target_pairs={{0,576},{192,0},{384,192},{576,384},{1,577},{193,1},{385,193},{577... | collective-permute-start | bytes 1032200 | tf_op jit(solution)/shard_map/ppermute | solution.py:21
  56.6 8.6 %collective-permute-done.3.t2b = bf16[112,1536]{1,0:T(8,128)(2,1)S(1)} collective-permute-done((bf16[112,1536]{1,0:T(8,128)(2,1)S(1)}, bf16[112,1536]{1,0:T(8,128)(2,1)S(1)}, u32[]{:S(2)}, u32[]{:S(2)}) %collective-permute-start.3) | collective-permute-done | bytes 344096 | tf_op jit(solution)/shard_map/ppermute | solution.py:21
  65.2 0.0 collective-permute-done.4.t2c
  65.2 0.0 all-to-all-done.1.mine
  65.3 1.9 %collective-permute-start.5 = (bf16[16,48,384]{2,1,0:T(8,128)(2,1)S(1)}, bf16[16,48,384]{2,1,0:T(8,128)(2,1)S(1)}, u32[]{:S(2)}, u32[]{:S(2)}) collective-permute-start(bf16[16,48,384]{2,1,0:T(8,128)(2,1)S(1)} %all-to-all-done.1.mine), channel_id=1, source_target_pairs={{0,24},{24,0},{1,25},{25,1},{2,26},{26,2},{3,27},{27,3},{4,28},{28... | collective-permute-start | bytes 1769480 | tf_op jit(solution)/shard_map/ppermute | solution.py:21
  67.2 2.0 %collective-permute-done.5.theirs = bf16[16,48,384]{2,1,0:T(8,128)(2,1)S(1)} collective-permute-done((bf16[16,48,384]{2,1,0:T(8,128)(2,1)S(1)}, bf16[16,48,384]{2,1,0:T(8,128)(2,1)S(1)}, u32[]{:S(2)}, u32[]{:S(2)}) %collective-permute-start.5) | collective-permute-done | bytes 589856 | tf_op jit(solution)/shard_map/ppermute | solution.py:21
  69.2 0.8 copy-done.9
  70.0 5.5 %cycle.1 = (bf16[24,64,256]{2,1,0:T(8,128)(2,1)}, bf16[384,256]{1,0:T(8,128)(2,1)}, bf16[384,256]{1,0:T(8,128)(2,1)}, bf16[384,256]{1,0:T(8,128)(2,1)}, bf16[384,256]{1,0:T(8,128)(2,1)}) custom-call(bf16[16,48,384]{2,1,0:T(8,128)(2,1)} %copy-done.3, bf16[16,48,384]{2,1,0:T(8,128)(2,1)} %copy-done.9, bf16[256,1536]{1,0:T(8,128)(2,1)} %bitcast.13, ...), custom_call_target="tpu_custom_call" | custom-call | flops 1210000000 | bytes 6000000 | tf_op jit(solution)/shard_map/cycle/pallas_call | solution.py:154
  75.5 0.0 copy-start.1
  75.5 9.9 %all-to-all-start.2 = ((bf16[96,16,256]{2,1,0:T(8,128)(2,1)}), bf16[96,16,256]{2,1,0:T(8,128)(2,1)S(1)}, u32[]{:S(2)}, u32[]{:S(2)}) async-start(bf16[96,16,256]{2,1,0:T(8,128)(2,1)} %bitcast.16), calls=%async_computation.2 | async-start | bytes 1572864 | tf_op jit(solution)/shard_map/all_to_all | solution.py:169
  85.5 0.1 dynamic_slice.15
  85.6 0.1 fusion
  85.7 0.1 broadcast_add_fusion
  85.7 4.5 %collective-permute-start.6 = (bf16[384,256]{1,0:T(8,128)(2,1)S(1)}, bf16[384,256]{1,0:T(8,128)(2,1)S(1)}, u32[]{:S(2)}, u32[]{:S(2)}) collective-permute-start(bf16[384,256]{1,0:T(8,128)(2,1)S(1)} %copy-done.14), channel_id=1, source_target_pairs={{0,576},{192,0},{384,192},{576,384},{1,577},{193,1},{385,193},{577... | collective-permute-start | bytes 589832 | tf_op jit(solution)/shard_map/ppermute | solution.py:21
  90.2 2.8 %collective-permute-start.7 = (bf16[384,256]{1,0:T(8,128)(2,1)S(1)}, bf16[384,256]{1,0:T(8,128)(2,1)S(1)}, u32[]{:S(2)}, u32[]{:S(2)}) collective-permute-start(bf16[384,256]{1,0:T(8,128)(2,1)S(1)} %copy-done.13), channel_id=1, source_target_pairs={{0,384},{192,576},{384,0},{576,192},{1,385},{193,577},{385,1},{577... | collective-permute-start | bytes 589832 | tf_op jit(solution)/shard_map/ppermute | solution.py:21
  93.0 2.8 %collective-permute-start.8 = (bf16[384,256]{1,0:T(8,128)(2,1)S(1)}, bf16[384,256]{1,0:T(8,128)(2,1)S(1)}, u32[]{:S(2)}, u32[]{:S(2)}) collective-permute-start(bf16[384,256]{1,0:T(8,128)(2,1)S(1)} %copy-done.12), channel_id=1, source_target_pairs={{0,192},{192,384},{384,576},{576,0},{1,193},{193,385},{385,577},{5... | collective-permute-start | bytes 589832 | tf_op jit(solution)/shard_map/ppermute | solution.py:21
  95.8 0.1 broadcast_subtract_fusion
  95.8 0.1 sub.27.row_term
  96.0 4.9 %collective-permute-done.6.own1 = bf16[384,256]{1,0:T(8,128)(2,1)S(1)} collective-permute-done((bf16[384,256]{1,0:T(8,128)(2,1)S(1)}, bf16[384,256]{1,0:T(8,128)(2,1)S(1)}, u32[]{:S(2)}, u32[]{:S(2)}) %collective-permute-start.6) | collective-permute-done | bytes 196640 | tf_op jit(solution)/shard_map/ppermute | solution.py:21
  100.9 1.7 %collective-permute-done.7.own2 = bf16[384,256]{1,0:T(8,128)(2,1)S(1)} collective-permute-done((bf16[384,256]{1,0:T(8,128)(2,1)S(1)}, bf16[384,256]{1,0:T(8,128)(2,1)S(1)}, u32[]{:S(2)}, u32[]{:S(2)}) %collective-permute-start.7) | collective-permute-done | bytes 196640 | tf_op jit(solution)/shard_map/ppermute | solution.py:21
  102.5 4.3 %collective-permute-done.8.own3 = bf16[384,256]{1,0:T(8,128)(2,1)S(1)} collective-permute-done((bf16[384,256]{1,0:T(8,128)(2,1)S(1)}, bf16[384,256]{1,0:T(8,128)(2,1)S(1)}, u32[]{:S(2)}, u32[]{:S(2)}) %collective-permute-start.8) | collective-permute-done | bytes 196640 | tf_op jit(solution)/shard_map/ppermute | solution.py:21
  106.8 13.2 %all-to-all-done.2 = bf16[96,16,256]{2,1,0:T(8,128)(2,1)S(1)} async-done(((bf16[96,16,256]{2,1,0:T(8,128)(2,1)}), bf16[96,16,256]{2,1,0:T(8,128)(2,1)S(1)}, u32[]{:S(2)}, u32[]{:S(2)}) %all-to-all-start.2) | async-done | bytes 786464 | tf_op jit(solution)/shard_map/all_to_all | solution.py:169
  120.0 2.0 %finish.1 = bf16[256,1536]{1,0:T(8,128)(2,1)} custom-call(bf16[24,64,256]{2,1,0:T(8,128)(2,1)S(1)} %bitcast.10, bf16[384,256]{1,0:T(8,128)(2,1)S(1)} %copy-done.2, bf16[384,256]{1,0:T(8,128)(2,1)S(1)} %collective-permute-done.6.own1, bf16[384,256]{1,0:T(8,128)(2,1)S(1)} %collective-permute-done.7.own2, bf16[384,256]{1,0:T(8,128)(2,1)S(1)} %collective-permute-done.8.own3, ...), custom_call_target="tpu_custom_call" | custom-call | flops 600000000 | bytes 4000000 | tf_op jit(solution)/shard_map/finish/pallas_call | solution.py:181
  (29 shorter events, 0.2 us)
Async XLA Ops:
  0.0 7.2 %copy-start = (bf16[64,48]{0,1:T(8,128)(2,1)S(1)}, bf16[64,48]{0,1:T(8,128)(2,1)}, u32[]{:S(2)}) copy-start(bf16[64,48]{0,1:T(8,128)(2,1)} %param.6) | copy-start | bytes 18436
  0.0 27.5 %collective-permute-start = (bf16[256,1536]{1,0:T(8,128)(2,1)}, bf16[256,1536]{1,0:T(8,128)(2,1)S(1)}, u32[]{:S(2)}, u32[]{:S(2)}) collective-permute-start(bf16[256,1536]{1,0:T(8,128)(2,1)} %bitcast.11), channel_id=1, source_target_pairs={{0,192},{192,384},{384,576},{576,0},{1,193},{193,385},{385,577},{5... | collective-permute-start | bytes 2359304 | tf_op jit(solution)/shard_map/ppermute | solution.py:21
  3.5 36.9 %collective-permute-start.1 = (bf16[256,1536]{1,0:T(8,128)(2,1)}, bf16[256,1536]{1,0:T(8,128)(2,1)S(1)}, u32[]{:S(2)}, u32[]{:S(2)}) collective-permute-start(bf16[256,1536]{1,0:T(8,128)(2,1)} %bitcast.12), channel_id=1, source_target_pairs={{0,576},{192,0},{384,192},{576,384},{1,577},{193,1},{385,193},{577... | collective-permute-start | bytes 2359304 | tf_op jit(solution)/shard_map/ppermute | solution.py:21
  8.1 32.0 %all-to-all-start = ((bf16[24,2,1536]{2,1,0:T(2,128)(2,1)}), bf16[24,2,1536]{2,1,0:T(2,128)(2,1)S(1)}, u32[]{:S(2)}, u32[]{:S(2)}) async-start(bf16[24,2,1536]{2,1,0:T(2,128)(2,1)} %reshape.81), calls=%async_computation | async-start | bytes 294912 | tf_op jit(solution)/shard_map/all_to_all | solution.py:31
  26.7 0.7 copy-start.6
  27.5 22.0 %copy-start.4 = (bf16[256,1536]{1,0:T(8,128)(2,1)}, bf16[256,1536]{1,0:T(8,128)(2,1)S(1)}, u32[]{:S(2)}) copy-start(bf16[256,1536]{1,0:T(8,128)(2,1)S(1)} %collective-permute-done.t1) | copy-start | bytes 2359300
  27.5 12.9 %collective-permute-start.2 = (bf16[32,1536]{1,0:T(8,128)(2,1)S(1)}, bf16[32,1536]{1,0:T(8,128)(2,1)S(1)}, u32[]{:S(2)}, u32[]{:S(2)}) collective-permute-start(bf16[32,1536]{1,0:T(8,128)(2,1)S(1)} %slice.12), channel_id=1, source_target_pairs={{0,192},{192,384},{384,576},{576,0},{1,193},{193,385},{385,577},{5... | collective-permute-start | bytes 294920 | tf_op jit(solution)/shard_map/ppermute | solution.py:21
  40.4 12.5 %copy-start.5 = (bf16[256,1536]{1,0:T(8,128)(2,1)}, bf16[256,1536]{1,0:T(8,128)(2,1)S(1)}, u32[]{:S(2)}) copy-start(bf16[256,1536]{1,0:T(8,128)(2,1)S(1)} %collective-permute-done.1.t3) | copy-start | bytes 2359300
  40.4 0.7 copy-start.15
  42.2 23.0 %all-to-all-start.1 = ((bf16[16,48,384]{2,1,0:T(8,128)(2,1)}), bf16[16,48,384]{2,1,0:T(8,128)(2,1)S(1)}, u32[]{:S(2)}, u32[]{:S(2)}) async-start(bf16[16,48,384]{2,1,0:T(8,128)(2,1)} %turn.1), calls=%async_computation.1 | async-start | bytes 1179648 | tf_op jit(solution)/shard_map/all_to_all | solution.py:149
  49.5 15.7 %collective-permute-start.3 = (bf16[112,1536]{1,0:T(8,128)(2,1)S(1)}, bf16[112,1536]{1,0:T(8,128)(2,1)S(1)}, u32[]{:S(2)}, u32[]{:S(2)}) collective-permute-start(bf16[112,1536]{1,0:T(8,128)(2,1)S(1)} %slice.10), channel_id=1, source_target_pairs={{0,192},{192,384},{384,576},{576,0},{1,193},{193,385},{385,577},{5... | collective-permute-start | bytes 1032200 | tf_op jit(solution)/shard_map/ppermute | solution.py:21
  52.9 12.3 %collective-permute-start.4 = (bf16[112,1536]{1,0:T(8,128)(2,1)S(1)}, bf16[112,1536]{1,0:T(8,128)(2,1)S(1)}, u32[]{:S(2)}, u32[]{:S(2)}) collective-permute-start(bf16[112,1536]{1,0:T(8,128)(2,1)S(1)} %slice.11), channel_id=1, source_target_pairs={{0,576},{192,0},{384,192},{576,384},{1,577},{193,1},{385,193},{577... | collective-permute-start | bytes 1032200 | tf_op jit(solution)/shard_map/ppermute | solution.py:21
  65.2 3.9 %copy-start.10 = (bf16[112,1536]{1,0:T(8,128)(2,1)}, bf16[112,1536]{1,0:T(8,128)(2,1)S(1)}, u32[]{:S(2)}) copy-start(bf16[112,1536]{1,0:T(8,128)(2,1)S(1)} %collective-permute-done.3.t2b) | copy-start | bytes 1032196
  65.2 3.9 %copy-start.11 = (bf16[112,1536]{1,0:T(8,128)(2,1)}, bf16[112,1536]{1,0:T(8,128)(2,1)S(1)}, u32[]{:S(2)}) copy-start(bf16[112,1536]{1,0:T(8,128)(2,1)S(1)} %collective-permute-done.4.t2c) | copy-start | bytes 1032196
  65.2 3.9 %copy-start.3 = (bf16[16,48,384]{2,1,0:T(8,128)(2,1)}, bf16[16,48,384]{2,1,0:T(8,128)(2,1)S(1)}, u32[]{:S(2)}) copy-start(bf16[16,48,384]{2,1,0:T(8,128)(2,1)S(1)} %all-to-all-done.1.mine) | copy-start | bytes 1769476
  65.3 3.9 %collective-permute-start.5 = (bf16[16,48,384]{2,1,0:T(8,128)(2,1)S(1)}, bf16[16,48,384]{2,1,0:T(8,128)(2,1)S(1)}, u32[]{:S(2)}, u32[]{:S(2)}) collective-permute-start(bf16[16,48,384]{2,1,0:T(8,128)(2,1)S(1)} %all-to-all-done.1.mine), channel_id=1, source_target_pairs={{0,24},{24,0},{1,25},{25,1},{2,26},{26,2},{3,27},{27,3},{4,28},{28... | collective-permute-start | bytes 1769480 | tf_op jit(solution)/shard_map/ppermute | solution.py:21
  69.2 0.8 copy-start.9
  75.5 10.0 %copy-start.7 = (f32[1536]{0:T(1024)S(1)}, f32[1536]{0:T(1024)}, u32[]{:S(2)}) copy-start(f32[1536]{0:T(1024)} %param.9) | copy-start | bytes 18436
  75.5 10.1 %copy-start.8 = (f32[64]{0:T(128)S(1)}, f32[64]{0:T(128)}, u32[]{:S(2)}) copy-start(f32[64]{0:T(128)} %param.8) | copy-start | bytes 772
  75.5 10.2 %copy-start.14 = (bf16[384,256]{1,0:T(8,128)(2,1)S(1)}, bf16[384,256]{1,0:T(8,128)(2,1)}, u32[]{:S(2)}) copy-start(bf16[384,256]{1,0:T(8,128)(2,1)} %get-tuple-element.26) | copy-start | bytes 589828
  75.5 14.7 %copy-start.13 = (bf16[384,256]{1,0:T(8,128)(2,1)S(1)}, bf16[384,256]{1,0:T(8,128)(2,1)}, u32[]{:S(2)}) copy-start(bf16[384,256]{1,0:T(8,128)(2,1)} %get-tuple-element.27) | copy-start | bytes 589828
  75.5 17.5 %copy-start.12 = (bf16[384,256]{1,0:T(8,128)(2,1)S(1)}, bf16[384,256]{1,0:T(8,128)(2,1)}, u32[]{:S(2)}) copy-start(bf16[384,256]{1,0:T(8,128)(2,1)} %get-tuple-element.28) | copy-start | bytes 589828
  75.5 44.5 %copy-start.1 = (bf16[1,2,2,64,1536]{4,3,2,1,0:T(8,128)(2,1)S(1)}, bf16[1,2,2,64,1536]{4,3,2,1,0:T(8,128)(2,1)}, u32[]{:S(2)}) copy-start(bf16[1,2,2,64,1536]{4,3,2,1,0:T(8,128)(2,1)} %param.5) | copy-start | bytes 2359300
  75.5 44.5 %all-to-all-start.2 = ((bf16[96,16,256]{2,1,0:T(8,128)(2,1)}), bf16[96,16,256]{2,1,0:T(8,128)(2,1)S(1)}, u32[]{:S(2)}, u32[]{:S(2)}) async-start(bf16[96,16,256]{2,1,0:T(8,128)(2,1)} %bitcast.16), calls=%async_computation.2 | async-start | bytes 1572864 | tf_op jit(solution)/shard_map/all_to_all | solution.py:169
  85.4 34.6 %copy-start.2 = (bf16[384,256]{1,0:T(8,128)(2,1)S(1)}, bf16[384,256]{1,0:T(8,128)(2,1)}, u32[]{:S(2)}) copy-start(bf16[384,256]{1,0:T(8,128)(2,1)} %get-tuple-element.25.own0) | copy-start | bytes 589828
  85.7 15.1 %collective-permute-start.6 = (bf16[384,256]{1,0:T(8,128)(2,1)S(1)}, bf16[384,256]{1,0:T(8,128)(2,1)S(1)}, u32[]{:S(2)}, u32[]{:S(2)}) collective-permute-start(bf16[384,256]{1,0:T(8,128)(2,1)S(1)} %copy-done.14), channel_id=1, source_target_pairs={{0,576},{192,0},{384,192},{576,384},{1,577},{193,1},{385,193},{577... | collective-permute-start | bytes 589832 | tf_op jit(solution)/shard_map/ppermute | solution.py:21
  90.2 12.3 %collective-permute-start.7 = (bf16[384,256]{1,0:T(8,128)(2,1)S(1)}, bf16[384,256]{1,0:T(8,128)(2,1)S(1)}, u32[]{:S(2)}, u32[]{:S(2)}) collective-permute-start(bf16[384,256]{1,0:T(8,128)(2,1)S(1)} %copy-done.13), channel_id=1, source_target_pairs={{0,384},{192,576},{384,0},{576,192},{1,385},{193,577},{385,1},{577... | collective-permute-start | bytes 589832 | tf_op jit(solution)/shard_map/ppermute | solution.py:21
  93.0 13.8 %collective-permute-start.8 = (bf16[384,256]{1,0:T(8,128)(2,1)S(1)}, bf16[384,256]{1,0:T(8,128)(2,1)S(1)}, u32[]{:S(2)}, u32[]{:S(2)}) collective-permute-start(bf16[384,256]{1,0:T(8,128)(2,1)S(1)} %copy-done.12), channel_id=1, source_target_pairs={{0,192},{192,384},{384,576},{576,0},{1,193},{193,385},{385,577},{5... | collective-permute-start | bytes 589832 | tf_op jit(solution)/shard_map/ppermute | solution.py:21

commit v8 on v7

--- a/solution.py
+++ b/solution.py
@@ -129,7 +129,7 @@
     t1 = passed_along(flat, "x", 1)
     t3 = passed_along(flat, "x", 3)
 
-    pieces = spread(integrals, VIRT, NVIRT)
+    pieces = spread(integrals.reshape(2, -1), VIRT, NVIRT).reshape(NVIRT, width, depth)
     labels_c = lax.dynamic_slice_in_dim(irreps, index * depth, depth)[:, None]
     labels_a = jnp.transpose(irreps.reshape(NVIRT, X, quarter), (1, 0, 2)).reshape(X, NVIRT * quarter)
     early, middle = lanes // 8, lanes * 9 // 16

time: 123 us -> 121 us (0.984)
  the two profiles are of different devices: /device:TPU:64 before, /device:TPU:192 now
where the time goes in v8:
time: 121 us; the launch traced here: 120 us
  starting transfers between devices  61.6 us (51%)
  waiting for transfers between devices  45 us (37%)
  Pallas kernels  8.56 us (7%)
  local copies, waits for them, and re-layouts  4.31 us (4%)
    ppermute x9, starting transfers between devices, passed_along(): return lax.ppermute(value, axis, pairs)  28.2 us
    ppermute x9, waiting for transfers between devices, passed_along(): return lax.ppermute(value, axis, pairs)  18.2 us
    all_to_all x1, starting transfers between devices, spread(): return lax.all_to_all(copies, axis, split_axis=0, concat_axis=0, tiled=True)  16.7 us
    all_to_all x1, waiting for transfers between devices, local(): lax.all_to_all(mirror.reshape(NVIRT * X, quarter, lanes), VIRT + ('x',),...  15.8 us
    all_to_all x1, waiting for transfers between devices, spread(): return lax.all_to_all(copies, axis, split_axis=0, concat_axis=0, tiled=True)  11 us
    all_to_all x1, starting transfers between devices, local(): lax.all_to_all(mirror.reshape(NVIRT * X, quarter, lanes), VIRT + ('x',),...  10.3 us
    all_to_all x1, starting transfers between devices, local(): lax.all_to_all(sent, ('x', 'zl'), split_axis=0, concat_axis=0, tiled=True)  6.36 us
    pallas_call x1, Pallas kernels, local(): pl.pallas_call(cycle_kernel, out_shape=[jax.ShapeDtypeStruct((NVIRT, widt...  5.5 us
  transfers between devices with their start and end apart: 12, of which 7 were waited for; matrix products, arithmetic and copies ran while one was open for 2% of the time, Pallas kernels for 0%

profile of v8, /device:TPU:192, one launch (start us, length us, event | category | flops | bytes accessed | tf_op | source)
XLA Modules:
  0.0 120.0 jit_solution(11945429948748692157)
XLA Ops:
  0.0 3.4 %collective-permute-start = (bf16[256,1536]{1,0:T(8,128)(2,1)}, bf16[256,1536]{1,0:T(8,128)(2,1)S(1)}, u32[]{:S(2)}, u32[]{:S(2)}) collective-permute-start(bf16[256,1536]{1,0:T(8,128)(2,1)} %bitcast.8), channel_id=1, source_target_pairs={{0,192},{192,384},{384,576},{576,0},{1,193},{193,385},{385,577},{5... | collective-permute-start | bytes 2359304 | tf_op jit(solution)/shard_map/ppermute | solution.py:21
  3.4 3.7 %collective-permute-start.1 = (bf16[256,1536]{1,0:T(8,128)(2,1)}, bf16[256,1536]{1,0:T(8,128)(2,1)S(1)}, u32[]{:S(2)}, u32[]{:S(2)}) collective-permute-start(bf16[256,1536]{1,0:T(8,128)(2,1)} %bitcast.9), channel_id=1, source_target_pairs={{0,576},{192,0},{384,192},{576,384},{1,577},{193,1},{385,193},{577... | collective-permute-start | bytes 2359304 | tf_op jit(solution)/shard_map/ppermute | solution.py:21
  7.1 0.8 copy.8
  7.9 0.1 broadcast_in_dim.17
  8.0 0.8 broadcast_in_dim.18
  8.7 16.7 %all-to-all-start = ((bf16[24,2,1536]{2,1,0:T(2,128)(2,1)}), bf16[24,2,1536]{2,1,0:T(2,128)(2,1)S(1)}, u32[]{:S(2)}, u32[]{:S(2)}) async-start(bf16[24,2,1536]{2,1,0:T(2,128)(2,1)} %broadcast_in_dim.18), calls=%async_computation | async-start | bytes 294912 | tf_op jit(solution)/shard_map/all_to_all | solution.py:31
  25.5 0.0 copy-start.5
  25.5 0.7 copy-done.5
  26.2 0.1 reshape.78
  26.3 0.0 collective-permute-done.t1
  26.3 0.0 copy-start.3
  26.3 2.2 %collective-permute-start.2 = (bf16[32,1536]{1,0:T(8,128)(2,1)S(1)}, bf16[32,1536]{1,0:T(8,128)(2,1)S(1)}, u32[]{:S(2)}, u32[]{:S(2)}) collective-permute-start(bf16[32,1536]{1,0:T(8,128)(2,1)S(1)} %slice.12), channel_id=1, source_target_pairs={{0,192},{192,384},{384,576},{576,0},{1,193},{193,385},{385,577},{5... | collective-permute-start | bytes 294920 | tf_op jit(solution)/shard_map/ppermute | solution.py:21
  28.5 0.1 dynamic-slice_bitcast_fusion
  28.6 0.1 copy.9.labels_c
  28.7 0.1 reshape.79.labels_a
  28.8 11.0 %all-to-all-done = bf16[24,2,1536]{2,1,0:T(2,128)(2,1)S(1)} async-done(((bf16[24,2,1536]{2,1,0:T(2,128)(2,1)}), bf16[24,2,1536]{2,1,0:T(2,128)(2,1)S(1)}, u32[]{:S(2)}, u32[]{:S(2)}) %all-to-all-start) | async-done | bytes 147488 | tf_op jit(solution)/shard_map/all_to_all | solution.py:31
  39.8 0.4 reshape.80.pieces
  40.2 0.0 collective-permute-done.1.t3
  40.2 0.0 copy-start.4
  40.2 0.0 collective-permute-done.2.t2a
  40.2 1.1 turn.1
  41.4 6.4 %all-to-all-start.1 = ((bf16[16,48,384]{2,1,0:T(8,128)(2,1)}), bf16[16,48,384]{2,1,0:T(8,128)(2,1)S(1)}, u32[]{:S(2)}, u32[]{:S(2)}) async-start(bf16[16,48,384]{2,1,0:T(8,128)(2,1)} %turn.1), calls=%async_computation.1 | async-start | bytes 1179648 | tf_op jit(solution)/shard_map/all_to_all | solution.py:149
  47.8 3.4 %collective-permute-start.3 = (bf16[112,1536]{1,0:T(8,128)(2,1)S(1)}, bf16[112,1536]{1,0:T(8,128)(2,1)S(1)}, u32[]{:S(2)}, u32[]{:S(2)}) collective-permute-start(bf16[112,1536]{1,0:T(8,128)(2,1)S(1)} %slice.10), channel_id=1, source_target_pairs={{0,192},{192,384},{384,576},{576,0},{1,193},{193,385},{385,577},{5... | collective-permute-start | bytes 1032200 | tf_op jit(solution)/shard_map/ppermute | solution.py:21
  51.2 3.7 %collective-permute-start.4 = (bf16[112,1536]{1,0:T(8,128)(2,1)S(1)}, bf16[112,1536]{1,0:T(8,128)(2,1)S(1)}, u32[]{:S(2)}, u32[]{:S(2)}) collective-permute-start(bf16[112,1536]{1,0:T(8,128)(2,1)S(1)} %slice.11), channel_id=1, source_target_pairs={{0,576},{192,0},{384,192},{576,384},{1,577},{193,1},{385,193},{577... | collective-permute-start | bytes 1032200 | tf_op jit(solution)/shard_map/ppermute | solution.py:21
  54.9 7.7 %collective-permute-done.3.t2b = bf16[112,1536]{1,0:T(8,128)(2,1)S(1)} collective-permute-done((bf16[112,1536]{1,0:T(8,128)(2,1)S(1)}, bf16[112,1536]{1,0:T(8,128)(2,1)S(1)}, u32[]{:S(2)}, u32[]{:S(2)}) %collective-permute-start.3) | collective-permute-done | bytes 344096 | tf_op jit(solution)/shard_map/ppermute | solution.py:21
  62.6 0.0 collective-permute-done.4.t2c
  62.6 0.0 all-to-all-done.1.mine
  62.6 0.0 copy-start.2
  62.6 1.9 %collective-permute-start.5 = (bf16[16,48,384]{2,1,0:T(8,128)(2,1)S(1)}, bf16[16,48,384]{2,1,0:T(8,128)(2,1)S(1)}, u32[]{:S(2)}, u32[]{:S(2)}) collective-permute-start(bf16[16,48,384]{2,1,0:T(8,128)(2,1)S(1)} %all-to-all-done.1.mine), channel_id=1, source_target_pairs={{0,24},{24,0},{1,25},{25,1},{2,26},{26,2},{3,27},{27,3},{4,28},{28... | collective-permute-start | bytes 1769480 | tf_op jit(solution)/shard_map/ppermute | solution.py:21
  64.6 2.0 %collective-permute-done.5.theirs = bf16[16,48,384]{2,1,0:T(8,128)(2,1)S(1)} collective-permute-done((bf16[16,48,384]{2,1,0:T(8,128)(2,1)S(1)}, bf16[16,48,384]{2,1,0:T(8,128)(2,1)S(1)}, u32[]{:S(2)}, u32[]{:S(2)}) %collective-permute-start.5) | collective-permute-done | bytes 589856 | tf_op jit(solution)/shard_map/ppermute | solution.py:21
  66.5 0.0 copy-done.9
  66.5 0.8 copy-done.8
  67.4 5.5 %cycle.1 = (bf16[24,64,256]{2,1,0:T(8,128)(2,1)}, bf16[384,256]{1,0:T(8,128)(2,1)}, bf16[384,256]{1,0:T(8,128)(2,1)}, bf16[384,256]{1,0:T(8,128)(2,1)}, bf16[384,256]{1,0:T(8,128)(2,1)}) custom-call(bf16[16,48,384]{2,1,0:T(8,128)(2,1)} %copy-done.2, bf16[16,48,384]{2,1,0:T(8,128)(2,1)} %copy-done.8, bf16[256,1536]{1,0:T(8,128)(2,1)} %bitcast.10, ...), custom_call_target="tpu_custom_call" | custom-call | flops 1210000000 | bytes 6000000 | tf_op jit(solution)/shard_map/cycle/pallas_call | solution.py:154
  72.9 0.0 copy-start
  72.9 10.3 %all-to-all-start.2 = ((bf16[96,16,256]{2,1,0:T(8,128)(2,1)}), bf16[96,16,256]{2,1,0:T(8,128)(2,1)S(1)}, u32[]{:S(2)}, u32[]{:S(2)}) async-start(bf16[96,16,256]{2,1,0:T(8,128)(2,1)} %bitcast.12), calls=%async_computation.2 | async-start | bytes 1572864 | tf_op jit(solution)/shard_map/all_to_all | solution.py:169
  83.3 0.1 dynamic_slice.15
  83.4 0.1 fusion
  83.4 0.1 broadcast_add_fusion
  83.5 4.5 %collective-permute-start.6 = (bf16[384,256]{1,0:T(8,128)(2,1)S(1)}, bf16[384,256]{1,0:T(8,128)(2,1)S(1)}, u32[]{:S(2)}, u32[]{:S(2)}) collective-permute-start(bf16[384,256]{1,0:T(8,128)(2,1)S(1)} %copy-done.13), channel_id=1, source_target_pairs={{0,576},{192,0},{384,192},{576,384},{1,577},{193,1},{385,193},{577... | collective-permute-start | bytes 589832 | tf_op jit(solution)/shard_map/ppermute | solution.py:21
  88.0 2.8 %collective-permute-start.7 = (bf16[384,256]{1,0:T(8,128)(2,1)S(1)}, bf16[384,256]{1,0:T(8,128)(2,1)S(1)}, u32[]{:S(2)}, u32[]{:S(2)}) collective-permute-start(bf16[384,256]{1,0:T(8,128)(2,1)S(1)} %copy-done.12), channel_id=1, source_target_pairs={{0,384},{192,576},{384,0},{576,192},{1,385},{193,577},{385,1},{577... | collective-permute-start | bytes 589832 | tf_op jit(solution)/shard_map/ppermute | solution.py:21
  90.8 2.8 %collective-permute-start.8 = (bf16[384,256]{1,0:T(8,128)(2,1)S(1)}, bf16[384,256]{1,0:T(8,128)(2,1)S(1)}, u32[]{:S(2)}, u32[]{:S(2)}) collective-permute-start(bf16[384,256]{1,0:T(8,128)(2,1)S(1)} %copy-done.11), channel_id=1, source_target_pairs={{0,192},{192,384},{384,576},{576,0},{1,193},{193,385},{385,577},{5... | collective-permute-start | bytes 589832 | tf_op jit(solution)/shard_map/ppermute | solution.py:21
  93.6 0.1 broadcast_subtract_fusion
  93.6 0.1 sub.27.row_term
  93.8 4.1 %collective-permute-done.6.own1 = bf16[384,256]{1,0:T(8,128)(2,1)S(1)} collective-permute-done((bf16[384,256]{1,0:T(8,128)(2,1)S(1)}, bf16[384,256]{1,0:T(8,128)(2,1)S(1)}, u32[]{:S(2)}, u32[]{:S(2)}) %collective-permute-start.6) | collective-permute-done | bytes 196640 | tf_op jit(solution)/shard_map/ppermute | solution.py:21
  97.9 2.0 %collective-permute-done.7.own2 = bf16[384,256]{1,0:T(8,128)(2,1)S(1)} collective-permute-done((bf16[384,256]{1,0:T(8,128)(2,1)S(1)}, bf16[384,256]{1,0:T(8,128)(2,1)S(1)}, u32[]{:S(2)}, u32[]{:S(2)}) %collective-permute-start.7) | collective-permute-done | bytes 196640 | tf_op jit(solution)/shard_map/ppermute | solution.py:21
  99.9 2.4 %collective-permute-done.8.own3 = bf16[384,256]{1,0:T(8,128)(2,1)S(1)} collective-permute-done((bf16[384,256]{1,0:T(8,128)(2,1)S(1)}, bf16[384,256]{1,0:T(8,128)(2,1)S(1)}, u32[]{:S(2)}, u32[]{:S(2)}) %collective-permute-start.8) | collective-permute-done | bytes 196640 | tf_op jit(solution)/shard_map/ppermute | solution.py:21
  102.3 15.8 %all-to-all-done.2 = bf16[96,16,256]{2,1,0:T(8,128)(2,1)S(1)} async-done(((bf16[96,16,256]{2,1,0:T(8,128)(2,1)}), bf16[96,16,256]{2,1,0:T(8,128)(2,1)S(1)}, u32[]{:S(2)}, u32[]{:S(2)}) %all-to-all-start.2) | async-done | bytes 786464 | tf_op jit(solution)/shard_map/all_to_all | solution.py:169
  118.1 1.9 %finish.1 = bf16[256,1536]{1,0:T(8,128)(2,1)} custom-call(bf16[24,64,256]{2,1,0:T(8,128)(2,1)S(1)} %bitcast.7, bf16[384,256]{1,0:T(8,128)(2,1)S(1)} %copy-done.1, bf16[384,256]{1,0:T(8,128)(2,1)S(1)} %collective-permute-done.6.own1, bf16[384,256]{1,0:T(8,128)(2,1)S(1)} %collective-permute-done.7.own2, bf16[384,256]{1,0:T(8,128)(2,1)S(1)} %collective-permute-done.8.own3, ...), custom_call_target="tpu_custom_call" | custom-call | flops 600000000 | bytes 4000000 | tf_op jit(solution)/shard_map/finish/pallas_call | solution.py:181
  (27 shorter events, 0.1 us)
Async XLA Ops:
  0.0 26.3 %collective-permute-start = (bf16[256,1536]{1,0:T(8,128)(2,1)}, bf16[256,1536]{1,0:T(8,128)(2,1)S(1)}, u32[]{:S(2)}, u32[]{:S(2)}) collective-permute-start(bf16[256,1536]{1,0:T(8,128)(2,1)} %bitcast.8), channel_id=1, source_target_pairs={{0,192},{192,384},{384,576},{576,0},{1,193},{193,385},{385,577},{5... | collective-permute-start | bytes 2359304 | tf_op jit(solution)/shard_map/ppermute | solution.py:21
  3.4 36.8 %collective-permute-start.1 = (bf16[256,1536]{1,0:T(8,128)(2,1)}, bf16[256,1536]{1,0:T(8,128)(2,1)S(1)}, u32[]{:S(2)}, u32[]{:S(2)}) collective-permute-start(bf16[256,1536]{1,0:T(8,128)(2,1)} %bitcast.9), channel_id=1, source_target_pairs={{0,576},{192,0},{384,192},{576,384},{1,577},{193,1},{385,193},{577... | collective-permute-start | bytes 2359304 | tf_op jit(solution)/shard_map/ppermute | solution.py:21
  8.7 31.1 %all-to-all-start = ((bf16[24,2,1536]{2,1,0:T(2,128)(2,1)}), bf16[24,2,1536]{2,1,0:T(2,128)(2,1)S(1)}, u32[]{:S(2)}, u32[]{:S(2)}) async-start(bf16[24,2,1536]{2,1,0:T(2,128)(2,1)} %broadcast_in_dim.18), calls=%async_computation | async-start | bytes 294912 | tf_op jit(solution)/shard_map/all_to_all | solution.py:31
  25.5 0.7 copy-start.5
  26.3 21.5 %copy-start.3 = (bf16[256,1536]{1,0:T(8,128)(2,1)}, bf16[256,1536]{1,0:T(8,128)(2,1)S(1)}, u32[]{:S(2)}) copy-start(bf16[256,1536]{1,0:T(8,128)(2,1)S(1)} %collective-permute-done.t1) | copy-start | bytes 2359300
  26.3 13.9 %collective-permute-start.2 = (bf16[32,1536]{1,0:T(8,128)(2,1)S(1)}, bf16[32,1536]{1,0:T(8,128)(2,1)S(1)}, u32[]{:S(2)}, u32[]{:S(2)}) collective-permute-start(bf16[32,1536]{1,0:T(8,128)(2,1)S(1)} %slice.12), channel_id=1, source_target_pairs={{0,192},{192,384},{384,576},{576,0},{1,193},{193,385},{385,577},{5... | collective-permute-start | bytes 294920 | tf_op jit(solution)/shard_map/ppermute | solution.py:21
  40.2 11.0 %copy-start.4 = (bf16[256,1536]{1,0:T(8,128)(2,1)}, bf16[256,1536]{1,0:T(8,128)(2,1)S(1)}, u32[]{:S(2)}) copy-start(bf16[256,1536]{1,0:T(8,128)(2,1)S(1)} %collective-permute-done.1.t3) | copy-start | bytes 2359300
  40.2 1.1 copy-start.14
  41.4 21.2 %all-to-all-start.1 = ((bf16[16,48,384]{2,1,0:T(8,128)(2,1)}), bf16[16,48,384]{2,1,0:T(8,128)(2,1)S(1)}, u32[]{:S(2)}, u32[]{:S(2)}) async-start(bf16[16,48,384]{2,1,0:T(8,128)(2,1)} %turn.1), calls=%async_computation.1 | async-start | bytes 1179648 | tf_op jit(solution)/shard_map/all_to_all | solution.py:149
  47.8 14.8 %collective-permute-start.3 = (bf16[112,1536]{1,0:T(8,128)(2,1)S(1)}, bf16[112,1536]{1,0:T(8,128)(2,1)S(1)}, u32[]{:S(2)}, u32[]{:S(2)}) collective-permute-start(bf16[112,1536]{1,0:T(8,128)(2,1)S(1)} %slice.10), channel_id=1, source_target_pairs={{0,192},{192,384},{384,576},{576,0},{1,193},{193,385},{385,577},{5... | collective-permute-start | bytes 1032200 | tf_op jit(solution)/shard_map/ppermute | solution.py:21
  51.2 11.4 %collective-permute-start.4 = (bf16[112,1536]{1,0:T(8,128)(2,1)S(1)}, bf16[112,1536]{1,0:T(8,128)(2,1)S(1)}, u32[]{:S(2)}, u32[]{:S(2)}) collective-permute-start(bf16[112,1536]{1,0:T(8,128)(2,1)S(1)} %slice.11), channel_id=1, source_target_pairs={{0,576},{192,0},{384,192},{576,384},{1,577},{193,1},{385,193},{577... | collective-permute-start | bytes 1032200 | tf_op jit(solution)/shard_map/ppermute | solution.py:21
  62.6 3.9 %copy-start.9 = (bf16[112,1536]{1,0:T(8,128)(2,1)}, bf16[112,1536]{1,0:T(8,128)(2,1)S(1)}, u32[]{:S(2)}) copy-start(bf16[112,1536]{1,0:T(8,128)(2,1)S(1)} %collective-permute-done.3.t2b) | copy-start | bytes 1032196
  62.6 3.9 %copy-start.10 = (bf16[112,1536]{1,0:T(8,128)(2,1)}, bf16[112,1536]{1,0:T(8,128)(2,1)S(1)}, u32[]{:S(2)}) copy-start(bf16[112,1536]{1,0:T(8,128)(2,1)S(1)} %collective-permute-done.4.t2c) | copy-start | bytes 1032196
  62.6 3.9 %copy-start.2 = (bf16[16,48,384]{2,1,0:T(8,128)(2,1)}, bf16[16,48,384]{2,1,0:T(8,128)(2,1)S(1)}, u32[]{:S(2)}) copy-start(bf16[16,48,384]{2,1,0:T(8,128)(2,1)S(1)} %all-to-all-done.1.mine) | copy-start | bytes 1769476
  62.6 3.9 %collective-permute-start.5 = (bf16[16,48,384]{2,1,0:T(8,128)(2,1)S(1)}, bf16[16,48,384]{2,1,0:T(8,128)(2,1)S(1)}, u32[]{:S(2)}, u32[]{:S(2)}) collective-permute-start(bf16[16,48,384]{2,1,0:T(8,128)(2,1)S(1)} %all-to-all-done.1.mine), channel_id=1, source_target_pairs={{0,24},{24,0},{1,25},{25,1},{2,26},{26,2},{3,27},{27,3},{4,28},{28... | collective-permute-start | bytes 1769480 | tf_op jit(solution)/shard_map/ppermute | solution.py:21
  66.5 0.8 copy-start.8
  72.9 10.4 %copy-start.6 = (f32[1536]{0:T(1024)S(1)}, f32[1536]{0:T(1024)}, u32[]{:S(2)}) copy-start(f32[1536]{0:T(1024)} %param.9) | copy-start | bytes 18436
  72.9 10.5 %copy-start.7 = (f32[64]{0:T(128)S(1)}, f32[64]{0:T(128)}, u32[]{:S(2)}) copy-start(f32[64]{0:T(128)} %param.8) | copy-start | bytes 772
  72.9 10.7 %copy-start.13 = (bf16[384,256]{1,0:T(8,128)(2,1)S(1)}, bf16[384,256]{1,0:T(8,128)(2,1)}, u32[]{:S(2)}) copy-start(bf16[384,256]{1,0:T(8,128)(2,1)} %get-tuple-element.26) | copy-start | bytes 589828
  72.9 15.1 %copy-start.12 = (bf16[384,256]{1,0:T(8,128)(2,1)S(1)}, bf16[384,256]{1,0:T(8,128)(2,1)}, u32[]{:S(2)}) copy-start(bf16[384,256]{1,0:T(8,128)(2,1)} %get-tuple-element.27) | copy-start | bytes 589828
  72.9 17.9 %copy-start.11 = (bf16[384,256]{1,0:T(8,128)(2,1)S(1)}, bf16[384,256]{1,0:T(8,128)(2,1)}, u32[]{:S(2)}) copy-start(bf16[384,256]{1,0:T(8,128)(2,1)} %get-tuple-element.28) | copy-start | bytes 589828
  72.9 45.2 %copy-start = (bf16[1,2,2,64,1536]{4,3,2,1,0:T(8,128)(2,1)S(1)}, bf16[1,2,2,64,1536]{4,3,2,1,0:T(8,128)(2,1)}, u32[]{:S(2)}) copy-start(bf16[1,2,2,64,1536]{4,3,2,1,0:T(8,128)(2,1)} %param.5) | copy-start | bytes 2359300
  72.9 45.2 %all-to-all-start.2 = ((bf16[96,16,256]{2,1,0:T(8,128)(2,1)}), bf16[96,16,256]{2,1,0:T(8,128)(2,1)S(1)}, u32[]{:S(2)}, u32[]{:S(2)}) async-start(bf16[96,16,256]{2,1,0:T(8,128)(2,1)} %bitcast.12), calls=%async_computation.2 | async-start | bytes 1572864 | tf_op jit(solution)/shard_map/all_to_all | solution.py:169
  83.2 34.9 %copy-start.1 = (bf16[384,256]{1,0:T(8,128)(2,1)S(1)}, bf16[384,256]{1,0:T(8,128)(2,1)}, u32[]{:S(2)}) copy-start(bf16[384,256]{1,0:T(8,128)(2,1)} %get-tuple-element.25.own0) | copy-start | bytes 589828
  83.5 14.4 %collective-permute-start.6 = (bf16[384,256]{1,0:T(8,128)(2,1)S(1)}, bf16[384,256]{1,0:T(8,128)(2,1)S(1)}, u32[]{:S(2)}, u32[]{:S(2)}) collective-permute-start(bf16[384,256]{1,0:T(8,128)(2,1)S(1)} %copy-done.13), channel_id=1, source_target_pairs={{0,576},{192,0},{384,192},{576,384},{1,577},{193,1},{385,193},{577... | collective-permute-start | bytes 589832 | tf_op jit(solution)/shard_map/ppermute | solution.py:21
  88.0 11.9 %collective-permute-start.7 = (bf16[384,256]{1,0:T(8,128)(2,1)S(1)}, bf16[384,256]{1,0:T(8,128)(2,1)S(1)}, u32[]{:S(2)}, u32[]{:S(2)}) collective-permute-start(bf16[384,256]{1,0:T(8,128)(2,1)S(1)} %copy-done.12), channel_id=1, source_target_pairs={{0,384},{192,576},{384,0},{576,192},{1,385},{193,577},{385,1},{577... | collective-permute-start | bytes 589832 | tf_op jit(solution)/shard_map/ppermute | solution.py:21
  90.8 11.5 %collective-permute-start.8 = (bf16[384,256]{1,0:T(8,128)(2,1)S(1)}, bf16[384,256]{1,0:T(8,128)(2,1)S(1)}, u32[]{:S(2)}, u32[]{:S(2)}) collective-permute-start(bf16[384,256]{1,0:T(8,128)(2,1)S(1)} %copy-done.11), channel_id=1, source_target_pairs={{0,192},{192,384},{384,576},{576,0},{1,193},{193,385},{385,577},{5... | collective-permute-start | bytes 589832 | tf_op jit(solution)/shard_map/ppermute | solution.py:21

commit v9 on v8

--- a/solution.py
+++ b/solution.py
@@ -129,7 +129,7 @@
     t1 = passed_along(flat, "x", 1)
     t3 = passed_along(flat, "x", 3)
 
-    pieces = spread(integrals.reshape(2, -1), VIRT, NVIRT).reshape(NVIRT, width, depth)
+    pieces = spread(integrals.reshape(-1, 128), VIRT, NVIRT).reshape(NVIRT, width, depth)
     labels_c = lax.dynamic_slice_in_dim(irreps, index * depth, depth)[:, None]
     labels_a = jnp.transpose(irreps.reshape(NVIRT, X, quarter), (1, 0, 2)).reshape(X, NVIRT * quarter)
     early, middle = lanes // 8, lanes * 9 // 16

time: 121 us -> 121 us (level)
  the two profiles are of different devices: /device:TPU:192 before, /device:TPU:72 now
where the time goes in v9:
time: 121 us; the launch traced here: 120 us
  starting transfers between devices  63.2 us (52%)
  waiting for transfers between devices  44 us (36%)
  Pallas kernels  8.57 us (7%)
  local copies, waits for them, and re-layouts  4.22 us (3%)
    ppermute x9, starting transfers between devices, passed_along(): return lax.ppermute(value, axis, pairs)  28.3 us
    ppermute x9, waiting for transfers between devices, passed_along(): return lax.ppermute(value, axis, pairs)  23.1 us
    all_to_all x1, starting transfers between devices, spread(): return lax.all_to_all(copies, axis, split_axis=0, concat_axis=0, tiled=True)  18.8 us
    all_to_all x1, waiting for transfers between devices, local(): lax.all_to_all(mirror.reshape(NVIRT * X, quarter, lanes), VIRT + ('x',),...  11.9 us
    all_to_all x1, waiting for transfers between devices, spread(): return lax.all_to_all(copies, axis, split_axis=0, concat_axis=0, tiled=True)  9.01 us
    all_to_all x1, starting transfers between devices, local(): lax.all_to_all(mirror.reshape(NVIRT * X, quarter, lanes), VIRT + ('x',),...  8.85 us
    all_to_all x1, starting transfers between devices, local(): lax.all_to_all(sent, ('x', 'zl'), split_axis=0, concat_axis=0, tiled=True)  7.27 us
    pallas_call x1, Pallas kernels, local(): pl.pallas_call(cycle_kernel, out_shape=[jax.ShapeDtypeStruct((NVIRT, widt...  5.5 us
  transfers between devices with their start and end apart: 12, of which 7 were waited for; matrix products, arithmetic and copies ran while one was open for 2% of the time, Pallas kernels for 0%

profile of v9, /device:TPU:72, one launch (start us, length us, event | category | flops | bytes accessed | tf_op | source)
XLA Modules:
  0.0 120.5 jit_solution(12063795833239641721)
XLA Ops:
  0.0 3.4 %collective-permute-start = (bf16[256,1536]{1,0:T(8,128)(2,1)}, bf16[256,1536]{1,0:T(8,128)(2,1)S(1)}, u32[]{:S(2)}, u32[]{:S(2)}) collective-permute-start(bf16[256,1536]{1,0:T(8,128)(2,1)} %bitcast.8), channel_id=1, source_target_pairs={{0,192},{192,384},{384,576},{576,0},{1,193},{193,385},{385,577},{5... | collective-permute-start | bytes 2359304 | tf_op jit(solution)/shard_map/ppermute | solution.py:21
  3.4 3.7 %collective-permute-start.1 = (bf16[256,1536]{1,0:T(8,128)(2,1)}, bf16[256,1536]{1,0:T(8,128)(2,1)S(1)}, u32[]{:S(2)}, u32[]{:S(2)}) collective-permute-start(bf16[256,1536]{1,0:T(8,128)(2,1)} %bitcast.9), channel_id=1, source_target_pairs={{0,576},{192,0},{384,192},{576,384},{1,577},{193,1},{385,193},{577... | collective-permute-start | bytes 2359304 | tf_op jit(solution)/shard_map/ppermute | solution.py:21
  7.1 0.8 copy.8
  7.9 0.1 broadcast_in_dim.17
  7.9 0.7 broadcast_in_dim.18
  8.7 18.8 %all-to-all-start = ((bf16[24,24,128]{2,1,0:T(8,128)(2,1)}), bf16[24,24,128]{2,1,0:T(8,128)(2,1)S(1)}, u32[]{:S(2)}, u32[]{:S(2)}) async-start(bf16[24,24,128]{2,1,0:T(8,128)(2,1)} %broadcast_in_dim.18), calls=%async_computation | async-start | bytes 294912 | tf_op jit(solution)/shard_map/all_to_all | solution.py:31
  27.5 0.0 copy-start.5
  27.5 0.7 copy-done.5
  28.2 0.1 reshape.78
  28.3 0.0 collective-permute-done.t1
  28.3 0.0 copy-start.3
  28.3 2.2 %collective-permute-start.2 = (bf16[32,1536]{1,0:T(8,128)(2,1)S(1)}, bf16[32,1536]{1,0:T(8,128)(2,1)S(1)}, u32[]{:S(2)}, u32[]{:S(2)}) collective-permute-start(bf16[32,1536]{1,0:T(8,128)(2,1)S(1)} %slice.12), channel_id=1, source_target_pairs={{0,192},{192,384},{384,576},{576,0},{1,193},{193,385},{385,577},{5... | collective-permute-start | bytes 294920 | tf_op jit(solution)/shard_map/ppermute | solution.py:21
  30.5 0.1 dynamic-slice_bitcast_fusion
  30.6 0.1 copy.9.labels_c
  30.7 0.1 reshape.79.labels_a
  30.8 9.0 %all-to-all-done = bf16[24,24,128]{2,1,0:T(8,128)(2,1)S(1)} async-done(((bf16[24,24,128]{2,1,0:T(8,128)(2,1)}), bf16[24,24,128]{2,1,0:T(8,128)(2,1)S(1)}, u32[]{:S(2)}, u32[]{:S(2)}) %all-to-all-start) | async-done | bytes 147488 | tf_op jit(solution)/shard_map/all_to_all | solution.py:31
  39.8 0.3 reshape.80.pieces
  40.1 0.0 collective-permute-done.1.t3
  40.1 0.0 copy-start.4
  40.2 0.0 collective-permute-done.2.t2a
  40.2 1.1 turn.1
  41.3 7.3 %all-to-all-start.1 = ((bf16[16,48,384]{2,1,0:T(8,128)(2,1)}), bf16[16,48,384]{2,1,0:T(8,128)(2,1)S(1)}, u32[]{:S(2)}, u32[]{:S(2)}) async-start(bf16[16,48,384]{2,1,0:T(8,128)(2,1)} %turn.1), calls=%async_computation.1 | async-start | bytes 1179648 | tf_op jit(solution)/shard_map/all_to_all | solution.py:149
  48.6 3.4 %collective-permute-start.3 = (bf16[112,1536]{1,0:T(8,128)(2,1)S(1)}, bf16[112,1536]{1,0:T(8,128)(2,1)S(1)}, u32[]{:S(2)}, u32[]{:S(2)}) collective-permute-start(bf16[112,1536]{1,0:T(8,128)(2,1)S(1)} %slice.10), channel_id=1, source_target_pairs={{0,192},{192,384},{384,576},{576,0},{1,193},{193,385},{385,577},{5... | collective-permute-start | bytes 1032200 | tf_op jit(solution)/shard_map/ppermute | solution.py:21
  52.1 3.7 %collective-permute-start.4 = (bf16[112,1536]{1,0:T(8,128)(2,1)S(1)}, bf16[112,1536]{1,0:T(8,128)(2,1)S(1)}, u32[]{:S(2)}, u32[]{:S(2)}) collective-permute-start(bf16[112,1536]{1,0:T(8,128)(2,1)S(1)} %slice.11), channel_id=1, source_target_pairs={{0,576},{192,0},{384,192},{576,384},{1,577},{193,1},{385,193},{577... | collective-permute-start | bytes 1032200 | tf_op jit(solution)/shard_map/ppermute | solution.py:21
  55.7 9.9 %collective-permute-done.3.t2b = bf16[112,1536]{1,0:T(8,128)(2,1)S(1)} collective-permute-done((bf16[112,1536]{1,0:T(8,128)(2,1)S(1)}, bf16[112,1536]{1,0:T(8,128)(2,1)S(1)}, u32[]{:S(2)}, u32[]{:S(2)}) %collective-permute-start.3) | collective-permute-done | bytes 344096 | tf_op jit(solution)/shard_map/ppermute | solution.py:21
  65.6 0.0 collective-permute-done.4.t2c
  65.6 0.0 all-to-all-done.1.mine
  65.6 1.9 %collective-permute-start.5 = (bf16[16,48,384]{2,1,0:T(8,128)(2,1)S(1)}, bf16[16,48,384]{2,1,0:T(8,128)(2,1)S(1)}, u32[]{:S(2)}, u32[]{:S(2)}) collective-permute-start(bf16[16,48,384]{2,1,0:T(8,128)(2,1)S(1)} %all-to-all-done.1.mine), channel_id=1, source_target_pairs={{0,24},{24,0},{1,25},{25,1},{2,26},{26,2},{3,27},{27,3},{4,28},{28... | collective-permute-start | bytes 1769480 | tf_op jit(solution)/shard_map/ppermute | solution.py:21
  67.5 2.0 %collective-permute-done.5.theirs = bf16[16,48,384]{2,1,0:T(8,128)(2,1)S(1)} collective-permute-done((bf16[16,48,384]{2,1,0:T(8,128)(2,1)S(1)}, bf16[16,48,384]{2,1,0:T(8,128)(2,1)S(1)}, u32[]{:S(2)}, u32[]{:S(2)}) %collective-permute-start.5) | collective-permute-done | bytes 589856 | tf_op jit(solution)/shard_map/ppermute | solution.py:21
  69.5 0.0 copy-done.2
  69.5 0.0 copy-start.8
  69.5 0.8 copy-done.8
  70.4 5.5 %cycle.1 = (bf16[24,64,256]{2,1,0:T(8,128)(2,1)}, bf16[384,256]{1,0:T(8,128)(2,1)}, bf16[384,256]{1,0:T(8,128)(2,1)}, bf16[384,256]{1,0:T(8,128)(2,1)}, bf16[384,256]{1,0:T(8,128)(2,1)}) custom-call(bf16[16,48,384]{2,1,0:T(8,128)(2,1)} %copy-done.2, bf16[16,48,384]{2,1,0:T(8,128)(2,1)} %copy-done.8, bf16[256,1536]{1,0:T(8,128)(2,1)} %bitcast.10, ...), custom_call_target="tpu_custom_call" | custom-call | flops 1210000000 | bytes 6000000 | tf_op jit(solution)/shard_map/cycle/pallas_call | solution.py:154
  75.9 0.0 copy-start
  75.9 8.8 %all-to-all-start.2 = ((bf16[96,16,256]{2,1,0:T(8,128)(2,1)}), bf16[96,16,256]{2,1,0:T(8,128)(2,1)S(1)}, u32[]{:S(2)}, u32[]{:S(2)}) async-start(bf16[96,16,256]{2,1,0:T(8,128)(2,1)} %bitcast.12), calls=%async_computation.2 | async-start | bytes 1572864 | tf_op jit(solution)/shard_map/all_to_all | solution.py:169
  84.8 0.1 dynamic_slice.15
  84.9 0.1 fusion
  85.0 0.1 broadcast_add_fusion
  85.1 4.6 %collective-permute-start.6 = (bf16[384,256]{1,0:T(8,128)(2,1)S(1)}, bf16[384,256]{1,0:T(8,128)(2,1)S(1)}, u32[]{:S(2)}, u32[]{:S(2)}) collective-permute-start(bf16[384,256]{1,0:T(8,128)(2,1)S(1)} %copy-done.13), channel_id=1, source_target_pairs={{0,576},{192,0},{384,192},{576,384},{1,577},{193,1},{385,193},{577... | collective-permute-start | bytes 589832 | tf_op jit(solution)/shard_map/ppermute | solution.py:21
  89.6 2.8 %collective-permute-start.7 = (bf16[384,256]{1,0:T(8,128)(2,1)S(1)}, bf16[384,256]{1,0:T(8,128)(2,1)S(1)}, u32[]{:S(2)}, u32[]{:S(2)}) collective-permute-start(bf16[384,256]{1,0:T(8,128)(2,1)S(1)} %copy-done.12), channel_id=1, source_target_pairs={{0,384},{192,576},{384,0},{576,192},{1,385},{193,577},{385,1},{577... | collective-permute-start | bytes 589832 | tf_op jit(solution)/shard_map/ppermute | solution.py:21
  92.4 2.8 %collective-permute-start.8 = (bf16[384,256]{1,0:T(8,128)(2,1)S(1)}, bf16[384,256]{1,0:T(8,128)(2,1)S(1)}, u32[]{:S(2)}, u32[]{:S(2)}) collective-permute-start(bf16[384,256]{1,0:T(8,128)(2,1)S(1)} %copy-done.11), channel_id=1, source_target_pairs={{0,192},{192,384},{384,576},{576,0},{1,193},{193,385},{385,577},{5... | collective-permute-start | bytes 589832 | tf_op jit(solution)/shard_map/ppermute | solution.py:21
  95.2 0.1 broadcast_subtract_fusion
  95.3 0.1 sub.27.row_term
  95.4 5.3 %collective-permute-done.6.own1 = bf16[384,256]{1,0:T(8,128)(2,1)S(1)} collective-permute-done((bf16[384,256]{1,0:T(8,128)(2,1)S(1)}, bf16[384,256]{1,0:T(8,128)(2,1)S(1)}, u32[]{:S(2)}, u32[]{:S(2)}) %collective-permute-start.6) | collective-permute-done | bytes 196640 | tf_op jit(solution)/shard_map/ppermute | solution.py:21
  100.7 1.8 %collective-permute-done.7.own2 = bf16[384,256]{1,0:T(8,128)(2,1)S(1)} collective-permute-done((bf16[384,256]{1,0:T(8,128)(2,1)S(1)}, bf16[384,256]{1,0:T(8,128)(2,1)S(1)}, u32[]{:S(2)}, u32[]{:S(2)}) %collective-permute-start.7) | collective-permute-done | bytes 196640 | tf_op jit(solution)/shard_map/ppermute | solution.py:21
  102.5 4.1 %collective-permute-done.8.own3 = bf16[384,256]{1,0:T(8,128)(2,1)S(1)} collective-permute-done((bf16[384,256]{1,0:T(8,128)(2,1)S(1)}, bf16[384,256]{1,0:T(8,128)(2,1)S(1)}, u32[]{:S(2)}, u32[]{:S(2)}) %collective-permute-start.8) | collective-permute-done | bytes 196640 | tf_op jit(solution)/shard_map/ppermute | solution.py:21
  106.6 11.9 %all-to-all-done.2 = bf16[96,16,256]{2,1,0:T(8,128)(2,1)S(1)} async-done(((bf16[96,16,256]{2,1,0:T(8,128)(2,1)}), bf16[96,16,256]{2,1,0:T(8,128)(2,1)S(1)}, u32[]{:S(2)}, u32[]{:S(2)}) %all-to-all-start.2) | async-done | bytes 786464 | tf_op jit(solution)/shard_map/all_to_all | solution.py:169
  118.6 1.9 %finish.1 = bf16[256,1536]{1,0:T(8,128)(2,1)} custom-call(bf16[24,64,256]{2,1,0:T(8,128)(2,1)S(1)} %bitcast.7, bf16[384,256]{1,0:T(8,128)(2,1)S(1)} %copy-done.1, bf16[384,256]{1,0:T(8,128)(2,1)S(1)} %collective-permute-done.6.own1, bf16[384,256]{1,0:T(8,128)(2,1)S(1)} %collective-permute-done.7.own2, bf16[384,256]{1,0:T(8,128)(2,1)S(1)} %collective-permute-done.8.own3, ...), custom_call_target="tpu_custom_call" | custom-call | flops 600000000 | bytes 4000000 | tf_op jit(solution)/shard_map/finish/pallas_call | solution.py:181
  (27 shorter events, 0.1 us)
Async XLA Ops:
  0.0 28.3 %collective-permute-start = (bf16[256,1536]{1,0:T(8,128)(2,1)}, bf16[256,1536]{1,0:T(8,128)(2,1)S(1)}, u32[]{:S(2)}, u32[]{:S(2)}) collective-permute-start(bf16[256,1536]{1,0:T(8,128)(2,1)} %bitcast.8), channel_id=1, source_target_pairs={{0,192},{192,384},{384,576},{576,0},{1,193},{193,385},{385,577},{5... | collective-permute-start | bytes 2359304 | tf_op jit(solution)/shard_map/ppermute | solution.py:21
  3.4 36.7 %collective-permute-start.1 = (bf16[256,1536]{1,0:T(8,128)(2,1)}, bf16[256,1536]{1,0:T(8,128)(2,1)S(1)}, u32[]{:S(2)}, u32[]{:S(2)}) collective-permute-start(bf16[256,1536]{1,0:T(8,128)(2,1)} %bitcast.9), channel_id=1, source_target_pairs={{0,576},{192,0},{384,192},{576,384},{1,577},{193,1},{385,193},{577... | collective-permute-start | bytes 2359304 | tf_op jit(solution)/shard_map/ppermute | solution.py:21
  8.7 31.1 %all-to-all-start = ((bf16[24,24,128]{2,1,0:T(8,128)(2,1)}), bf16[24,24,128]{2,1,0:T(8,128)(2,1)S(1)}, u32[]{:S(2)}, u32[]{:S(2)}) async-start(bf16[24,24,128]{2,1,0:T(8,128)(2,1)} %broadcast_in_dim.18), calls=%async_computation | async-start | bytes 294912 | tf_op jit(solution)/shard_map/all_to_all | solution.py:31
  27.5 0.7 copy-start.5
  28.3 20.3 %copy-start.3 = (bf16[256,1536]{1,0:T(8,128)(2,1)}, bf16[256,1536]{1,0:T(8,128)(2,1)S(1)}, u32[]{:S(2)}) copy-start(bf16[256,1536]{1,0:T(8,128)(2,1)S(1)} %collective-permute-done.t1) | copy-start | bytes 2359300
  28.3 11.9 %collective-permute-start.2 = (bf16[32,1536]{1,0:T(8,128)(2,1)S(1)}, bf16[32,1536]{1,0:T(8,128)(2,1)S(1)}, u32[]{:S(2)}, u32[]{:S(2)}) collective-permute-start(bf16[32,1536]{1,0:T(8,128)(2,1)S(1)} %slice.12), channel_id=1, source_target_pairs={{0,192},{192,384},{384,576},{576,0},{1,193},{193,385},{385,577},{5... | collective-permute-start | bytes 294920 | tf_op jit(solution)/shard_map/ppermute | solution.py:21
  40.1 11.9 %copy-start.4 = (bf16[256,1536]{1,0:T(8,128)(2,1)}, bf16[256,1536]{1,0:T(8,128)(2,1)S(1)}, u32[]{:S(2)}) copy-start(bf16[256,1536]{1,0:T(8,128)(2,1)S(1)} %collective-permute-done.1.t3) | copy-start | bytes 2359300
  40.2 1.1 copy-start.14
  41.3 24.3 %all-to-all-start.1 = ((bf16[16,48,384]{2,1,0:T(8,128)(2,1)}), bf16[16,48,384]{2,1,0:T(8,128)(2,1)S(1)}, u32[]{:S(2)}, u32[]{:S(2)}) async-start(bf16[16,48,384]{2,1,0:T(8,128)(2,1)} %turn.1), calls=%async_computation.1 | async-start | bytes 1179648 | tf_op jit(solution)/shard_map/all_to_all | solution.py:149
  48.6 17.0 %collective-permute-start.3 = (bf16[112,1536]{1,0:T(8,128)(2,1)S(1)}, bf16[112,1536]{1,0:T(8,128)(2,1)S(1)}, u32[]{:S(2)}, u32[]{:S(2)}) collective-permute-start(bf16[112,1536]{1,0:T(8,128)(2,1)S(1)} %slice.10), channel_id=1, source_target_pairs={{0,192},{192,384},{384,576},{576,0},{1,193},{193,385},{385,577},{5... | collective-permute-start | bytes 1032200 | tf_op jit(solution)/shard_map/ppermute | solution.py:21
  52.1 13.5 %collective-permute-start.4 = (bf16[112,1536]{1,0:T(8,128)(2,1)S(1)}, bf16[112,1536]{1,0:T(8,128)(2,1)S(1)}, u32[]{:S(2)}, u32[]{:S(2)}) collective-permute-start(bf16[112,1536]{1,0:T(8,128)(2,1)S(1)} %slice.11), channel_id=1, source_target_pairs={{0,576},{192,0},{384,192},{576,384},{1,577},{193,1},{385,193},{577... | collective-permute-start | bytes 1032200 | tf_op jit(solution)/shard_map/ppermute | solution.py:21
  65.6 3.9 %copy-start.9 = (bf16[112,1536]{1,0:T(8,128)(2,1)}, bf16[112,1536]{1,0:T(8,128)(2,1)S(1)}, u32[]{:S(2)}) copy-start(bf16[112,1536]{1,0:T(8,128)(2,1)S(1)} %collective-permute-done.3.t2b) | copy-start | bytes 1032196
  65.6 3.9 %copy-start.10 = (bf16[112,1536]{1,0:T(8,128)(2,1)}, bf16[112,1536]{1,0:T(8,128)(2,1)S(1)}, u32[]{:S(2)}) copy-start(bf16[112,1536]{1,0:T(8,128)(2,1)S(1)} %collective-permute-done.4.t2c) | copy-start | bytes 1032196
  65.6 3.9 %copy-start.2 = (bf16[16,48,384]{2,1,0:T(8,128)(2,1)}, bf16[16,48,384]{2,1,0:T(8,128)(2,1)S(1)}, u32[]{:S(2)}) copy-start(bf16[16,48,384]{2,1,0:T(8,128)(2,1)S(1)} %all-to-all-done.1.mine) | copy-start | bytes 1769476
  65.6 3.9 %collective-permute-start.5 = (bf16[16,48,384]{2,1,0:T(8,128)(2,1)S(1)}, bf16[16,48,384]{2,1,0:T(8,128)(2,1)S(1)}, u32[]{:S(2)}, u32[]{:S(2)}) collective-permute-start(bf16[16,48,384]{2,1,0:T(8,128)(2,1)S(1)} %all-to-all-done.1.mine), channel_id=1, source_target_pairs={{0,24},{24,0},{1,25},{25,1},{2,26},{26,2},{3,27},{27,3},{4,28},{28... | collective-permute-start | bytes 1769480 | tf_op jit(solution)/shard_map/ppermute | solution.py:21
  69.5 0.8 copy-start.8
  75.9 8.9 %copy-start.6 = (f32[1536]{0:T(1024)S(1)}, f32[1536]{0:T(1024)}, u32[]{:S(2)}) copy-start(f32[1536]{0:T(1024)} %param.9) | copy-start | bytes 18436
  75.9 9.0 %copy-start.7 = (f32[64]{0:T(128)S(1)}, f32[64]{0:T(128)}, u32[]{:S(2)}) copy-start(f32[64]{0:T(128)} %param.8) | copy-start | bytes 772
  75.9 9.2 %copy-start.13 = (bf16[384,256]{1,0:T(8,128)(2,1)S(1)}, bf16[384,256]{1,0:T(8,128)(2,1)}, u32[]{:S(2)}) copy-start(bf16[384,256]{1,0:T(8,128)(2,1)} %get-tuple-element.26) | copy-start | bytes 589828
  75.9 13.8 %copy-start.12 = (bf16[384,256]{1,0:T(8,128)(2,1)S(1)}, bf16[384,256]{1,0:T(8,128)(2,1)}, u32[]{:S(2)}) copy-start(bf16[384,256]{1,0:T(8,128)(2,1)} %get-tuple-element.27) | copy-start | bytes 589828
  75.9 16.5 %copy-start.11 = (bf16[384,256]{1,0:T(8,128)(2,1)S(1)}, bf16[384,256]{1,0:T(8,128)(2,1)}, u32[]{:S(2)}) copy-start(bf16[384,256]{1,0:T(8,128)(2,1)} %get-tuple-element.28) | copy-start | bytes 589828
  75.9 42.7 %copy-start = (bf16[1,2,2,64,1536]{4,3,2,1,0:T(8,128)(2,1)S(1)}, bf16[1,2,2,64,1536]{4,3,2,1,0:T(8,128)(2,1)}, u32[]{:S(2)}) copy-start(bf16[1,2,2,64,1536]{4,3,2,1,0:T(8,128)(2,1)} %param.5) | copy-start | bytes 2359300
  75.9 42.7 %all-to-all-start.2 = ((bf16[96,16,256]{2,1,0:T(8,128)(2,1)}), bf16[96,16,256]{2,1,0:T(8,128)(2,1)S(1)}, u32[]{:S(2)}, u32[]{:S(2)}) async-start(bf16[96,16,256]{2,1,0:T(8,128)(2,1)} %bitcast.12), calls=%async_computation.2 | async-start | bytes 1572864 | tf_op jit(solution)/shard_map/all_to_all | solution.py:169
  84.8 33.8 %copy-start.1 = (bf16[384,256]{1,0:T(8,128)(2,1)S(1)}, bf16[384,256]{1,0:T(8,128)(2,1)}, u32[]{:S(2)}) copy-start(bf16[384,256]{1,0:T(8,128)(2,1)} %get-tuple-element.25.own0) | copy-start | bytes 589828
  85.1 15.7 %collective-permute-start.6 = (bf16[384,256]{1,0:T(8,128)(2,1)S(1)}, bf16[384,256]{1,0:T(8,128)(2,1)S(1)}, u32[]{:S(2)}, u32[]{:S(2)}) collective-permute-start(bf16[384,256]{1,0:T(8,128)(2,1)S(1)} %copy-done.13), channel_id=1, source_target_pairs={{0,576},{192,0},{384,192},{576,384},{1,577},{193,1},{385,193},{577... | collective-permute-start | bytes 589832 | tf_op jit(solution)/shard_map/ppermute | solution.py:21
  89.6 12.9 %collective-permute-start.7 = (bf16[384,256]{1,0:T(8,128)(2,1)S(1)}, bf16[384,256]{1,0:T(8,128)(2,1)S(1)}, u32[]{:S(2)}, u32[]{:S(2)}) collective-permute-start(bf16[384,256]{1,0:T(8,128)(2,1)S(1)} %copy-done.12), channel_id=1, source_target_pairs={{0,384},{192,576},{384,0},{576,192},{1,385},{193,577},{385,1},{577... | collective-permute-start | bytes 589832 | tf_op jit(solution)/shard_map/ppermute | solution.py:21
  92.4 14.2 %collective-permute-start.8 = (bf16[384,256]{1,0:T(8,128)(2,1)S(1)}, bf16[384,256]{1,0:T(8,128)(2,1)S(1)}, u32[]{:S(2)}, u32[]{:S(2)}) collective-permute-start(bf16[384,256]{1,0:T(8,128)(2,1)S(1)} %copy-done.11), channel_id=1, source_target_pairs={{0,192},{192,384},{384,576},{576,0},{1,193},{193,385},{385,577},{5... | collective-permute-start | bytes 589832 | tf_op jit(solution)/shard_map/ppermute | solution.py:21

commit v10 on v8

--- a/solution.py
+++ b/solution.py
@@ -132,7 +132,7 @@
     pieces = spread(integrals.reshape(2, -1), VIRT, NVIRT).reshape(NVIRT, width, depth)
     labels_c = lax.dynamic_slice_in_dim(irreps, index * depth, depth)[:, None]
     labels_a = jnp.transpose(irreps.reshape(NVIRT, X, quarter), (1, 0, 2)).reshape(X, NVIRT * quarter)
-    early, middle = lanes // 8, lanes * 9 // 16
+    early, middle = lanes // 8, lanes * 5 // 8
     t2a = passed_along(t1[:early], "x", 1)
     pieces, t1, t3, t2a = lax.optimization_barrier((pieces, t1, t3, t2a))
     t2c = passed_along(t3[middle:], "x", 3)

time: 121 us -> 122 us (level)
  the two profiles are of different devices: /device:TPU:192 before, /device:TPU:64 now
where the time goes in v10:
time: 122 us
  starting transfers between devices  62.2 us (51%)
  waiting for transfers between devices  46.2 us (38%)
  Pallas kernels  8.56 us (7%)
  local copies, waits for them, and re-layouts  4.31 us (4%)
    ppermute x9, starting transfers between devices, passed_along(): return lax.ppermute(value, axis, pairs)  28.2 us
    ppermute x9, waiting for transfers between devices, passed_along(): return lax.ppermute(value, axis, pairs)  22.5 us
    all_to_all x1, starting transfers between devices, spread(): return lax.all_to_all(copies, axis, split_axis=0, concat_axis=0, tiled=True)  18.5 us
    all_to_all x1, waiting for transfers between devices, local(): lax.all_to_all(mirror.reshape(NVIRT * X, quarter, lanes), VIRT + ('x',),...  13.5 us
    all_to_all x1, waiting for transfers between devices, spread(): return lax.all_to_all(copies, axis, split_axis=0, concat_axis=0, tiled=True)  10.2 us
    all_to_all x1, starting transfers between devices, local(): lax.all_to_all(mirror.reshape(NVIRT * X, quarter, lanes), VIRT + ('x',),...  8.28 us
    all_to_all x1, starting transfers between devices, local(): lax.all_to_all(sent, ('x', 'zl'), split_axis=0, concat_axis=0, tiled=True)  7.23 us
    pallas_call x1, Pallas kernels, local(): pl.pallas_call(cycle_kernel, out_shape=[jax.ShapeDtypeStruct((NVIRT, widt...  5.5 us
  transfers between devices with their start and end apart: 12, of which 8 were waited for; matrix products, arithmetic and copies ran while one was open for 2% of the time, Pallas kernels for 0%

profile of v10, /device:TPU:64, one launch (start us, length us, event | category | flops | bytes accessed | tf_op | source)
XLA Modules:
  0.0 121.8 jit_solution(9036102002408041066)
XLA Ops:
  0.0 3.4 %collective-permute-start = (bf16[256,1536]{1,0:T(8,128)(2,1)}, bf16[256,1536]{1,0:T(8,128)(2,1)S(1)}, u32[]{:S(2)}, u32[]{:S(2)}) collective-permute-start(bf16[256,1536]{1,0:T(8,128)(2,1)} %bitcast.8), channel_id=1, source_target_pairs={{0,192},{192,384},{384,576},{576,0},{1,193},{193,385},{385,577},{5... | collective-permute-start | bytes 2359304 | tf_op jit(solution)/shard_map/ppermute | solution.py:21
  3.4 3.7 %collective-permute-start.1 = (bf16[256,1536]{1,0:T(8,128)(2,1)}, bf16[256,1536]{1,0:T(8,128)(2,1)S(1)}, u32[]{:S(2)}, u32[]{:S(2)}) collective-permute-start(bf16[256,1536]{1,0:T(8,128)(2,1)} %bitcast.9), channel_id=1, source_target_pairs={{0,576},{192,0},{384,192},{576,384},{1,577},{193,1},{385,193},{577... | collective-permute-start | bytes 2359304 | tf_op jit(solution)/shard_map/ppermute | solution.py:21
  7.1 0.8 copy.8
  7.9 0.1 broadcast_in_dim.17
  8.0 0.8 broadcast_in_dim.18
  8.7 18.5 %all-to-all-start = ((bf16[24,2,1536]{2,1,0:T(2,128)(2,1)}), bf16[24,2,1536]{2,1,0:T(2,128)(2,1)S(1)}, u32[]{:S(2)}, u32[]{:S(2)}) async-start(bf16[24,2,1536]{2,1,0:T(2,128)(2,1)} %broadcast_in_dim.18), calls=%async_computation | async-start | bytes 294912 | tf_op jit(solution)/shard_map/all_to_all | solution.py:31
  27.3 0.0 copy-start.5
  27.3 0.7 copy-done.5
  28.0 0.1 reshape.78
  28.1 0.0 collective-permute-done.t1
  28.1 0.0 copy-start.3
  28.1 2.2 %collective-permute-start.2 = (bf16[32,1536]{1,0:T(8,128)(2,1)S(1)}, bf16[32,1536]{1,0:T(8,128)(2,1)S(1)}, u32[]{:S(2)}, u32[]{:S(2)}) collective-permute-start(bf16[32,1536]{1,0:T(8,128)(2,1)S(1)} %slice.12), channel_id=1, source_target_pairs={{0,192},{192,384},{384,576},{576,0},{1,193},{193,385},{385,577},{5... | collective-permute-start | bytes 294920 | tf_op jit(solution)/shard_map/ppermute | solution.py:21
  30.3 0.1 dynamic-slice_bitcast_fusion
  30.4 0.1 copy.9.labels_c
  30.5 0.1 reshape.79.labels_a
  30.6 10.2 %all-to-all-done = bf16[24,2,1536]{2,1,0:T(2,128)(2,1)S(1)} async-done(((bf16[24,2,1536]{2,1,0:T(2,128)(2,1)}), bf16[24,2,1536]{2,1,0:T(2,128)(2,1)S(1)}, u32[]{:S(2)}, u32[]{:S(2)}) %all-to-all-start) | async-done | bytes 147488 | tf_op jit(solution)/shard_map/all_to_all | solution.py:31
  40.8 0.4 reshape.80.pieces
  41.1 0.0 collective-permute-done.1.t3
  41.2 0.0 copy-start.4
  41.2 0.0 collective-permute-done.2.t2a
  41.2 1.1 turn.1
  42.3 7.2 %all-to-all-start.1 = ((bf16[16,48,384]{2,1,0:T(8,128)(2,1)}), bf16[16,48,384]{2,1,0:T(8,128)(2,1)S(1)}, u32[]{:S(2)}, u32[]{:S(2)}) async-start(bf16[16,48,384]{2,1,0:T(8,128)(2,1)} %turn.1), calls=%async_computation.1 | async-start | bytes 1179648 | tf_op jit(solution)/shard_map/all_to_all | solution.py:149
  49.6 3.4 %collective-permute-start.3 = (bf16[128,1536]{1,0:T(8,128)(2,1)S(1)}, bf16[128,1536]{1,0:T(8,128)(2,1)S(1)}, u32[]{:S(2)}, u32[]{:S(2)}) collective-permute-start(bf16[128,1536]{1,0:T(8,128)(2,1)S(1)} %slice.10), channel_id=1, source_target_pairs={{0,192},{192,384},{384,576},{576,0},{1,193},{193,385},{385,577},{5... | collective-permute-start | bytes 1179656 | tf_op jit(solution)/shard_map/ppermute | solution.py:21
  53.0 3.7 %collective-permute-start.4 = (bf16[96,1536]{1,0:T(8,128)(2,1)S(1)}, bf16[96,1536]{1,0:T(8,128)(2,1)S(1)}, u32[]{:S(2)}, u32[]{:S(2)}) collective-permute-start(bf16[96,1536]{1,0:T(8,128)(2,1)S(1)} %slice.11), channel_id=1, source_target_pairs={{0,576},{192,0},{384,192},{576,384},{1,577},{193,1},{385,193},{577... | collective-permute-start | bytes 884744 | tf_op jit(solution)/shard_map/ppermute | solution.py:21
  56.7 7.0 %collective-permute-done.4.t2c = bf16[96,1536]{1,0:T(8,128)(2,1)S(1)} collective-permute-done((bf16[96,1536]{1,0:T(8,128)(2,1)S(1)}, bf16[96,1536]{1,0:T(8,128)(2,1)S(1)}, u32[]{:S(2)}, u32[]{:S(2)}) %collective-permute-start.4) | collective-permute-done | bytes 294944 | tf_op jit(solution)/shard_map/ppermute | solution.py:21
  63.7 2.7 %collective-permute-done.3.t2b = bf16[128,1536]{1,0:T(8,128)(2,1)S(1)} collective-permute-done((bf16[128,1536]{1,0:T(8,128)(2,1)S(1)}, bf16[128,1536]{1,0:T(8,128)(2,1)S(1)}, u32[]{:S(2)}, u32[]{:S(2)}) %collective-permute-start.3) | collective-permute-done | bytes 393248 | tf_op jit(solution)/shard_map/ppermute | solution.py:21
  66.4 0.0 all-to-all-done.1.mine
  66.4 1.9 %collective-permute-start.5 = (bf16[16,48,384]{2,1,0:T(8,128)(2,1)S(1)}, bf16[16,48,384]{2,1,0:T(8,128)(2,1)S(1)}, u32[]{:S(2)}, u32[]{:S(2)}) collective-permute-start(bf16[16,48,384]{2,1,0:T(8,128)(2,1)S(1)} %all-to-all-done.1.mine), channel_id=1, source_target_pairs={{0,24},{24,0},{1,25},{25,1},{2,26},{26,2},{3,27},{27,3},{4,28},{28... | collective-permute-start | bytes 1769480 | tf_op jit(solution)/shard_map/ppermute | solution.py:21
  68.3 2.0 %collective-permute-done.5.theirs = bf16[16,48,384]{2,1,0:T(8,128)(2,1)S(1)} collective-permute-done((bf16[16,48,384]{2,1,0:T(8,128)(2,1)S(1)}, bf16[16,48,384]{2,1,0:T(8,128)(2,1)S(1)}, u32[]{:S(2)}, u32[]{:S(2)}) %collective-permute-start.5) | collective-permute-done | bytes 589856 | tf_op jit(solution)/shard_map/ppermute | solution.py:21
  70.3 0.0 copy-done.9
  70.3 0.8 copy-done.8
  71.1 5.5 %cycle.1 = (bf16[24,64,256]{2,1,0:T(8,128)(2,1)}, bf16[384,256]{1,0:T(8,128)(2,1)}, bf16[384,256]{1,0:T(8,128)(2,1)}, bf16[384,256]{1,0:T(8,128)(2,1)}, bf16[384,256]{1,0:T(8,128)(2,1)}) custom-call(bf16[16,48,384]{2,1,0:T(8,128)(2,1)} %copy-done.2, bf16[16,48,384]{2,1,0:T(8,128)(2,1)} %copy-done.8, bf16[256,1536]{1,0:T(8,128)(2,1)} %bitcast.10, ...), custom_call_target="tpu_custom_call" | custom-call | flops 1210000000 | bytes 6000000 | tf_op jit(solution)/shard_map/cycle/pallas_call | solution.py:154
  76.6 0.0 copy-start.12
  76.6 0.0 copy-start
  76.7 8.3 %all-to-all-start.2 = ((bf16[96,16,256]{2,1,0:T(8,128)(2,1)}), bf16[96,16,256]{2,1,0:T(8,128)(2,1)S(1)}, u32[]{:S(2)}, u32[]{:S(2)}) async-start(bf16[96,16,256]{2,1,0:T(8,128)(2,1)} %bitcast.12), calls=%async_computation.2 | async-start | bytes 1572864 | tf_op jit(solution)/shard_map/all_to_all | solution.py:169
  85.0 0.1 dynamic_slice.15
  85.1 0.1 fusion
  85.2 0.1 broadcast_add_fusion
  85.2 4.5 %collective-permute-start.6 = (bf16[384,256]{1,0:T(8,128)(2,1)S(1)}, bf16[384,256]{1,0:T(8,128)(2,1)S(1)}, u32[]{:S(2)}, u32[]{:S(2)}) collective-permute-start(bf16[384,256]{1,0:T(8,128)(2,1)S(1)} %copy-done.13), channel_id=1, source_target_pairs={{0,576},{192,0},{384,192},{576,384},{1,577},{193,1},{385,193},{577... | collective-permute-start | bytes 589832 | tf_op jit(solution)/shard_map/ppermute | solution.py:21
  89.7 2.8 %collective-permute-start.7 = (bf16[384,256]{1,0:T(8,128)(2,1)S(1)}, bf16[384,256]{1,0:T(8,128)(2,1)S(1)}, u32[]{:S(2)}, u32[]{:S(2)}) collective-permute-start(bf16[384,256]{1,0:T(8,128)(2,1)S(1)} %copy-done.12), channel_id=1, source_target_pairs={{0,384},{192,576},{384,0},{576,192},{1,385},{193,577},{385,1},{577... | collective-permute-start | bytes 589832 | tf_op jit(solution)/shard_map/ppermute | solution.py:21
  92.5 2.8 %collective-permute-start.8 = (bf16[384,256]{1,0:T(8,128)(2,1)S(1)}, bf16[384,256]{1,0:T(8,128)(2,1)S(1)}, u32[]{:S(2)}, u32[]{:S(2)}) collective-permute-start(bf16[384,256]{1,0:T(8,128)(2,1)S(1)} %copy-done.11), channel_id=1, source_target_pairs={{0,192},{192,384},{384,576},{576,0},{1,193},{193,385},{385,577},{5... | collective-permute-start | bytes 589832 | tf_op jit(solution)/shard_map/ppermute | solution.py:21
  95.3 0.1 broadcast_subtract_fusion
  95.3 0.1 sub.27.row_term
  95.5 5.0 %collective-permute-done.6.own1 = bf16[384,256]{1,0:T(8,128)(2,1)S(1)} collective-permute-done((bf16[384,256]{1,0:T(8,128)(2,1)S(1)}, bf16[384,256]{1,0:T(8,128)(2,1)S(1)}, u32[]{:S(2)}, u32[]{:S(2)}) %collective-permute-start.6) | collective-permute-done | bytes 196640 | tf_op jit(solution)/shard_map/ppermute | solution.py:21
  100.5 1.6 %collective-permute-done.7.own2 = bf16[384,256]{1,0:T(8,128)(2,1)S(1)} collective-permute-done((bf16[384,256]{1,0:T(8,128)(2,1)S(1)}, bf16[384,256]{1,0:T(8,128)(2,1)S(1)}, u32[]{:S(2)}, u32[]{:S(2)}) %collective-permute-start.7) | collective-permute-done | bytes 196640 | tf_op jit(solution)/shard_map/ppermute | solution.py:21
  102.1 4.3 %collective-permute-done.8.own3 = bf16[384,256]{1,0:T(8,128)(2,1)S(1)} collective-permute-done((bf16[384,256]{1,0:T(8,128)(2,1)S(1)}, bf16[384,256]{1,0:T(8,128)(2,1)S(1)}, u32[]{:S(2)}, u32[]{:S(2)}) %collective-permute-start.8) | collective-permute-done | bytes 196640 | tf_op jit(solution)/shard_map/ppermute | solution.py:21
  106.4 13.5 %all-to-all-done.2 = bf16[96,16,256]{2,1,0:T(8,128)(2,1)S(1)} async-done(((bf16[96,16,256]{2,1,0:T(8,128)(2,1)}), bf16[96,16,256]{2,1,0:T(8,128)(2,1)S(1)}, u32[]{:S(2)}, u32[]{:S(2)}) %all-to-all-start.2) | async-done | bytes 786464 | tf_op jit(solution)/shard_map/all_to_all | solution.py:169
  119.8 1.9 %finish.1 = bf16[256,1536]{1,0:T(8,128)(2,1)} custom-call(bf16[24,64,256]{2,1,0:T(8,128)(2,1)S(1)} %bitcast.7, bf16[384,256]{1,0:T(8,128)(2,1)S(1)} %copy-done.1, bf16[384,256]{1,0:T(8,128)(2,1)S(1)} %collective-permute-done.6.own1, bf16[384,256]{1,0:T(8,128)(2,1)S(1)} %collective-permute-done.7.own2, bf16[384,256]{1,0:T(8,128)(2,1)S(1)} %collective-permute-done.8.own3, ...), custom_call_target="tpu_custom_call" | custom-call | flops 600000000 | bytes 4000000 | tf_op jit(solution)/shard_map/finish/pallas_call | solution.py:181
  (27 shorter events, 0.1 us)
Async XLA Ops:
  0.0 28.1 %collective-permute-start = (bf16[256,1536]{1,0:T(8,128)(2,1)}, bf16[256,1536]{1,0:T(8,128)(2,1)S(1)}, u32[]{:S(2)}, u32[]{:S(2)}) collective-permute-start(bf16[256,1536]{1,0:T(8,128)(2,1)} %bitcast.8), channel_id=1, source_target_pairs={{0,192},{192,384},{384,576},{576,0},{1,193},{193,385},{385,577},{5... | collective-permute-start | bytes 2359304 | tf_op jit(solution)/shard_map/ppermute | solution.py:21
  3.4 37.7 %collective-permute-start.1 = (bf16[256,1536]{1,0:T(8,128)(2,1)}, bf16[256,1536]{1,0:T(8,128)(2,1)S(1)}, u32[]{:S(2)}, u32[]{:S(2)}) collective-permute-start(bf16[256,1536]{1,0:T(8,128)(2,1)} %bitcast.9), channel_id=1, source_target_pairs={{0,576},{192,0},{384,192},{576,384},{1,577},{193,1},{385,193},{577... | collective-permute-start | bytes 2359304 | tf_op jit(solution)/shard_map/ppermute | solution.py:21
  8.7 32.0 %all-to-all-start = ((bf16[24,2,1536]{2,1,0:T(2,128)(2,1)}), bf16[24,2,1536]{2,1,0:T(2,128)(2,1)S(1)}, u32[]{:S(2)}, u32[]{:S(2)}) async-start(bf16[24,2,1536]{2,1,0:T(2,128)(2,1)} %broadcast_in_dim.18), calls=%async_computation | async-start | bytes 294912 | tf_op jit(solution)/shard_map/all_to_all | solution.py:31
  27.3 0.7 copy-start.5
  28.1 21.5 %copy-start.3 = (bf16[256,1536]{1,0:T(8,128)(2,1)}, bf16[256,1536]{1,0:T(8,128)(2,1)S(1)}, u32[]{:S(2)}) copy-start(bf16[256,1536]{1,0:T(8,128)(2,1)S(1)} %collective-permute-done.t1) | copy-start | bytes 2359300
  28.1 13.1 %collective-permute-start.2 = (bf16[32,1536]{1,0:T(8,128)(2,1)S(1)}, bf16[32,1536]{1,0:T(8,128)(2,1)S(1)}, u32[]{:S(2)}, u32[]{:S(2)}) collective-permute-start(bf16[32,1536]{1,0:T(8,128)(2,1)S(1)} %slice.12), channel_id=1, source_target_pairs={{0,192},{192,384},{384,576},{576,0},{1,193},{193,385},{385,577},{5... | collective-permute-start | bytes 294920 | tf_op jit(solution)/shard_map/ppermute | solution.py:21
  41.2 11.8 %copy-start.4 = (bf16[256,1536]{1,0:T(8,128)(2,1)}, bf16[256,1536]{1,0:T(8,128)(2,1)S(1)}, u32[]{:S(2)}) copy-start(bf16[256,1536]{1,0:T(8,128)(2,1)S(1)} %collective-permute-done.1.t3) | copy-start | bytes 2359300
  41.2 1.2 copy-start.14
  42.3 24.0 %all-to-all-start.1 = ((bf16[16,48,384]{2,1,0:T(8,128)(2,1)}), bf16[16,48,384]{2,1,0:T(8,128)(2,1)S(1)}, u32[]{:S(2)}, u32[]{:S(2)}) async-start(bf16[16,48,384]{2,1,0:T(8,128)(2,1)} %turn.1), calls=%async_computation.1 | async-start | bytes 1179648 | tf_op jit(solution)/shard_map/all_to_all | solution.py:149
  49.6 16.8 %collective-permute-start.3 = (bf16[128,1536]{1,0:T(8,128)(2,1)S(1)}, bf16[128,1536]{1,0:T(8,128)(2,1)S(1)}, u32[]{:S(2)}, u32[]{:S(2)}) collective-permute-start(bf16[128,1536]{1,0:T(8,128)(2,1)S(1)} %slice.10), channel_id=1, source_target_pairs={{0,192},{192,384},{384,576},{576,0},{1,193},{193,385},{385,577},{5... | collective-permute-start | bytes 1179656 | tf_op jit(solution)/shard_map/ppermute | solution.py:21
  53.0 10.7 %collective-permute-start.4 = (bf16[96,1536]{1,0:T(8,128)(2,1)S(1)}, bf16[96,1536]{1,0:T(8,128)(2,1)S(1)}, u32[]{:S(2)}, u32[]{:S(2)}) collective-permute-start(bf16[96,1536]{1,0:T(8,128)(2,1)S(1)} %slice.11), channel_id=1, source_target_pairs={{0,576},{192,0},{384,192},{576,384},{1,577},{193,1},{385,193},{577... | collective-permute-start | bytes 884744 | tf_op jit(solution)/shard_map/ppermute | solution.py:21
  63.7 6.6 %copy-start.10 = (bf16[96,1536]{1,0:T(8,128)(2,1)}, bf16[96,1536]{1,0:T(8,128)(2,1)S(1)}, u32[]{:S(2)}) copy-start(bf16[96,1536]{1,0:T(8,128)(2,1)S(1)} %collective-permute-done.4.t2c) | copy-start | bytes 884740
  66.4 3.9 %copy-start.9 = (bf16[128,1536]{1,0:T(8,128)(2,1)}, bf16[128,1536]{1,0:T(8,128)(2,1)S(1)}, u32[]{:S(2)}) copy-start(bf16[128,1536]{1,0:T(8,128)(2,1)S(1)} %collective-permute-done.3.t2b) | copy-start | bytes 1179652
  66.4 3.9 %copy-start.2 = (bf16[16,48,384]{2,1,0:T(8,128)(2,1)}, bf16[16,48,384]{2,1,0:T(8,128)(2,1)S(1)}, u32[]{:S(2)}) copy-start(bf16[16,48,384]{2,1,0:T(8,128)(2,1)S(1)} %all-to-all-done.1.mine) | copy-start | bytes 1769476
  66.4 3.9 %collective-permute-start.5 = (bf16[16,48,384]{2,1,0:T(8,128)(2,1)S(1)}, bf16[16,48,384]{2,1,0:T(8,128)(2,1)S(1)}, u32[]{:S(2)}, u32[]{:S(2)}) collective-permute-start(bf16[16,48,384]{2,1,0:T(8,128)(2,1)S(1)} %all-to-all-done.1.mine), channel_id=1, source_target_pairs={{0,24},{24,0},{1,25},{25,1},{2,26},{26,2},{3,27},{27,3},{4,28},{28... | collective-permute-start | bytes 1769480 | tf_op jit(solution)/shard_map/ppermute | solution.py:21
  70.3 0.8 copy-start.8
  76.6 8.4 %copy-start.6 = (f32[1536]{0:T(1024)S(1)}, f32[1536]{0:T(1024)}, u32[]{:S(2)}) copy-start(f32[1536]{0:T(1024)} %param.9) | copy-start | bytes 18436
  76.6 8.5 %copy-start.7 = (f32[64]{0:T(128)S(1)}, f32[64]{0:T(128)}, u32[]{:S(2)}) copy-start(f32[64]{0:T(128)} %param.8) | copy-start | bytes 772
  76.6 8.6 %copy-start.13 = (bf16[384,256]{1,0:T(8,128)(2,1)S(1)}, bf16[384,256]{1,0:T(8,128)(2,1)}, u32[]{:S(2)}) copy-start(bf16[384,256]{1,0:T(8,128)(2,1)} %get-tuple-element.26) | copy-start | bytes 589828
  76.6 13.1 %copy-start.12 = (bf16[384,256]{1,0:T(8,128)(2,1)S(1)}, bf16[384,256]{1,0:T(8,128)(2,1)}, u32[]{:S(2)}) copy-start(bf16[384,256]{1,0:T(8,128)(2,1)} %get-tuple-element.27) | copy-start | bytes 589828
  76.6 15.9 %copy-start.11 = (bf16[384,256]{1,0:T(8,128)(2,1)S(1)}, bf16[384,256]{1,0:T(8,128)(2,1)}, u32[]{:S(2)}) copy-start(bf16[384,256]{1,0:T(8,128)(2,1)} %get-tuple-element.28) | copy-start | bytes 589828
  76.6 43.2 %copy-start = (bf16[1,2,2,64,1536]{4,3,2,1,0:T(8,128)(2,1)S(1)}, bf16[1,2,2,64,1536]{4,3,2,1,0:T(8,128)(2,1)}, u32[]{:S(2)}) copy-start(bf16[1,2,2,64,1536]{4,3,2,1,0:T(8,128)(2,1)} %param.5) | copy-start | bytes 2359300
  76.7 43.2 %all-to-all-start.2 = ((bf16[96,16,256]{2,1,0:T(8,128)(2,1)}), bf16[96,16,256]{2,1,0:T(8,128)(2,1)S(1)}, u32[]{:S(2)}, u32[]{:S(2)}) async-start(bf16[96,16,256]{2,1,0:T(8,128)(2,1)} %bitcast.12), calls=%async_computation.2 | async-start | bytes 1572864 | tf_op jit(solution)/shard_map/all_to_all | solution.py:169
  84.9 34.9 %copy-start.1 = (bf16[384,256]{1,0:T(8,128)(2,1)S(1)}, bf16[384,256]{1,0:T(8,128)(2,1)}, u32[]{:S(2)}) copy-start(bf16[384,256]{1,0:T(8,128)(2,1)} %get-tuple-element.25.own0) | copy-start | bytes 589828
  85.2 15.3 %collective-permute-start.6 = (bf16[384,256]{1,0:T(8,128)(2,1)S(1)}, bf16[384,256]{1,0:T(8,128)(2,1)S(1)}, u32[]{:S(2)}, u32[]{:S(2)}) collective-permute-start(bf16[384,256]{1,0:T(8,128)(2,1)S(1)} %copy-done.13), channel_id=1, source_target_pairs={{0,576},{192,0},{384,192},{576,384},{1,577},{193,1},{385,193},{577... | collective-permute-start | bytes 589832 | tf_op jit(solution)/shard_map/ppermute | solution.py:21
  89.7 12.3 %collective-permute-start.7 = (bf16[384,256]{1,0:T(8,128)(2,1)S(1)}, bf16[384,256]{1,0:T(8,128)(2,1)S(1)}, u32[]{:S(2)}, u32[]{:S(2)}) collective-permute-start(bf16[384,256]{1,0:T(8,128)(2,1)S(1)} %copy-done.12), channel_id=1, source_target_pairs={{0,384},{192,576},{384,0},{576,192},{1,385},{193,577},{385,1},{577... | collective-permute-start | bytes 589832 | tf_op jit(solution)/shard_map/ppermute | solution.py:21
  92.5 13.9 %collective-permute-start.8 = (bf16[384,256]{1,0:T(8,128)(2,1)S(1)}, bf16[384,256]{1,0:T(8,128)(2,1)S(1)}, u32[]{:S(2)}, u32[]{:S(2)}) collective-permute-start(bf16[384,256]{1,0:T(8,128)(2,1)S(1)} %copy-done.11), channel_id=1, source_target_pairs={{0,192},{192,384},{384,576},{576,0},{1,193},{193,385},{385,577},{5... | collective-permute-start | bytes 589832 | tf_op jit(solution)/shard_map/ppermute | solution.py:21
